TPU v7x, 32 devices: a whole 2x2x4 slice. The times are simulated.
32 devices in a mesh: samp: 8 (over z, core), par: 4 (over y, x).
Axes of the slice: x: 2, y: 2, z: 4, core: 2. Of those that a mesh axis runs over, the one named last changes fastest.
Arguments:
- activations: bfloat16 [128, 2, 64, 256], P('samp'), may hold values from 0 to 2
- cotangents: bfloat16 [128, 2, 64, 256], P('samp', None, 'par'), may hold values from -0.029907227 to 0.099609375
- energies: float32 [128], P('samp'), may hold values from -3 to -1
Outputs:
- update: float32 [64, 1152], P('par')
- coeffs: float32 [128], P('samp')
All inputs are finite; a program needn't handle non-finite values.
Results may differ from a plain program's by a relative error of at most 0.0034.
Values may be sent and summed in bfloat16 or wider, within the bound.
No kernel may reach another device: no remote copies, remote signals or barrier semaphores. Data moves between devices by JAX's collectives and lax.ppermute only.
A program may use at most 128 MiB of HBM per device.

v0:
```python
import functools
import math

import jax
import jax.numpy as jnp
from jax import lax
from jax.experimental import pallas as pl
from jax.experimental.pallas import tpu as pltpu
from jax.sharding import PartitionSpec as P

C = 64
SIDE = 16
LAYERS = 2
SITES = SIDE * SIDE
OFFSETS = 9
LANES = 128
CORES = 2


reg_shift = 0.1
F32 = jnp.float32
BF16 = jnp.bfloat16
VMEM_LIMIT = 48 * 1024 * 1024


def kernel_call(body, out_shape, scratch_shapes=()):
    return pl.pallas_call(
        body,
        out_shape=out_shape,
        scratch_shapes=scratch_shapes,
        compiler_params=pltpu.CompilerParams(vmem_limit_bytes=VMEM_LIMIT),
    )


def swap(x, axis, mask):
    count = lax.axis_size(axis)
    return lax.ppermute(x, axis, [(i, i ^ mask) for i in range(count)])


def grads_body(acts_ref, cots_ref, keep_ref, send_ref, shifted_ref):
    samples, layers, owned, sites = cots_ref.shape
    half = owned // CORES
    core = lax.axis_index("samp") % CORES
    field = cots_ref[...].reshape(samples * layers, CORES, half, sites).astype(F32)
    swapped = jnp.concatenate([field[:, 1:], field[:, :1]], axis=1)
    field = jnp.where(core == 1, swapped, field).reshape(samples * layers * owned, sites).astype(BF16)
    source = lax.broadcasted_iota(jnp.int32, (sites, sites), 0)
    target = lax.broadcasted_iota(jnp.int32, (1, sites), 1)
    for offset in range(OFFSETS):
        row, col = target // SIDE, target % SIDE
        row = (row + SIDE - (offset // 3 - 1)) % SIDE
        col = (col + SIDE - (offset % 3 - 1)) % SIDE
        move = jnp.where(source == row * SIDE + col, 1.0, 0.0).astype(BF16)
        shifted_ref[offset] = jnp.dot(field, move, preferred_element_type=F32).astype(BF16)
    empty = jnp.zeros((C, sites), BF16)
    for sample in range(samples):
        left = []
        for layer in range(layers):
            first = (sample * layers + layer) * owned
            left.append(jnp.concatenate([shifted_ref[k, first : first + owned, :] for k in range(OFFSETS)], axis=0))
        right = [
            jnp.concatenate([acts_ref[sample, layer] if layer == other else empty for other in range(layers)], axis=1)
            for layer in range(layers)
        ]
        grads = lax.dot_general(
            jnp.concatenate(left, axis=1),
            jnp.concatenate(right, axis=0),
            (((1,), (1,)), ((), ())),
            preferred_element_type=F32,
        )
        for k in range(OFFSETS):
            rows = pl.ds(k * half * samples + sample, half, stride=samples)
            keep_ref[rows, :] = grads[k * owned : k * owned + half]
            send_ref[rows, :] = grads[k * owned + half : (k + 1) * owned]


def pack_body(keep_ref, recv_ref, *out_refs):
    offsets, chips, owned, samples, lanes = keep_ref.shape
    rows = offsets * owned
    position = lax.axis_index("samp")
    core, chip = position % CORES, position // CORES
    own_ref = out_refs[0]
    mine = pl.multiple_of(core * samples, samples)
    other = pl.multiple_of((1 - core) * samples, samples)
    own_ref[:, pl.ds(mine, samples), :] = keep_ref[:, chip].reshape(rows, samples, lanes)
    own_ref[:, pl.ds(other, samples), :] = recv_ref[:, chip].reshape(rows, samples, lanes)
    for slot in range(1, chips):
        values_ref, side_ref = out_refs[2 * slot - 1], out_refs[2 * slot]
        first = keep_ref[:, chip ^ slot].reshape(rows, samples, lanes)
        second = recv_ref[:, chip ^ slot].reshape(rows, samples, lanes)
        mean = (jnp.sum(first, axis=1) + jnp.sum(second, axis=1)) * (1.0 / (2 * samples))
        first, second = first - mean[:, None, :], second - mean[:, None, :]
        top = jnp.maximum(jnp.max(jnp.abs(first), axis=0), jnp.max(jnp.abs(second), axis=0))
        top = jnp.maximum(jnp.max(top, axis=0, keepdims=True), 1e-30)
        scale = 32768.0 / top
        values_ref[:, pl.ds(mine, samples), :] = first * scale
        values_ref[:, pl.ds(other, samples), :] = second * scale
        side_ref[0:rows, :] = mean
        side_ref[rows : rows + 1, :] = top * (1.0 / 32768.0)


def gram_body(total, params_all, energies_ref, own_ref, *refs):
    rows, group, lanes = own_ref.shape
    chips = total // group
    centered_ref, gram_ref = refs[2 * (chips - 1) :]
    chip = lax.axis_index("samp") // CORES
    gram = jnp.zeros((total, total), F32)
    pair = []
    for row in range(rows):
        blocks = [own_ref[row]]
        for slot in range(1, chips):
            values_ref, side_ref = refs[2 * slot - 2], refs[2 * slot - 1]
            blocks.append(values_ref[row] * side_ref[rows : rows + 1, :] + side_ref[row : row + 1, :])
        mean = sum(jnp.sum(block, axis=0, keepdims=True) for block in blocks) / total
        for slot in range(chips):
            place = pl.ds(pl.multiple_of((chip ^ slot) * group, group), group)
            centered_ref[row, place, :] = ((blocks[slot] - mean) * (1.0 / math.sqrt(params_all))).astype(BF16)
        pair.append(centered_ref[row])
        if len(pair) == 2 or row == rows - 1:
            both = jnp.concatenate(pair, axis=1)
            gram = gram + lax.dot_general(both, both, (((1,), (1,)), ((), ())), preferred_element_type=F32)
            pair = []
    gram_ref[0:total, :] = gram
    gram_ref[total : total + 8, :] = energies_ref[...]


def update_body(scale, coeffs_ref, centered_ref, update_ref):
    rows, total, lanes = centered_ref.shape
    coeffs = coeffs_ref[...] * scale
    terms = [jnp.sum(centered_ref[row].astype(F32) * coeffs, axis=0, keepdims=True) for row in range(rows)]
    owned = rows // OFFSETS
    padded = -(-rows // 8) * 8
    table = jnp.concatenate(terms + [jnp.zeros((padded - rows, lanes), F32)], axis=0)
    row_index = lax.broadcasted_iota(jnp.int32, (padded, lanes), 0)
    for tile in range(OFFSETS):
        place = lax.broadcasted_iota(jnp.int32, (padded, lanes), 1) + tile * lanes
        picked = jnp.take_along_axis(table, place // OFFSETS, axis=1)
        for channel in range(owned):
            mask = row_index == (place % OFFSETS) * owned + channel
            update_ref[channel : channel + 1, tile * lanes : (tile + 1) * lanes] = jnp.sum(
                jnp.where(mask, picked, 0.0), axis=0, keepdims=True
            )


def in_order(x, axis, mask):
    other = swap(x, axis, mask)
    low = (lax.axis_index(axis) & mask) == 0
    return jnp.where(low, jnp.concatenate([x, other]), jnp.concatenate([other, x]))


def solve_system(gram, dev_all, total):
    regular = gram + reg_shift * jnp.eye(total, dtype=F32)
    factor = jnp.linalg.cholesky(regular)
    forward = lax.linalg.triangular_solve(factor, dev_all[:, None], left_side=True, lower=True)
    return lax.linalg.triangular_solve(factor, forward, left_side=True, lower=True, transpose_a=True)[:, 0]


def local_split(activations, cotangents, energies):
    samples, layers, channels, sites = activations.shape
    owned = cotangents.shape[2]
    members = lax.axis_size("samp")
    chips = members // CORES
    group = CORES * samples
    total = members * samples
    position = lax.axis_index("samp")
    params_all = LAYERS * C * C * OFFSETS
    mine = owned // members
    rows = OFFSETS * mine

    half_rows = OFFSETS * (owned // CORES) * samples
    half_grads = jax.ShapeDtypeStruct((half_rows, LANES), F32)
    keep, send = kernel_call(
        grads_body, (half_grads, half_grads), [pltpu.VMEM((OFFSETS, samples * layers * owned, sites), BF16)]
    )(activations, cotangents)
    recv = swap(send, "samp", 1)
    split = (OFFSETS, chips, mine, samples, LANES)
    block = jax.ShapeDtypeStruct((rows, group, LANES), F32)
    side = jax.ShapeDtypeStruct((-(-(rows + 1) // 8) * 8, LANES), F32)
    packed = kernel_call(pack_body, (block,) + (block, side) * (chips - 1))(keep.reshape(split), recv.reshape(split))
    arrived = []
    for slot in range(1, chips):
        values, means = packed[2 * slot - 1], packed[2 * slot]
        arrived.append(swap(values.astype(jnp.float16), "samp", CORES * slot).astype(F32))
        arrived.append(swap(means, "samp", CORES * slot))

    lane = jnp.arange(total) // samples
    here = (lane == position) & (lax.axis_index("par") == 0)
    spread = jnp.where(here, jnp.tile(energies, members), 0.0)
    spread = jnp.where(jnp.arange(8)[:, None] == 0, spread[None, :], 0.0)
    centered, partial_gram = kernel_call(
        functools.partial(gram_body, total, params_all),
        (jax.ShapeDtypeStruct((rows, total, LANES), BF16), jax.ShapeDtypeStruct((total + 8, total), F32)),
    )(spread, packed[0], *arrived)

    summed = partial_gram + swap(partial_gram, "samp", 1)
    mask = 1
    while mask < lax.axis_size("par"):
        summed = summed + swap(summed, "par", mask)
        mask *= 2
    summed = summed + sum(swap(summed, "samp", CORES * slot) for slot in range(1, chips))

    energies_all = summed[total]
    deviation = energies_all - jnp.sum(energies_all) / total
    coeffs = solve_system(summed[:total], deviation, total)
    local_coeffs = lax.dynamic_slice_in_dim(coeffs, position * samples, samples)
    update = kernel_call(
        functools.partial(update_body, -math.sqrt(params_all / total)),
        jax.ShapeDtypeStruct((mine, OFFSETS * LANES), F32),
    )(coeffs[:, None], centered)
    mask = CORES
    while mask < members:
        update = in_order(update, "samp", mask)
        mask *= 2
    return in_order(update, "samp", 1), local_coeffs


def local_gather(activations, cotangents, energies):
    samples, layers, channels, sites = activations.shape
    owned = cotangents.shape[2]
    position = lax.axis_index("samp")
    total = lax.axis_size("samp") * samples
    params_all = LAYERS * C * C * OFFSETS
    field = cotangents.reshape(samples, layers, owned, SIDE, SIDE)
    shifted = [jnp.roll(field, (row - 1, col - 1), axis=(3, 4)) for row in range(3) for col in range(3)]
    stacked = jnp.stack(shifted, axis=3).reshape(samples, layers, owned * OFFSETS, sites)
    grads = jnp.einsum("slkx,slix->slki", stacked, activations, preferred_element_type=F32)
    grads = grads.reshape(samples, layers, owned, OFFSETS, channels).transpose(0, 2, 1, 4, 3)
    grads = grads.reshape(samples, owned * layers * channels * OFFSETS)
    col_sums, energy_sum = lax.psum((jnp.sum(grads, axis=0), jnp.sum(energies)), "samp")
    centered = ((grads - col_sums / total) * (1.0 / math.sqrt(params_all))).astype(BF16)
    everyone = lax.all_gather(centered, "samp", axis=0, tiled=True)
    partial_gram = lax.dot_general(centered, everyone, (((1,), (1,)), ((), ())), preferred_element_type=F32)
    gram = lax.all_gather(lax.psum(partial_gram, "par"), "samp", axis=0, tiled=True)
    deviation = lax.all_gather(energies - energy_sum / total, "samp", axis=0, tiled=True)
    coeffs = solve_system(gram, deviation, total)
    local_coeffs = lax.dynamic_slice_in_dim(coeffs, position * samples, samples)
    term = jnp.dot(local_coeffs[None, :], centered.astype(F32), precision=lax.Precision.HIGHEST)[0]
    update = -math.sqrt(params_all / total) * lax.psum(term, "samp")
    return update.reshape(owned, -1), local_coeffs


def local(activations, cotangents, energies):
    if cotangents.shape[2] % lax.axis_size("samp"):
        return local_gather(activations, cotangents, energies)
    return local_split(activations, cotangents, energies)


def solution(mesh):
    return jax.shard_map(
        local,
        mesh=mesh,
        in_specs=(P("samp", None, None, None), P("samp", None, "par", None), P("samp")),
        out_specs=(P("par", None), P("samp")),
        check_vma=False,
    )
```

profile of v0, /device:TPU:0, one launch (start us, length us, event | category | flops | bytes accessed | tf_op | source)
XLA Modules:
  0.0 82.3 jit_solution(9661947389242839411)
XLA Ops:
  0.6 0.0 copy-start
  0.6 1.2 %copy-done = bf16[16,2,64,256]{3,2,1,0:T(8,128)(2,1)S(1)} copy-done((bf16[16,2,64,256]{3,2,1,0:T(8,128)(2,1)S(1)}, bf16[16,2,64,256]{3,2,1,0:T(8,128)(2,1)}, u32[]{:S(2)}) %copy-start) | copy-done | bytes 1048600
  1.9 0.0 copy-start.1
  1.9 0.9 %copy-done.1 = bf16[16,2,16,256]{3,2,1,0:T(8,128)(2,1)S(1)} copy-done((bf16[16,2,16,256]{3,2,1,0:T(8,128)(2,1)S(1)}, bf16[16,2,16,256]{3,2,1,0:T(8,128)(2,1)}, u32[]{:S(2)}) %copy-start.1) | copy-done | bytes 262168
  2.8 1.6 %shard_map.50 = (f32[1152,128]{1,0:T(8,128)S(1)}, f32[1152,128]{1,0:T(8,128)S(1)}) custom-call(bf16[16,2,64,256]{3,2,1,0:T(8,128)(2,1)S(1)} %copy-done, bf16[16,2,16,256]{3,2,1,0:T(8,128)(2,1)S(1)} %copy-done.1), custom_call_target="tpu_custom_call" | custom-call | tf_op jit(solution)/shard_map/pallas_call | solution.py:172
  4.4 0.5 collective-permute-start
  4.9 0.0 copy-start.2
  4.9 0.7 copy-done.2
  5.6 0.1 tile.10
  5.6 0.9 %collective-permute-done = f32[1152,128]{1,0:T(8,128)S(1)} collective-permute-done((f32[1152,128]{1,0:T(8,128)S(1)}, f32[1152,128]{1,0:T(8,128)S(1)}, u32[]{:S(2)}, u32[]{:S(2)}) %collective-permute-start) | collective-permute-done | bytes 589856 | tf_op jit(solution)/shard_map/ppermute | solution.py:37
  6.5 0.3 shard_map.51
  6.8 3.0 %collective-permute-start.1 = (f16[18,32,128]{2,1,0:T(8,128)(2,1)S(1)}, f16[18,32,128]{2,1,0:T(8,128)(2,1)S(1)}, u32[]{:S(2)}, u32[]{:S(2)}) collective-permute-start(f16[18,32,128]{2,1,0:T(8,128)(2,1)S(1)} %convert_element_type.19), channel_id=1, source_target_pairs={{0,8},{4,12},{8,0},{12,4},{16,24},{20,28},{24,16},{28,20},{1,9},{5... | collective-permute-start | bytes 442376 | tf_op jit(solution)/shard_map/ppermute | solution.py:37
  9.9 2.7 %collective-permute-start.3 = (f16[18,32,128]{2,1,0:T(8,128)(2,1)S(1)}, f16[18,32,128]{2,1,0:T(8,128)(2,1)S(1)}, u32[]{:S(2)}, u32[]{:S(2)}) collective-permute-start(f16[18,32,128]{2,1,0:T(8,128)(2,1)S(1)} %convert_element_type.21), channel_id=1, source_target_pairs={{0,16},{4,20},{8,24},{12,28},{16,0},{20,4},{24,8},{28,12},{1,17},{... | collective-permute-start | bytes 442376 | tf_op jit(solution)/shard_map/ppermute | solution.py:37
  12.6 0.1 collective-permute-start.5
  12.7 0.9 %collective-permute-start.2 = (f32[24,128]{1,0:T(8,128)S(1)}, f32[24,128]{1,0:T(8,128)S(1)}, u32[]{:S(2)}, u32[]{:S(2)}) collective-permute-start(f32[24,128]{1,0:T(8,128)S(1)} %get-tuple-element.17), channel_id=1, source_target_pairs={{0,8},{4,12},{8,0},{12,4},{16,24},{20,28},{24,16},{28,20},{1,9},{5... | collective-permute-start | bytes 36872 | tf_op jit(solution)/shard_map/ppermute | solution.py:37
  13.6 3.5 %collective-permute-start.4 = (f32[24,128]{1,0:T(8,128)S(1)}, f32[24,128]{1,0:T(8,128)S(1)}, u32[]{:S(2)}, u32[]{:S(2)}) collective-permute-start(f32[24,128]{1,0:T(8,128)S(1)} %get-tuple-element.19), channel_id=1, source_target_pairs={{0,16},{4,20},{8,24},{12,28},{16,0},{20,4},{24,8},{28,12},{1,17},{... | collective-permute-start | bytes 36872 | tf_op jit(solution)/shard_map/ppermute | solution.py:37
  17.0 0.0 collective-permute-done.1
  17.0 2.7 %collective-permute-start.6 = (f32[24,128]{1,0:T(8,128)S(1)}, f32[24,128]{1,0:T(8,128)S(1)}, u32[]{:S(2)}, u32[]{:S(2)}) collective-permute-start(f32[24,128]{1,0:T(8,128)S(1)} %get-tuple-element.21), channel_id=1, source_target_pairs={{0,24},{4,28},{8,16},{12,20},{16,8},{20,12},{24,0},{28,4},{1,25},{... | collective-permute-start | bytes 36872 | tf_op jit(solution)/shard_map/ppermute | solution.py:37
  19.7 0.1 broadcast_select_fusion.energies_ref
  19.8 4.6 %collective-permute-done.3 = f16[18,32,128]{2,1,0:T(8,128)(2,1)S(1)} collective-permute-done((f16[18,32,128]{2,1,0:T(8,128)(2,1)S(1)}, f16[18,32,128]{2,1,0:T(8,128)(2,1)S(1)}, u32[]{:S(2)}, u32[]{:S(2)}) %collective-permute-start.3) | collective-permute-done | bytes 147488 | tf_op jit(solution)/shard_map/ppermute | solution.py:37
  24.5 0.0 collective-permute-done.5
  24.5 0.0 collective-permute-done.2.refs_1_
  24.5 2.4 %collective-permute-done.4.refs_3_ = f32[24,128]{1,0:T(8,128)S(1)} collective-permute-done((f32[24,128]{1,0:T(8,128)S(1)}, f32[24,128]{1,0:T(8,128)S(1)}, u32[]{:S(2)}, u32[]{:S(2)}) %collective-permute-start.4) | collective-permute-done | bytes 12320 | tf_op jit(solution)/shard_map/ppermute | solution.py:37
  26.9 0.0 collective-permute-done.6.refs_5_
  26.9 0.5 shard_map.52
  27.4 0.1 collective-permute-start.7
  27.5 1.2 %collective-permute-done.7 = f32[136,128]{1,0:T(8,128)S(1)} collective-permute-done((f32[136,128]{1,0:T(8,128)S(1)}, f32[136,128]{1,0:T(8,128)S(1)}, u32[]{:S(2)}, u32[]{:S(2)}) %collective-permute-start.7) | collective-permute-done | bytes 69664 | tf_op jit(solution)/shard_map/ppermute | solution.py:37
  28.8 1.6 %collective-permute-start.8 = (f32[136,128]{1,0:T(8,128)S(1)}, f32[136,128]{1,0:T(8,128)S(1)}, u32[]{:S(2)}, u32[]{:S(2)}) collective-permute-start(f32[136,128]{1,0:T(8,128)S(1)} %add.42), channel_id=1, source_target_pairs={{0,1},{1,0},{2,3},{3,2},{4,5},{5,4},{6,7},{7,6},{8,9},{9,8},{10,11... | collective-permute-start | bytes 208904 | tf_op jit(solution)/shard_map/ppermute | solution.py:37
  30.3 2.8 %collective-permute-done.8 = f32[136,128]{1,0:T(8,128)S(1)} collective-permute-done((f32[136,128]{1,0:T(8,128)S(1)}, f32[136,128]{1,0:T(8,128)S(1)}, u32[]{:S(2)}, u32[]{:S(2)}) %collective-permute-start.8) | collective-permute-done | bytes 69664 | tf_op jit(solution)/shard_map/ppermute | solution.py:37
  33.2 1.6 %collective-permute-start.9 = (f32[136,128]{1,0:T(8,128)S(1)}, f32[136,128]{1,0:T(8,128)S(1)}, u32[]{:S(2)}, u32[]{:S(2)}) collective-permute-start(f32[136,128]{1,0:T(8,128)S(1)} %add.43), channel_id=1, source_target_pairs={{0,2},{1,3},{2,0},{3,1},{4,6},{5,7},{6,4},{7,5},{8,10},{9,11},{10,... | collective-permute-start | bytes 208904 | tf_op jit(solution)/shard_map/ppermute | solution.py:37
  34.8 2.8 %collective-permute-done.9 = f32[136,128]{1,0:T(8,128)S(1)} collective-permute-done((f32[136,128]{1,0:T(8,128)S(1)}, f32[136,128]{1,0:T(8,128)S(1)}, u32[]{:S(2)}, u32[]{:S(2)}) %collective-permute-start.9) | collective-permute-done | bytes 69664 | tf_op jit(solution)/shard_map/ppermute | solution.py:37
  37.6 0.8 collective-permute-start.10
  38.3 2.3 %collective-permute-start.11 = (f32[136,128]{1,0:T(8,128)S(1)}, f32[136,128]{1,0:T(8,128)S(1)}, u32[]{:S(2)}, u32[]{:S(2)}) collective-permute-start(f32[136,128]{1,0:T(8,128)S(1)} %add.44), channel_id=1, source_target_pairs={{0,16},{4,20},{8,24},{12,28},{16,0},{20,4},{24,8},{28,12},{1,17},{... | collective-permute-start | bytes 208904 | tf_op jit(solution)/shard_map/ppermute | solution.py:37
  40.7 1.3 %collective-permute-start.12 = (f32[136,128]{1,0:T(8,128)S(1)}, f32[136,128]{1,0:T(8,128)S(1)}, u32[]{:S(2)}, u32[]{:S(2)}) collective-permute-start(f32[136,128]{1,0:T(8,128)S(1)} %add.44), channel_id=1, source_target_pairs={{0,24},{4,28},{8,16},{12,20},{16,8},{20,12},{24,0},{28,4},{1,25},{... | collective-permute-start | bytes 208904 | tf_op jit(solution)/shard_map/ppermute | solution.py:37
  42.0 0.0 collective-permute-done.10
  42.0 2.8 %collective-permute-done.11 = f32[136,128]{1,0:T(8,128)S(1)} collective-permute-done((f32[136,128]{1,0:T(8,128)S(1)}, f32[136,128]{1,0:T(8,128)S(1)}, u32[]{:S(2)}, u32[]{:S(2)}) %collective-permute-start.11) | collective-permute-done | bytes 69664 | tf_op jit(solution)/shard_map/ppermute | solution.py:37
  44.8 2.0 %collective-permute-done.12 = f32[136,128]{1,0:T(8,128)S(1)} collective-permute-done((f32[136,128]{1,0:T(8,128)S(1)}, f32[136,128]{1,0:T(8,128)S(1)}, u32[]{:S(2)}, u32[]{:S(2)}) %collective-permute-start.12) | collective-permute-done | bytes 69664 | tf_op jit(solution)/shard_map/ppermute | solution.py:37
  46.8 0.6 slice_reduce_fusion
  47.4 0.1 copy.5
  47.5 11.7 %cholesky.16 = f32[128,128]{1,0:T(8,128)S(1)} custom-call(f32[128,128]{1,0:T(8,128)S(1)} %fusion.4), custom_call_target="Cholesky" | custom-call | tf_op jit(solution)/shard_map/jit(cholesky)/cholesky | solution.py:153
  59.3 0.6 compare_reduce_fusion
  59.9 0.7 fusion
  60.6 9.8 %custom-call.8 = f32[1,128,128]{1,2,0:T(8,128)S(1)} custom-call(f32[1,128,128]{2,1,0:T(8,128)S(1)} %fusion), custom_call_target="InvertDiagBlocksLowerTriangular" | custom-call | tf_op jit(solution)/shard_map/triangular_solve | solution.py:155
  71.1 0.2 convolution_bitcast_fusion
  71.2 0.2 fusion.1
  71.4 0.2 copy.6.coeffs_ref
  71.6 0.3 shard_map.53
  71.9 0.1 collective-permute-start.13
  72.0 3.6 %collective-permute-done.13 = f32[2,1152]{1,0:T(2,128)S(1)} collective-permute-done((f32[2,1152]{1,0:T(2,128)S(1)}, f32[2,1152]{1,0:T(2,128)S(1)}, u32[]{:S(2)}, u32[]{:S(2)}) %collective-permute-start.13) | collective-permute-done | bytes 9248 | tf_op jit(solution)/shard_map/ppermute | solution.py:37
  75.7 0.6 collective-permute-start.14
  76.3 4.1 %collective-permute-done.14 = f32[4,1152]{1,0:T(4,128)S(1)} collective-permute-done((f32[4,1152]{1,0:T(4,128)S(1)}, f32[4,1152]{1,0:T(4,128)S(1)}, u32[]{:S(2)}, u32[]{:S(2)}) %collective-permute-start.14) | collective-permute-done | bytes 18464 | tf_op jit(solution)/shard_map/ppermute | solution.py:37
  80.4 0.1 collective-permute-start.15
  80.5 0.6 dynamic_slice.3
  81.1 0.6 collective-permute-done.15
  81.7 0.6 maximum_select_fusion
  (18 shorter events, 0.3 us)
Async XLA Ops:
  0.6 1.2 %copy-start = (bf16[16,2,64,256]{3,2,1,0:T(8,128)(2,1)S(1)}, bf16[16,2,64,256]{3,2,1,0:T(8,128)(2,1)}, u32[]{:S(2)}) copy-start(bf16[16,2,64,256]{3,2,1,0:T(8,128)(2,1)} %acts_ref.1) | copy-start | bytes 3145732
  1.9 0.9 %copy-start.1 = (bf16[16,2,16,256]{3,2,1,0:T(8,128)(2,1)S(1)}, bf16[16,2,16,256]{3,2,1,0:T(8,128)(2,1)}, u32[]{:S(2)}) copy-start(bf16[16,2,16,256]{3,2,1,0:T(8,128)(2,1)} %cots_ref.1) | copy-start | bytes 786436
  4.4 2.2 %collective-permute-start = (f32[1152,128]{1,0:T(8,128)S(1)}, f32[1152,128]{1,0:T(8,128)S(1)}, u32[]{:S(2)}, u32[]{:S(2)}) collective-permute-start(f32[1152,128]{1,0:T(8,128)S(1)} %get-tuple-element.14), channel_id=1, source_target_pairs={{0,4},{4,0},{8,12},{12,8},{16,20},{20,16},{24,28},{28,24},{1,5},{5... | collective-permute-start | bytes 1769480 | tf_op jit(solution)/shard_map/ppermute | solution.py:37
  4.9 0.7 copy-start.2
  6.8 10.2 %collective-permute-start.1 = (f16[18,32,128]{2,1,0:T(8,128)(2,1)S(1)}, f16[18,32,128]{2,1,0:T(8,128)(2,1)S(1)}, u32[]{:S(2)}, u32[]{:S(2)}) collective-permute-start(f16[18,32,128]{2,1,0:T(8,128)(2,1)S(1)} %convert_element_type.19), channel_id=1, source_target_pairs={{0,8},{4,12},{8,0},{12,4},{16,24},{20,28},{24,16},{28,20},{1,9},{5... | collective-permute-start | bytes 442376 | tf_op jit(solution)/shard_map/ppermute | solution.py:37
  9.9 14.5 %collective-permute-start.3 = (f16[18,32,128]{2,1,0:T(8,128)(2,1)S(1)}, f16[18,32,128]{2,1,0:T(8,128)(2,1)S(1)}, u32[]{:S(2)}, u32[]{:S(2)}) collective-permute-start(f16[18,32,128]{2,1,0:T(8,128)(2,1)S(1)} %convert_element_type.21), channel_id=1, source_target_pairs={{0,16},{4,20},{8,24},{12,28},{16,0},{20,4},{24,8},{28,12},{1,17},{... | collective-permute-start | bytes 442376 | tf_op jit(solution)/shard_map/ppermute | solution.py:37
  12.6 11.9 %collective-permute-start.5 = (f16[18,32,128]{2,1,0:T(8,128)(2,1)S(1)}, f16[18,32,128]{2,1,0:T(8,128)(2,1)S(1)}, u32[]{:S(2)}, u32[]{:S(2)}) collective-permute-start(f16[18,32,128]{2,1,0:T(8,128)(2,1)S(1)} %convert_element_type.23), channel_id=1, source_target_pairs={{0,24},{4,28},{8,16},{12,20},{16,8},{20,12},{24,0},{28,4},{1,25},{... | collective-permute-start | bytes 442376 | tf_op jit(solution)/shard_map/ppermute | solution.py:37
  12.7 11.9 %collective-permute-start.2 = (f32[24,128]{1,0:T(8,128)S(1)}, f32[24,128]{1,0:T(8,128)S(1)}, u32[]{:S(2)}, u32[]{:S(2)}) collective-permute-start(f32[24,128]{1,0:T(8,128)S(1)} %get-tuple-element.17), channel_id=1, source_target_pairs={{0,8},{4,12},{8,0},{12,4},{16,24},{20,28},{24,16},{28,20},{1,9},{5... | collective-permute-start | bytes 36872 | tf_op jit(solution)/shard_map/ppermute | solution.py:37
  13.6 13.4 %collective-permute-start.4 = (f32[24,128]{1,0:T(8,128)S(1)}, f32[24,128]{1,0:T(8,128)S(1)}, u32[]{:S(2)}, u32[]{:S(2)}) collective-permute-start(f32[24,128]{1,0:T(8,128)S(1)} %get-tuple-element.19), channel_id=1, source_target_pairs={{0,16},{4,20},{8,24},{12,28},{16,0},{20,4},{24,8},{28,12},{1,17},{... | collective-permute-start | bytes 36872 | tf_op jit(solution)/shard_map/ppermute | solution.py:37
  17.0 9.9 %collective-permute-start.6 = (f32[24,128]{1,0:T(8,128)S(1)}, f32[24,128]{1,0:T(8,128)S(1)}, u32[]{:S(2)}, u32[]{:S(2)}) collective-permute-start(f32[24,128]{1,0:T(8,128)S(1)} %get-tuple-element.21), channel_id=1, source_target_pairs={{0,24},{4,28},{8,16},{12,20},{16,8},{20,12},{24,0},{28,4},{1,25},{... | collective-permute-start | bytes 36872 | tf_op jit(solution)/shard_map/ppermute | solution.py:37
  27.4 1.3 %collective-permute-start.7 = (f32[136,128]{1,0:T(8,128)S(1)}, f32[136,128]{1,0:T(8,128)S(1)}, u32[]{:S(2)}, u32[]{:S(2)}) collective-permute-start(f32[136,128]{1,0:T(8,128)S(1)} %get-tuple-element.22), channel_id=1, source_target_pairs={{0,4},{4,0},{8,12},{12,8},{16,20},{20,16},{24,28},{28,24},{1,5},{5... | collective-permute-start | bytes 208904 | tf_op jit(solution)/shard_map/ppermute | solution.py:37
  28.8 4.4 %collective-permute-start.8 = (f32[136,128]{1,0:T(8,128)S(1)}, f32[136,128]{1,0:T(8,128)S(1)}, u32[]{:S(2)}, u32[]{:S(2)}) collective-permute-start(f32[136,128]{1,0:T(8,128)S(1)} %add.42), channel_id=1, source_target_pairs={{0,1},{1,0},{2,3},{3,2},{4,5},{5,4},{6,7},{7,6},{8,9},{9,8},{10,11... | collective-permute-start | bytes 208904 | tf_op jit(solution)/shard_map/ppermute | solution.py:37
  33.2 4.4 %collective-permute-start.9 = (f32[136,128]{1,0:T(8,128)S(1)}, f32[136,128]{1,0:T(8,128)S(1)}, u32[]{:S(2)}, u32[]{:S(2)}) collective-permute-start(f32[136,128]{1,0:T(8,128)S(1)} %add.43), channel_id=1, source_target_pairs={{0,2},{1,3},{2,0},{3,1},{4,6},{5,7},{6,4},{7,5},{8,10},{9,11},{10,... | collective-permute-start | bytes 208904 | tf_op jit(solution)/shard_map/ppermute | solution.py:37
  37.6 4.5 %collective-permute-start.10 = (f32[136,128]{1,0:T(8,128)S(1)}, f32[136,128]{1,0:T(8,128)S(1)}, u32[]{:S(2)}, u32[]{:S(2)}) collective-permute-start(f32[136,128]{1,0:T(8,128)S(1)} %add.44), channel_id=1, source_target_pairs={{0,8},{4,12},{8,0},{12,4},{16,24},{20,28},{24,16},{28,20},{1,9},{5... | collective-permute-start | bytes 208904 | tf_op jit(solution)/shard_map/ppermute | solution.py:37
  38.3 6.5 %collective-permute-start.11 = (f32[136,128]{1,0:T(8,128)S(1)}, f32[136,128]{1,0:T(8,128)S(1)}, u32[]{:S(2)}, u32[]{:S(2)}) collective-permute-start(f32[136,128]{1,0:T(8,128)S(1)} %add.44), channel_id=1, source_target_pairs={{0,16},{4,20},{8,24},{12,28},{16,0},{20,4},{24,8},{28,12},{1,17},{... | collective-permute-start | bytes 208904 | tf_op jit(solution)/shard_map/ppermute | solution.py:37
  40.7 6.1 %collective-permute-start.12 = (f32[136,128]{1,0:T(8,128)S(1)}, f32[136,128]{1,0:T(8,128)S(1)}, u32[]{:S(2)}, u32[]{:S(2)}) collective-permute-start(f32[136,128]{1,0:T(8,128)S(1)} %add.44), channel_id=1, source_target_pairs={{0,24},{4,28},{8,16},{12,20},{16,8},{20,12},{24,0},{28,4},{1,25},{... | collective-permute-start | bytes 208904 | tf_op jit(solution)/shard_map/ppermute | solution.py:37
  71.9 3.7 %collective-permute-start.13 = (f32[2,1152]{1,0:T(2,128)S(1)}, f32[2,1152]{1,0:T(2,128)S(1)}, u32[]{:S(2)}, u32[]{:S(2)}) collective-permute-start(f32[2,1152]{1,0:T(2,128)S(1)} %shard_map.53), channel_id=1, source_target_pairs={{0,8},{4,12},{8,0},{12,4},{16,24},{20,28},{24,16},{28,20},{1,9},{5... | collective-permute-start | bytes 27656 | tf_op jit(solution)/shard_map/ppermute | solution.py:37
  75.7 4.7 %collective-permute-start.14 = (f32[4,1152]{1,0:T(4,128)S(1)}, f32[4,1152]{1,0:T(4,128)S(1)}, u32[]{:S(2)}, u32[]{:S(2)}) collective-permute-start(f32[4,1152]{1,0:T(4,128)S(1)} %maximum_select_fusion.2), channel_id=1, source_target_pairs={{0,16},{4,20},{8,24},{12,28},{16,0},{20,4},{24,8},{28,12},{1,17},{... | collective-permute-start | bytes 55304 | tf_op jit(solution)/shard_map/ppermute | solution.py:37
  80.4 1.3 %collective-permute-start.15 = (f32[8,1152]{1,0:T(8,128)S(1)}, f32[8,1152]{1,0:T(8,128)S(1)}, u32[]{:S(2)}, u32[]{:S(2)}) collective-permute-start(f32[8,1152]{1,0:T(8,128)S(1)} %maximum_select_fusion.1), channel_id=1, source_target_pairs={{0,4},{4,0},{8,12},{12,8},{16,20},{20,16},{24,28},{28,24},{1,5},{5... | collective-permute-start | bytes 110600 | tf_op jit(solution)/shard_map/ppermute | solution.py:37
where the time goes:
time: 82.5 us; the launch traced here: 82.3 us
  waiting for transfers between devices  27.9 us (34%)
  other arithmetic  24.4 us (30%)
  starting transfers between devices  21.7 us (26%)
  local copies, waits for them, and re-layouts  3.73 us (5%)
  Pallas kernels  2.69 us (3%)
  between operations  1.49 us (2%)
    ppermute x16, waiting for transfers between devices, swap(): return lax.ppermute(x, axis, [(i, i ^ mask) for i in range(count)])  27.9 us
    ppermute x16, starting transfers between devices, swap(): return lax.ppermute(x, axis, [(i, i ^ mask) for i in range(count)])  21.7 us
    another operation x3, other arithmetic, solve_system(): factor = jnp.linalg.cholesky(regular)  12.4 us
    another operation x2, other arithmetic, solve_system(): lax.linalg.triangular_solve(factor, forward, left_side=True, lower=True,...  10.5 us
    unnamed x6, local copies, waits for them, and re-layouts  2.82 us
  transfers between devices with their start and end apart: 16, of which 11 were waited for; matrix products, arithmetic and copies ran while one was open for 1% of the time, Pallas kernels for 0%

commit v1 on v0

--- a/solution.py
+++ b/solution.py
@@ -124,10 +124,60 @@
     gram_ref[total : total + 8, :] = energies_ref[...]
 
 
-def update_body(scale, coeffs_ref, centered_ref, update_ref):
+def invert(matrix):
+    size = 8 * len(matrix)
+    row = lax.broadcasted_iota(jnp.int32, (8, size), 0)
+    lane = lax.broadcasted_iota(jnp.int32, (8, size), 1)
+    matrix = list(matrix)
+    for pivot in range(len(matrix)):
+        first = 8 * pivot
+        spread = [[jnp.broadcast_to(rows[:, first + c : first + c + 1], (8, size)) for c in range(8)] for rows in matrix]
+        inside = (lane >= first) & (lane < first + 8)
+        panel = jnp.where(inside, jnp.where(lane == row + first, 1.0, 0.0), matrix[pivot])
+        block = spread[pivot]
+        for step in range(8):
+            inverse = 1.0 / block[step][step : step + 1]
+            column, here = block[step], row == step
+            scaled = panel[step : step + 1] * inverse
+            panel = jnp.where(here, scaled, panel - column * scaled)
+            for c in range(step + 1, 8):
+                scaled = block[c][step : step + 1] * inverse
+                block[c] = jnp.where(here, scaled, block[c] - column * scaled)
+        for other in range(len(matrix)):
+            if other != pivot:
+                rows = jnp.where(inside, 0.0, matrix[other])
+                for c in range(8):
+                    rows = rows - spread[other][c] * panel[c : c + 1]
+                matrix[other] = rows
+        matrix[pivot] = panel
+    return matrix
+
+
+def solve_body(scale, centered_ref, *refs):
+    *part_refs, update_ref, coeffs_ref = refs
     rows, total, lanes = centered_ref.shape
-    coeffs = coeffs_ref[...] * scale
-    terms = [jnp.sum(centered_ref[row].astype(F32) * coeffs, axis=0, keepdims=True) for row in range(rows)]
+    samples = coeffs_ref.shape[1]
+    summed = part_refs[0][...]
+    for ref in part_refs[1:]:
+        summed = summed + ref[...]
+    row_index = lax.broadcasted_iota(jnp.int32, (8, total), 0)
+    lane_index = lax.broadcasted_iota(jnp.int32, (8, total), 1)
+    regular = [
+        summed[first : first + 8] + jnp.where(lane_index == row_index + first, reg_shift, 0.0) for first in range(0, total, 8)
+    ]
+    energies = summed[total : total + 1]
+    deviation = energies - jnp.sum(energies, axis=1, keepdims=True) / total
+    coeffs = jnp.concatenate([jnp.sum(part * deviation, axis=1, keepdims=True) for part in invert(regular)], axis=0)
+
+    position = lax.axis_index("samp")
+    sample = lax.broadcasted_iota(jnp.int32, (total, lanes), 0)
+    lane = lax.broadcasted_iota(jnp.int32, (total, lanes), 1)
+    spread = jnp.broadcast_to(coeffs, (total, lanes))
+    own = jnp.sum(jnp.where(sample == lane + position * samples, spread, 0.0), axis=0, keepdims=True)
+    coeffs_ref[...] = own[:, :samples]
+
+    spread = spread * scale
+    terms = [jnp.sum(centered_ref[row].astype(F32) * spread, axis=0, keepdims=True) for row in range(rows)]
     owned = rows // OFFSETS
     padded = -(-rows // 8) * 8
     table = jnp.concatenate(terms + [jnp.zeros((padded - rows, lanes), F32)], axis=0)
@@ -197,21 +247,16 @@
     while mask < lax.axis_size("par"):
         summed = summed + swap(summed, "par", mask)
         mask *= 2
-    summed = summed + sum(swap(summed, "samp", CORES * slot) for slot in range(1, chips))
-
-    energies_all = summed[total]
-    deviation = energies_all - jnp.sum(energies_all) / total
-    coeffs = solve_system(summed[:total], deviation, total)
-    local_coeffs = lax.dynamic_slice_in_dim(coeffs, position * samples, samples)
-    update = kernel_call(
-        functools.partial(update_body, -math.sqrt(params_all / total)),
-        jax.ShapeDtypeStruct((mine, OFFSETS * LANES), F32),
-    )(coeffs[:, None], centered)
+    parts = [summed] + [swap(summed, "samp", CORES * slot) for slot in range(1, chips)]
+    update, local_coeffs = kernel_call(
+        functools.partial(solve_body, -math.sqrt(params_all / total)),
+        (jax.ShapeDtypeStruct((mine, OFFSETS * LANES), F32), jax.ShapeDtypeStruct((1, samples), F32)),
+    )(centered, *parts)
     mask = CORES
     while mask < members:
         update = in_order(update, "samp", mask)
         mask *= 2
-    return in_order(update, "samp", 1), local_coeffs
+    return in_order(update, "samp", 1), local_coeffs[0]
 
 
 def local_gather(activations, cotangents, energies):

time: 82.5 us -> 62.6 us (0.76)
  other arithmetic: 24.4 us -> 0.93 us
  Pallas kernels: 2.69 us -> 7.63 us
    another operation x5 -> x0, other arithmetic: 22.9 us -> none  [the longest x3 12.4 us: solve_system(): factor = jnp.linalg.cholesky(regular)]
    pallas_call x1, Pallas kernels: 0.33 us -> 5.27 us  [local_split(): kernel_call(functools.partial(solve_body, -math.sqrt(params_all / total))...]
  transfers between devices with their start and end apart: 16 -> 16, of which waited for: 11 -> 11; matrix products, arithmetic and copies ran while one was open for 1% -> 0% of each run, Pallas kernels for 0% -> 0%
where the time goes in v1:
time: 62.6 us; the launch traced here: 62.4 us
  waiting for transfers between devices  28.5 us (46%)
  starting transfers between devices  21.7 us (35%)
  Pallas kernels  7.63 us (12%)
  local copies, waits for them, and re-layouts  2.91 us (5%)
  other arithmetic  0.93 us (1%)
  between operations  0.78 us (1%)
    ppermute x16, waiting for transfers between devices, swap(): return lax.ppermute(x, axis, [(i, i ^ mask) for i in range(count)])  28.5 us
    ppermute x16, starting transfers between devices, swap(): return lax.ppermute(x, axis, [(i, i ^ mask) for i in range(count)])  21.7 us
    pallas_call x1, Pallas kernels, local_split(): kernel_call(functools.partial(solve_body, -math.sqrt(params_all / total))...  5.27 us
    unnamed x6, local copies, waits for them, and re-layouts  2.82 us
    pallas_call x1, Pallas kernels, local_split(): kernel_call(grads_body, (half_grads, half_grads), [pltpu.VMEM((OFFSETS, s...  1.57 us
  transfers between devices with their start and end apart: 16, of which 11 were waited for; matrix products, arithmetic and copies ran while one was open for 0% of the time, Pallas kernels for 0%

profile of v1, /device:TPU:0, one launch (start us, length us, event | category | flops | bytes accessed | tf_op | source)
XLA Modules:
  0.0 62.4 jit_solution(17943941751228597914)
XLA Ops:
  0.6 0.0 copy-start
  0.6 1.2 %copy-done = bf16[16,2,64,256]{3,2,1,0:T(8,128)(2,1)S(1)} copy-done((bf16[16,2,64,256]{3,2,1,0:T(8,128)(2,1)S(1)}, bf16[16,2,64,256]{3,2,1,0:T(8,128)(2,1)}, u32[]{:S(2)}) %copy-start) | copy-done | bytes 1048600
  1.9 0.0 copy-start.1
  1.9 0.9 %copy-done.1 = bf16[16,2,16,256]{3,2,1,0:T(8,128)(2,1)S(1)} copy-done((bf16[16,2,16,256]{3,2,1,0:T(8,128)(2,1)S(1)}, bf16[16,2,16,256]{3,2,1,0:T(8,128)(2,1)}, u32[]{:S(2)}) %copy-start.1) | copy-done | bytes 262168
  2.8 1.6 %shard_map.50 = (f32[1152,128]{1,0:T(8,128)S(1)}, f32[1152,128]{1,0:T(8,128)S(1)}) custom-call(bf16[16,2,64,256]{3,2,1,0:T(8,128)(2,1)S(1)} %copy-done, bf16[16,2,16,256]{3,2,1,0:T(8,128)(2,1)S(1)} %copy-done.1), custom_call_target="tpu_custom_call" | custom-call | tf_op jit(solution)/shard_map/pallas_call | solution.py:222
  4.4 0.5 collective-permute-start
  4.9 0.0 copy-start.2
  4.9 0.7 %copy-done.2 = f32[16]{0:T(128)S(1)} copy-done((f32[16]{0:T(128)S(1)}, f32[16]{0:T(128)}, u32[]{:S(2)}) %copy-start.2) | copy-done | bytes 88
  5.6 0.1 tile.10
  5.6 0.9 %collective-permute-done = f32[1152,128]{1,0:T(8,128)S(1)} collective-permute-done((f32[1152,128]{1,0:T(8,128)S(1)}, f32[1152,128]{1,0:T(8,128)S(1)}, u32[]{:S(2)}, u32[]{:S(2)}) %collective-permute-start) | collective-permute-done | bytes 589856 | tf_op jit(solution)/shard_map/ppermute | solution.py:37
  6.5 0.3 shard_map.51
  6.8 3.0 %collective-permute-start.1 = (f16[18,32,128]{2,1,0:T(8,128)(2,1)S(1)}, f16[18,32,128]{2,1,0:T(8,128)(2,1)S(1)}, u32[]{:S(2)}, u32[]{:S(2)}) collective-permute-start(f16[18,32,128]{2,1,0:T(8,128)(2,1)S(1)} %convert_element_type.18), channel_id=1, source_target_pairs={{0,8},{4,12},{8,0},{12,4},{16,24},{20,28},{24,16},{28,20},{1,9},{5... | collective-permute-start | bytes 442376 | tf_op jit(solution)/shard_map/ppermute | solution.py:37
  9.9 2.7 %collective-permute-start.3 = (f16[18,32,128]{2,1,0:T(8,128)(2,1)S(1)}, f16[18,32,128]{2,1,0:T(8,128)(2,1)S(1)}, u32[]{:S(2)}, u32[]{:S(2)}) collective-permute-start(f16[18,32,128]{2,1,0:T(8,128)(2,1)S(1)} %convert_element_type.20), channel_id=1, source_target_pairs={{0,16},{4,20},{8,24},{12,28},{16,0},{20,4},{24,8},{28,12},{1,17},{... | collective-permute-start | bytes 442376 | tf_op jit(solution)/shard_map/ppermute | solution.py:37
  12.6 0.1 collective-permute-start.5
  12.7 0.9 %collective-permute-start.2 = (f32[24,128]{1,0:T(8,128)S(1)}, f32[24,128]{1,0:T(8,128)S(1)}, u32[]{:S(2)}, u32[]{:S(2)}) collective-permute-start(f32[24,128]{1,0:T(8,128)S(1)} %get-tuple-element.19), channel_id=1, source_target_pairs={{0,8},{4,12},{8,0},{12,4},{16,24},{20,28},{24,16},{28,20},{1,9},{5... | collective-permute-start | bytes 36872 | tf_op jit(solution)/shard_map/ppermute | solution.py:37
  13.6 3.5 %collective-permute-start.4 = (f32[24,128]{1,0:T(8,128)S(1)}, f32[24,128]{1,0:T(8,128)S(1)}, u32[]{:S(2)}, u32[]{:S(2)}) collective-permute-start(f32[24,128]{1,0:T(8,128)S(1)} %get-tuple-element.21), channel_id=1, source_target_pairs={{0,16},{4,20},{8,24},{12,28},{16,0},{20,4},{24,8},{28,12},{1,17},{... | collective-permute-start | bytes 36872 | tf_op jit(solution)/shard_map/ppermute | solution.py:37
  17.0 0.0 collective-permute-done.1
  17.0 2.7 %collective-permute-start.6 = (f32[24,128]{1,0:T(8,128)S(1)}, f32[24,128]{1,0:T(8,128)S(1)}, u32[]{:S(2)}, u32[]{:S(2)}) collective-permute-start(f32[24,128]{1,0:T(8,128)S(1)} %get-tuple-element.23), channel_id=1, source_target_pairs={{0,24},{4,28},{8,16},{12,20},{16,8},{20,12},{24,0},{28,4},{1,25},{... | collective-permute-start | bytes 36872 | tf_op jit(solution)/shard_map/ppermute | solution.py:37
  19.7 0.1 broadcast_select_fusion.energies_ref
  19.8 4.6 %collective-permute-done.3 = f16[18,32,128]{2,1,0:T(8,128)(2,1)S(1)} collective-permute-done((f16[18,32,128]{2,1,0:T(8,128)(2,1)S(1)}, f16[18,32,128]{2,1,0:T(8,128)(2,1)S(1)}, u32[]{:S(2)}, u32[]{:S(2)}) %collective-permute-start.3) | collective-permute-done | bytes 147488 | tf_op jit(solution)/shard_map/ppermute | solution.py:37
  24.5 0.0 collective-permute-done.5
  24.5 0.0 collective-permute-done.2.refs_1_
  24.5 2.4 %collective-permute-done.4.refs_3_ = f32[24,128]{1,0:T(8,128)S(1)} collective-permute-done((f32[24,128]{1,0:T(8,128)S(1)}, f32[24,128]{1,0:T(8,128)S(1)}, u32[]{:S(2)}, u32[]{:S(2)}) %collective-permute-start.4) | collective-permute-done | bytes 12320 | tf_op jit(solution)/shard_map/ppermute | solution.py:37
  26.9 0.0 collective-permute-done.6.refs_5_
  26.9 0.5 shard_map.52
  27.5 0.1 collective-permute-start.7
  27.5 1.2 %collective-permute-done.7 = f32[136,128]{1,0:T(8,128)S(1)} collective-permute-done((f32[136,128]{1,0:T(8,128)S(1)}, f32[136,128]{1,0:T(8,128)S(1)}, u32[]{:S(2)}, u32[]{:S(2)}) %collective-permute-start.7) | collective-permute-done | bytes 69664 | tf_op jit(solution)/shard_map/ppermute | solution.py:37
  28.8 1.6 %collective-permute-start.8 = (f32[136,128]{1,0:T(8,128)S(1)}, f32[136,128]{1,0:T(8,128)S(1)}, u32[]{:S(2)}, u32[]{:S(2)}) collective-permute-start(f32[136,128]{1,0:T(8,128)S(1)} %add.14), channel_id=1, source_target_pairs={{0,1},{1,0},{2,3},{3,2},{4,5},{5,4},{6,7},{7,6},{8,9},{9,8},{10,11... | collective-permute-start | bytes 208904 | tf_op jit(solution)/shard_map/ppermute | solution.py:37
  30.3 2.8 %collective-permute-done.8 = f32[136,128]{1,0:T(8,128)S(1)} collective-permute-done((f32[136,128]{1,0:T(8,128)S(1)}, f32[136,128]{1,0:T(8,128)S(1)}, u32[]{:S(2)}, u32[]{:S(2)}) %collective-permute-start.8) | collective-permute-done | bytes 69664 | tf_op jit(solution)/shard_map/ppermute | solution.py:37
  33.2 1.6 %collective-permute-start.9 = (f32[136,128]{1,0:T(8,128)S(1)}, f32[136,128]{1,0:T(8,128)S(1)}, u32[]{:S(2)}, u32[]{:S(2)}) collective-permute-start(f32[136,128]{1,0:T(8,128)S(1)} %add.15), channel_id=1, source_target_pairs={{0,2},{1,3},{2,0},{3,1},{4,6},{5,7},{6,4},{7,5},{8,10},{9,11},{10,... | collective-permute-start | bytes 208904 | tf_op jit(solution)/shard_map/ppermute | solution.py:37
  34.8 2.8 %collective-permute-done.9 = f32[136,128]{1,0:T(8,128)S(1)} collective-permute-done((f32[136,128]{1,0:T(8,128)S(1)}, f32[136,128]{1,0:T(8,128)S(1)}, u32[]{:S(2)}, u32[]{:S(2)}) %collective-permute-start.9) | collective-permute-done | bytes 69664 | tf_op jit(solution)/shard_map/ppermute | solution.py:37
  37.6 0.8 %collective-permute-start.10 = (f32[136,128]{1,0:T(8,128)S(1)}, f32[136,128]{1,0:T(8,128)S(1)}, u32[]{:S(2)}, u32[]{:S(2)}) collective-permute-start(f32[136,128]{1,0:T(8,128)S(1)} %add.16.refs_0_), channel_id=1, source_target_pairs={{0,8},{4,12},{8,0},{12,4},{16,24},{20,28},{24,16},{28,20},{1,9},{5... | collective-permute-start | bytes 208904 | tf_op jit(solution)/shard_map/ppermute | solution.py:37
  38.3 2.3 %collective-permute-start.11 = (f32[136,128]{1,0:T(8,128)S(1)}, f32[136,128]{1,0:T(8,128)S(1)}, u32[]{:S(2)}, u32[]{:S(2)}) collective-permute-start(f32[136,128]{1,0:T(8,128)S(1)} %add.16.refs_0_), channel_id=1, source_target_pairs={{0,16},{4,20},{8,24},{12,28},{16,0},{20,4},{24,8},{28,12},{1,17},{... | collective-permute-start | bytes 208904 | tf_op jit(solution)/shard_map/ppermute | solution.py:37
  40.7 1.3 %collective-permute-start.12 = (f32[136,128]{1,0:T(8,128)S(1)}, f32[136,128]{1,0:T(8,128)S(1)}, u32[]{:S(2)}, u32[]{:S(2)}) collective-permute-start(f32[136,128]{1,0:T(8,128)S(1)} %add.16.refs_0_), channel_id=1, source_target_pairs={{0,24},{4,28},{8,16},{12,20},{16,8},{20,12},{24,0},{28,4},{1,25},{... | collective-permute-start | bytes 208904 | tf_op jit(solution)/shard_map/ppermute | solution.py:37
  42.0 0.0 collective-permute-done.10.refs_1_
  42.0 2.8 %collective-permute-done.11.refs_2_ = f32[136,128]{1,0:T(8,128)S(1)} collective-permute-done((f32[136,128]{1,0:T(8,128)S(1)}, f32[136,128]{1,0:T(8,128)S(1)}, u32[]{:S(2)}, u32[]{:S(2)}) %collective-permute-start.11) | collective-permute-done | bytes 69664 | tf_op jit(solution)/shard_map/ppermute | solution.py:37
  44.8 2.0 %collective-permute-done.12.refs_3_ = f32[136,128]{1,0:T(8,128)S(1)} collective-permute-done((f32[136,128]{1,0:T(8,128)S(1)}, f32[136,128]{1,0:T(8,128)S(1)}, u32[]{:S(2)}, u32[]{:S(2)}) %collective-permute-start.12) | collective-permute-done | bytes 69664 | tf_op jit(solution)/shard_map/ppermute | solution.py:37
  46.8 5.3 %shard_map.53 = (f32[2,1152]{1,0:T(2,128)S(1)}, f32[1,16]{1,0:T(1,128)}) custom-call(bf16[18,128,128]{2,1,0:T(8,128)(2,1)S(1)} %get-tuple-element.24.centered_ref, f32[136,128]{1,0:T(8,128)S(1)} %add.16.refs_0_, f32[136,128]{1,0:T(8,128)S(1)} %collective-permute-done.10.refs_1_, f32[136,128]{1,0:T(8,128)S(1)} %collective-permute-done.11.refs_2_, ...), custom_call_target="tpu_custom_call" | custom-call | tf_op jit(solution)/shard_map/pallas_call | solution.py:251
  52.1 0.0 collective-permute-start.13
  52.1 3.7 %collective-permute-done.13 = f32[2,1152]{1,0:T(2,128)S(1)} collective-permute-done((f32[2,1152]{1,0:T(2,128)S(1)}, f32[2,1152]{1,0:T(2,128)S(1)}, u32[]{:S(2)}, u32[]{:S(2)}) %collective-permute-start.13) | collective-permute-done | bytes 9248 | tf_op jit(solution)/shard_map/ppermute | solution.py:37
  55.7 0.6 %collective-permute-start.14 = (f32[4,1152]{1,0:T(4,128)S(1)}, f32[4,1152]{1,0:T(4,128)S(1)}, u32[]{:S(2)}, u32[]{:S(2)}) collective-permute-start(f32[4,1152]{1,0:T(4,128)S(1)} %maximum_select_fusion.2), channel_id=1, source_target_pairs={{0,16},{4,20},{8,24},{12,28},{16,0},{20,4},{24,8},{28,12},{1,17},{... | collective-permute-start | bytes 55304 | tf_op jit(solution)/shard_map/ppermute | solution.py:37
  56.4 4.1 %collective-permute-done.14 = f32[4,1152]{1,0:T(4,128)S(1)} collective-permute-done((f32[4,1152]{1,0:T(4,128)S(1)}, f32[4,1152]{1,0:T(4,128)S(1)}, u32[]{:S(2)}, u32[]{:S(2)}) %collective-permute-start.14) | collective-permute-done | bytes 18464 | tf_op jit(solution)/shard_map/ppermute | solution.py:37
  60.5 0.1 collective-permute-start.15
  60.6 1.2 %collective-permute-done.15 = f32[8,1152]{1,0:T(8,128)S(1)} collective-permute-done((f32[8,1152]{1,0:T(8,128)S(1)}, f32[8,1152]{1,0:T(8,128)S(1)}, u32[]{:S(2)}, u32[]{:S(2)}) %collective-permute-start.15) | collective-permute-done | bytes 36896 | tf_op jit(solution)/shard_map/ppermute | solution.py:37
  61.8 0.6 %maximum_select_fusion = f32[16,1152]{1,0:T(8,128)} fusion(f32[8,1152]{1,0:T(8,128)S(1)} %collective-permute-done.15, f32[8,1152]{1,0:T(8,128)S(1)} %maximum_select_fusion.1, pred[]{:T(512)S(6)} %eq.30), kind=kLoop, calls=%fused_computation | loop fusion | flops 55296 | bytes 147457 | tf_op jit(solution)/shard_map/jit(_where)/select_n | solution.py:198
  (14 shorter events, 0.2 us)
Async XLA Ops:
  0.6 1.2 %copy-start = (bf16[16,2,64,256]{3,2,1,0:T(8,128)(2,1)S(1)}, bf16[16,2,64,256]{3,2,1,0:T(8,128)(2,1)}, u32[]{:S(2)}) copy-start(bf16[16,2,64,256]{3,2,1,0:T(8,128)(2,1)} %acts_ref.1) | copy-start | bytes 3145732
  1.9 0.9 %copy-start.1 = (bf16[16,2,16,256]{3,2,1,0:T(8,128)(2,1)S(1)}, bf16[16,2,16,256]{3,2,1,0:T(8,128)(2,1)}, u32[]{:S(2)}) copy-start(bf16[16,2,16,256]{3,2,1,0:T(8,128)(2,1)} %cots_ref.1) | copy-start | bytes 786436
  4.4 2.2 %collective-permute-start = (f32[1152,128]{1,0:T(8,128)S(1)}, f32[1152,128]{1,0:T(8,128)S(1)}, u32[]{:S(2)}, u32[]{:S(2)}) collective-permute-start(f32[1152,128]{1,0:T(8,128)S(1)} %get-tuple-element.16), channel_id=1, source_target_pairs={{0,4},{4,0},{8,12},{12,8},{16,20},{20,16},{24,28},{28,24},{1,5},{5... | collective-permute-start | bytes 1769480 | tf_op jit(solution)/shard_map/ppermute | solution.py:37
  4.9 0.7 %copy-start.2 = (f32[16]{0:T(128)S(1)}, f32[16]{0:T(128)}, u32[]{:S(2)}) copy-start(f32[16]{0:T(128)} %param.5) | copy-start | bytes 196
  6.8 10.2 %collective-permute-start.1 = (f16[18,32,128]{2,1,0:T(8,128)(2,1)S(1)}, f16[18,32,128]{2,1,0:T(8,128)(2,1)S(1)}, u32[]{:S(2)}, u32[]{:S(2)}) collective-permute-start(f16[18,32,128]{2,1,0:T(8,128)(2,1)S(1)} %convert_element_type.18), channel_id=1, source_target_pairs={{0,8},{4,12},{8,0},{12,4},{16,24},{20,28},{24,16},{28,20},{1,9},{5... | collective-permute-start | bytes 442376 | tf_op jit(solution)/shard_map/ppermute | solution.py:37
  9.9 14.5 %collective-permute-start.3 = (f16[18,32,128]{2,1,0:T(8,128)(2,1)S(1)}, f16[18,32,128]{2,1,0:T(8,128)(2,1)S(1)}, u32[]{:S(2)}, u32[]{:S(2)}) collective-permute-start(f16[18,32,128]{2,1,0:T(8,128)(2,1)S(1)} %convert_element_type.20), channel_id=1, source_target_pairs={{0,16},{4,20},{8,24},{12,28},{16,0},{20,4},{24,8},{28,12},{1,17},{... | collective-permute-start | bytes 442376 | tf_op jit(solution)/shard_map/ppermute | solution.py:37
  12.6 11.9 %collective-permute-start.5 = (f16[18,32,128]{2,1,0:T(8,128)(2,1)S(1)}, f16[18,32,128]{2,1,0:T(8,128)(2,1)S(1)}, u32[]{:S(2)}, u32[]{:S(2)}) collective-permute-start(f16[18,32,128]{2,1,0:T(8,128)(2,1)S(1)} %convert_element_type.22), channel_id=1, source_target_pairs={{0,24},{4,28},{8,16},{12,20},{16,8},{20,12},{24,0},{28,4},{1,25},{... | collective-permute-start | bytes 442376 | tf_op jit(solution)/shard_map/ppermute | solution.py:37
  12.7 11.9 %collective-permute-start.2 = (f32[24,128]{1,0:T(8,128)S(1)}, f32[24,128]{1,0:T(8,128)S(1)}, u32[]{:S(2)}, u32[]{:S(2)}) collective-permute-start(f32[24,128]{1,0:T(8,128)S(1)} %get-tuple-element.19), channel_id=1, source_target_pairs={{0,8},{4,12},{8,0},{12,4},{16,24},{20,28},{24,16},{28,20},{1,9},{5... | collective-permute-start | bytes 36872 | tf_op jit(solution)/shard_map/ppermute | solution.py:37
  13.6 13.4 %collective-permute-start.4 = (f32[24,128]{1,0:T(8,128)S(1)}, f32[24,128]{1,0:T(8,128)S(1)}, u32[]{:S(2)}, u32[]{:S(2)}) collective-permute-start(f32[24,128]{1,0:T(8,128)S(1)} %get-tuple-element.21), channel_id=1, source_target_pairs={{0,16},{4,20},{8,24},{12,28},{16,0},{20,4},{24,8},{28,12},{1,17},{... | collective-permute-start | bytes 36872 | tf_op jit(solution)/shard_map/ppermute | solution.py:37
  17.0 9.9 %collective-permute-start.6 = (f32[24,128]{1,0:T(8,128)S(1)}, f32[24,128]{1,0:T(8,128)S(1)}, u32[]{:S(2)}, u32[]{:S(2)}) collective-permute-start(f32[24,128]{1,0:T(8,128)S(1)} %get-tuple-element.23), channel_id=1, source_target_pairs={{0,24},{4,28},{8,16},{12,20},{16,8},{20,12},{24,0},{28,4},{1,25},{... | collective-permute-start | bytes 36872 | tf_op jit(solution)/shard_map/ppermute | solution.py:37
  27.5 1.3 %collective-permute-start.7 = (f32[136,128]{1,0:T(8,128)S(1)}, f32[136,128]{1,0:T(8,128)S(1)}, u32[]{:S(2)}, u32[]{:S(2)}) collective-permute-start(f32[136,128]{1,0:T(8,128)S(1)} %get-tuple-element.25), channel_id=1, source_target_pairs={{0,4},{4,0},{8,12},{12,8},{16,20},{20,16},{24,28},{28,24},{1,5},{5... | collective-permute-start | bytes 208904 | tf_op jit(solution)/shard_map/ppermute | solution.py:37
  28.8 4.4 %collective-permute-start.8 = (f32[136,128]{1,0:T(8,128)S(1)}, f32[136,128]{1,0:T(8,128)S(1)}, u32[]{:S(2)}, u32[]{:S(2)}) collective-permute-start(f32[136,128]{1,0:T(8,128)S(1)} %add.14), channel_id=1, source_target_pairs={{0,1},{1,0},{2,3},{3,2},{4,5},{5,4},{6,7},{7,6},{8,9},{9,8},{10,11... | collective-permute-start | bytes 208904 | tf_op jit(solution)/shard_map/ppermute | solution.py:37
  33.2 4.4 %collective-permute-start.9 = (f32[136,128]{1,0:T(8,128)S(1)}, f32[136,128]{1,0:T(8,128)S(1)}, u32[]{:S(2)}, u32[]{:S(2)}) collective-permute-start(f32[136,128]{1,0:T(8,128)S(1)} %add.15), channel_id=1, source_target_pairs={{0,2},{1,3},{2,0},{3,1},{4,6},{5,7},{6,4},{7,5},{8,10},{9,11},{10,... | collective-permute-start | bytes 208904 | tf_op jit(solution)/shard_map/ppermute | solution.py:37
  37.6 4.5 %collective-permute-start.10 = (f32[136,128]{1,0:T(8,128)S(1)}, f32[136,128]{1,0:T(8,128)S(1)}, u32[]{:S(2)}, u32[]{:S(2)}) collective-permute-start(f32[136,128]{1,0:T(8,128)S(1)} %add.16.refs_0_), channel_id=1, source_target_pairs={{0,8},{4,12},{8,0},{12,4},{16,24},{20,28},{24,16},{28,20},{1,9},{5... | collective-permute-start | bytes 208904 | tf_op jit(solution)/shard_map/ppermute | solution.py:37
  38.3 6.5 %collective-permute-start.11 = (f32[136,128]{1,0:T(8,128)S(1)}, f32[136,128]{1,0:T(8,128)S(1)}, u32[]{:S(2)}, u32[]{:S(2)}) collective-permute-start(f32[136,128]{1,0:T(8,128)S(1)} %add.16.refs_0_), channel_id=1, source_target_pairs={{0,16},{4,20},{8,24},{12,28},{16,0},{20,4},{24,8},{28,12},{1,17},{... | collective-permute-start | bytes 208904 | tf_op jit(solution)/shard_map/ppermute | solution.py:37
  40.7 6.1 %collective-permute-start.12 = (f32[136,128]{1,0:T(8,128)S(1)}, f32[136,128]{1,0:T(8,128)S(1)}, u32[]{:S(2)}, u32[]{:S(2)}) collective-permute-start(f32[136,128]{1,0:T(8,128)S(1)} %add.16.refs_0_), channel_id=1, source_target_pairs={{0,24},{4,28},{8,16},{12,20},{16,8},{20,12},{24,0},{28,4},{1,25},{... | collective-permute-start | bytes 208904 | tf_op jit(solution)/shard_map/ppermute | solution.py:37
  52.1 3.7 %collective-permute-start.13 = (f32[2,1152]{1,0:T(2,128)S(1)}, f32[2,1152]{1,0:T(2,128)S(1)}, u32[]{:S(2)}, u32[]{:S(2)}) collective-permute-start(f32[2,1152]{1,0:T(2,128)S(1)} %get-tuple-element.26), channel_id=1, source_target_pairs={{0,8},{4,12},{8,0},{12,4},{16,24},{20,28},{24,16},{28,20},{1,9},{5... | collective-permute-start | bytes 27656 | tf_op jit(solution)/shard_map/ppermute | solution.py:37
  55.7 4.7 %collective-permute-start.14 = (f32[4,1152]{1,0:T(4,128)S(1)}, f32[4,1152]{1,0:T(4,128)S(1)}, u32[]{:S(2)}, u32[]{:S(2)}) collective-permute-start(f32[4,1152]{1,0:T(4,128)S(1)} %maximum_select_fusion.2), channel_id=1, source_target_pairs={{0,16},{4,20},{8,24},{12,28},{16,0},{20,4},{24,8},{28,12},{1,17},{... | collective-permute-start | bytes 55304 | tf_op jit(solution)/shard_map/ppermute | solution.py:37
  60.5 1.3 %collective-permute-start.15 = (f32[8,1152]{1,0:T(8,128)S(1)}, f32[8,1152]{1,0:T(8,128)S(1)}, u32[]{:S(2)}, u32[]{:S(2)}) collective-permute-start(f32[8,1152]{1,0:T(8,128)S(1)} %maximum_select_fusion.1), channel_id=1, source_target_pairs={{0,4},{4,0},{8,12},{12,8},{16,20},{20,16},{24,28},{28,24},{1,5},{5... | collective-permute-start | bytes 110600 | tf_op jit(solution)/shard_map/ppermute | solution.py:37

commit v2 on v1

--- a/solution.py
+++ b/solution.py
@@ -37,13 +37,22 @@
     return lax.ppermute(x, axis, [(i, i ^ mask) for i in range(count)])
 
 
-def grads_body(acts_ref, cots_ref, keep_ref, send_ref, shifted_ref):
+def exponent(values):
+    top = jnp.maximum(jnp.max(jnp.abs(values), axis=0, keepdims=True), 1e-30)
+    return 14.0 - jnp.floor(jnp.log2(top))
+
+
+def packed_rows(rows, samples):
+    return -(-(rows * samples + rows + 2) // 8) * 8
+
+
+def grads_body(acts_ref, cots_ref, own_ref, *refs):
     samples, layers, owned, sites = cots_ref.shape
-    half = owned // CORES
-    core = lax.axis_index("samp") % CORES
-    field = cots_ref[...].reshape(samples * layers, CORES, half, sites).astype(F32)
-    swapped = jnp.concatenate([field[:, 1:], field[:, :1]], axis=1)
-    field = jnp.where(core == 1, swapped, field).reshape(samples * layers * owned, sites).astype(BF16)
+    *out_refs, shifted_ref, grads_ref = refs
+    members = len(out_refs) + 1
+    mine = owned // members
+    rows = OFFSETS * mine
+    field = cots_ref[...].reshape(samples * layers * owned, sites)
     source = lax.broadcasted_iota(jnp.int32, (sites, sites), 0)
     target = lax.broadcasted_iota(jnp.int32, (1, sites), 1)
     for offset in range(OFFSETS):
@@ -62,66 +71,95 @@
             jnp.concatenate([acts_ref[sample, layer] if layer == other else empty for other in range(layers)], axis=1)
             for layer in range(layers)
         ]
-        grads = lax.dot_general(
+        grads_ref[pl.ds(sample, OFFSETS * owned, stride=samples), :] = lax.dot_general(
             jnp.concatenate(left, axis=1),
             jnp.concatenate(right, axis=0),
             (((1,), (1,)), ((), ())),
             preferred_element_type=F32,
         )
-        for k in range(OFFSETS):
-            rows = pl.ds(k * half * samples + sample, half, stride=samples)
-            keep_ref[rows, :] = grads[k * owned : k * owned + half]
-            send_ref[rows, :] = grads[k * owned + half : (k + 1) * owned]
-
-
-def pack_body(keep_ref, recv_ref, *out_refs):
-    offsets, chips, owned, samples, lanes = keep_ref.shape
-    rows = offsets * owned
-    position = lax.axis_index("samp")
-    core, chip = position % CORES, position // CORES
-    own_ref = out_refs[0]
-    mine = pl.multiple_of(core * samples, samples)
-    other = pl.multiple_of((1 - core) * samples, samples)
-    own_ref[:, pl.ds(mine, samples), :] = keep_ref[:, chip].reshape(rows, samples, lanes)
-    own_ref[:, pl.ds(other, samples), :] = recv_ref[:, chip].reshape(rows, samples, lanes)
-    for slot in range(1, chips):
-        values_ref, side_ref = out_refs[2 * slot - 1], out_refs[2 * slot]
-        first = keep_ref[:, chip ^ slot].reshape(rows, samples, lanes)
-        second = recv_ref[:, chip ^ slot].reshape(rows, samples, lanes)
-        mean = (jnp.sum(first, axis=1) + jnp.sum(second, axis=1)) * (1.0 / (2 * samples))
-        first, second = first - mean[:, None, :], second - mean[:, None, :]
-        top = jnp.maximum(jnp.max(jnp.abs(first), axis=0), jnp.max(jnp.abs(second), axis=0))
-        top = jnp.maximum(jnp.max(top, axis=0, keepdims=True), 1e-30)
-        scale = 32768.0 / top
-        values_ref[:, pl.ds(mine, samples), :] = first * scale
-        values_ref[:, pl.ds(other, samples), :] = second * scale
-        side_ref[0:rows, :] = mean
-        side_ref[rows : rows + 1, :] = top * (1.0 / 32768.0)
+    position = lax.axis_index("samp")
+    lanes = grads_ref.shape[1]
+    for slot in range(members):
+        start = (position ^ slot) * (mine * samples)
+        pieces = [
+            grads_ref[pl.ds(pl.multiple_of(k * owned * samples + start, mine * samples), mine * samples), :] for k in range(OFFSETS)
+        ]
+        values = jnp.concatenate(pieces, axis=0).reshape(rows, samples, lanes)
+        if slot == 0:
+            own_ref[...] = values
+            continue
+        values_ref = out_refs[slot - 1]
+        reference = (jnp.sum(values, axis=1) * (1.0 / samples)).astype(BF16).astype(F32)
+        values = values - reference[:, None, :]
+        shift = exponent(jnp.max(jnp.abs(values), axis=0))
+        reference_shift = exponent(reference)
+        last = rows * samples
+        values_ref[0:last, :] = (values * jnp.exp2(shift)).reshape(last, lanes)
+        values_ref[last : last + rows, :] = reference * jnp.exp2(reference_shift)
+        values_ref[last + rows : last + rows + 1, :] = shift
+        values_ref[last + rows + 1 : last + rows + 2, :] = reference_shift
+        spare = values_ref.shape[0] - (last + rows + 2)
+        if spare:
+            values_ref[last + rows + 2 :, :] = jnp.zeros((spare, lanes), F32)
+
+
+def halves(half):
+    row = lax.broadcasted_iota(jnp.int32, (half, 2 * half), 0)
+    lane = lax.broadcasted_iota(jnp.int32, (half, 2 * half), 1)
+    return row, lane
+
+
+def fold(matrix, energies):
+    half = matrix.shape[0] // 2
+    row, lane = halves(half)
+    top, bottom = matrix[:half], matrix[half:]
+    turned = pltpu.roll(bottom, half, 1)
+    diagonal = jnp.sum(jnp.where(lane == row, turned, 0.0), axis=0, keepdims=True)
+    first = lax.broadcasted_iota(jnp.int32, energies.shape, 0) == 0
+    rest = jnp.where(first, diagonal, energies)
+    return jnp.concatenate([jnp.where((lane > row) & (lane < half), turned, top), rest], axis=0)
+
+
+def unfold(folded):
+    half = folded.shape[1] // 2
+    row, lane = halves(half)
+    body, diagonal = folded[:half], folded[half : half + 1]
+    flipped = body.T
+    mixed, crossed = flipped[:half], flipped[half:]
+    both = jnp.concatenate([mixed, crossed], axis=1)
+    top = jnp.where((lane > row) & (lane < half), both, body)
+    lower = jnp.concatenate([crossed, mixed], axis=1)
+    turned = pltpu.roll(body, half, 1)
+    place = lane - half
+    corner = jnp.where(place > row, turned, jnp.where(place == row, pltpu.roll(jnp.broadcast_to(diagonal, turned.shape), half, 1), lower))
+    return jnp.concatenate([top, jnp.where(lane < half, lower, corner)], axis=0)
 
 
 def gram_body(total, params_all, energies_ref, own_ref, *refs):
     rows, group, lanes = own_ref.shape
-    chips = total // group
-    centered_ref, gram_ref = refs[2 * (chips - 1) :]
-    chip = lax.axis_index("samp") // CORES
+    *value_refs, centered_ref, gram_ref = refs
+    by_slot = dict(zip(far_first(len(value_refs) + 1), value_refs))
+    value_refs = [by_slot[slot] for slot in sorted(by_slot)]
+    position = lax.axis_index("samp")
     gram = jnp.zeros((total, total), F32)
+    last = rows * group
+    scales = [jnp.exp2(-ref[last + rows : last + rows + 1, :]) for ref in value_refs]
+    references = [ref[last : last + rows, :] * jnp.exp2(-ref[last + rows + 1 : last + rows + 2, :]) for ref in value_refs]
     pair = []
     for row in range(rows):
         blocks = [own_ref[row]]
-        for slot in range(1, chips):
-            values_ref, side_ref = refs[2 * slot - 2], refs[2 * slot - 1]
-            blocks.append(values_ref[row] * side_ref[rows : rows + 1, :] + side_ref[row : row + 1, :])
+        for ref, scale, reference in zip(value_refs, scales, references):
+            blocks.append(ref[row * group : (row + 1) * group, :] * scale + reference[row : row + 1, :])
         mean = sum(jnp.sum(block, axis=0, keepdims=True) for block in blocks) / total
-        for slot in range(chips):
-            place = pl.ds(pl.multiple_of((chip ^ slot) * group, group), group)
+        for slot in range(len(blocks)):
+            place = pl.ds(pl.multiple_of((position ^ slot) * group, group), group)
             centered_ref[row, place, :] = ((blocks[slot] - mean) * (1.0 / math.sqrt(params_all))).astype(BF16)
         pair.append(centered_ref[row])
         if len(pair) == 2 or row == rows - 1:
             both = jnp.concatenate(pair, axis=1)
             gram = gram + lax.dot_general(both, both, (((1,), (1,)), ((), ())), preferred_element_type=F32)
             pair = []
-    gram_ref[0:total, :] = gram
-    gram_ref[total : total + 8, :] = energies_ref[...]
+    gram_ref[...] = fold(gram, energies_ref[...])
 
 
 def invert(matrix):
@@ -160,12 +198,13 @@
     summed = part_refs[0][...]
     for ref in part_refs[1:]:
         summed = summed + ref[...]
+    matrix = unfold(summed)
     row_index = lax.broadcasted_iota(jnp.int32, (8, total), 0)
     lane_index = lax.broadcasted_iota(jnp.int32, (8, total), 1)
     regular = [
-        summed[first : first + 8] + jnp.where(lane_index == row_index + first, reg_shift, 0.0) for first in range(0, total, 8)
+        matrix[first : first + 8] + jnp.where(lane_index == row_index + first, reg_shift, 0.0) for first in range(0, total, 8)
     ]
-    energies = summed[total : total + 1]
+    energies = summed[total // 2 + 1 : total // 2 + 2]
     deviation = energies - jnp.sum(energies, axis=1, keepdims=True) / total
     coeffs = jnp.concatenate([jnp.sum(part * deviation, axis=1, keepdims=True) for part in invert(regular)], axis=0)
 
@@ -192,10 +231,25 @@
             )
 
 
-def in_order(x, axis, mask):
-    other = swap(x, axis, mask)
-    low = (lax.axis_index(axis) & mask) == 0
-    return jnp.where(low, jnp.concatenate([x, other]), jnp.concatenate([other, x]))
+def far_first(members):
+    far = range(2 * CORES, members)
+    return [CORES, *far, *range(CORES + 1, 2 * CORES), *range(1, CORES)]
+
+
+def swaps(x, axis, masks):
+    return {mask: swap(x, axis, mask) for mask in sorted(masks, reverse=True)}
+
+
+def in_order(x, axis, masks):
+    blocks = {0: x, **swaps(x, axis, masks)}
+    bits = lax.axis_index(axis) & functools.reduce(lambda a, b: a | b, masks)
+    placed = []
+    for place in sorted(blocks):
+        block = blocks[0]
+        for mask in sorted(masks):
+            block = jnp.where(bits == place ^ mask, blocks[mask], block)
+        placed.append(block)
+    return jnp.concatenate(placed)
 
 
 def solve_system(gram, dev_all, total):
@@ -210,53 +264,44 @@
     owned = cotangents.shape[2]
     members = lax.axis_size("samp")
     chips = members // CORES
-    group = CORES * samples
     total = members * samples
     position = lax.axis_index("samp")
     params_all = LAYERS * C * C * OFFSETS
     mine = owned // members
     rows = OFFSETS * mine
 
-    half_rows = OFFSETS * (owned // CORES) * samples
-    half_grads = jax.ShapeDtypeStruct((half_rows, LANES), F32)
-    keep, send = kernel_call(
-        grads_body, (half_grads, half_grads), [pltpu.VMEM((OFFSETS, samples * layers * owned, sites), BF16)]
+    own = jax.ShapeDtypeStruct((rows, samples, LANES), F32)
+    block = jax.ShapeDtypeStruct((packed_rows(rows, samples), LANES), F32)
+    own, *blocks = kernel_call(
+        grads_body,
+        (own,) + (block,) * (members - 1),
+        [
+            pltpu.VMEM((OFFSETS, samples * layers * owned, sites), BF16),
+            pltpu.VMEM((OFFSETS * owned * samples, LANES), F32),
+        ],
     )(activations, cotangents)
-    recv = swap(send, "samp", 1)
-    split = (OFFSETS, chips, mine, samples, LANES)
-    block = jax.ShapeDtypeStruct((rows, group, LANES), F32)
-    side = jax.ShapeDtypeStruct((-(-(rows + 1) // 8) * 8, LANES), F32)
-    packed = kernel_call(pack_body, (block,) + (block, side) * (chips - 1))(keep.reshape(split), recv.reshape(split))
-    arrived = []
-    for slot in range(1, chips):
-        values, means = packed[2 * slot - 1], packed[2 * slot]
-        arrived.append(swap(values.astype(jnp.float16), "samp", CORES * slot).astype(F32))
-        arrived.append(swap(means, "samp", CORES * slot))
+    order = far_first(members)
+    arrived = [swap(blocks[slot - 1].astype(jnp.float16), "samp", slot).astype(F32) for slot in order]
 
     lane = jnp.arange(total) // samples
     here = (lane == position) & (lax.axis_index("par") == 0)
     spread = jnp.where(here, jnp.tile(energies, members), 0.0)
-    spread = jnp.where(jnp.arange(8)[:, None] == 0, spread[None, :], 0.0)
+    spread = jnp.where(jnp.arange(8)[:, None] == 1, spread[None, :], 0.0)
     centered, partial_gram = kernel_call(
         functools.partial(gram_body, total, params_all),
-        (jax.ShapeDtypeStruct((rows, total, LANES), BF16), jax.ShapeDtypeStruct((total + 8, total), F32)),
-    )(spread, packed[0], *arrived)
+        (jax.ShapeDtypeStruct((rows, total, LANES), BF16), jax.ShapeDtypeStruct((total // 2 + 8, total), F32)),
+    )(spread, own, *arrived)
 
     summed = partial_gram + swap(partial_gram, "samp", 1)
-    mask = 1
-    while mask < lax.axis_size("par"):
-        summed = summed + swap(summed, "par", mask)
-        mask *= 2
-    parts = [summed] + [swap(summed, "samp", CORES * slot) for slot in range(1, chips)]
+    summed = summed + sum(swaps(summed, "par", range(1, lax.axis_size("par"))).values())
+    parts = [summed, *swaps(summed, "samp", range(CORES, members, CORES)).values()]
     update, local_coeffs = kernel_call(
         functools.partial(solve_body, -math.sqrt(params_all / total)),
         (jax.ShapeDtypeStruct((mine, OFFSETS * LANES), F32), jax.ShapeDtypeStruct((1, samples), F32)),
     )(centered, *parts)
-    mask = CORES
-    while mask < members:
-        update = in_order(update, "samp", mask)
-        mask *= 2
-    return in_order(update, "samp", 1), local_coeffs[0]
+    update = in_order(update, "samp", range(1, CORES))
+    update = in_order(update, "samp", range(CORES, members, CORES))
+    return update, local_coeffs[0]
 
 
 def local_gather(activations, cotangents, energies):

time: 62.6 us -> 54 us (0.86)
  waiting for transfers between devices: 28.5 us -> 19 us
    ppermute x16 -> x18, waiting for transfers between devices: 28.5 us -> 19 us  [swap(): return lax.ppermute(x, axis, [(i, i ^ mask) for i in range(count)])]
    concatenate x0 -> x2, other arithmetic: none -> 0.67 us  [in_order(): return jnp.concatenate(placed)]
    select_n x4 -> x3, other arithmetic: 0.75 us -> 0.11 us  [the longest x1 0.07 us: local_split(): spread = jnp.where(jnp.arange(8)[:, None] == 1, spread[None, :], 0.0)]
    ppermute x16 -> x18, starting transfers between devices: 21.7 us -> 22.2 us  [swap(): return lax.ppermute(x, axis, [(i, i ^ mask) for i in range(count)])]
    pallas_call x2 -> x1, Pallas kernels: 1.84 us -> 1.92 us  [local_split(): kernel_call(grads_body, (own,) + (block,) * (members - 1), [pltpu.VMEM((O...]
  transfers between devices with their start and end apart: 16 -> 18, of which waited for: 11 -> 13; matrix products, arithmetic and copies ran while one was open for 0% -> 1% of each run, Pallas kernels for 0% -> 0%
where the time goes in v2:
time: 54 us; the launch traced here: 53.8 us
  starting transfers between devices  22.2 us (41%)
  waiting for transfers between devices  19 us (35%)
  Pallas kernels  7.95 us (15%)
  local copies, waits for them, and re-layouts  2.9 us (5%)
  other arithmetic  1 us (2%)
  between operations  0.83 us (2%)
    ppermute x18, starting transfers between devices, swap(): return lax.ppermute(x, axis, [(i, i ^ mask) for i in range(count)])  22.2 us
    ppermute x18, waiting for transfers between devices, swap(): return lax.ppermute(x, axis, [(i, i ^ mask) for i in range(count)])  19 us
    pallas_call x1, Pallas kernels, local_split(): kernel_call(functools.partial(solve_body, -math.sqrt(params_all / total))...  5.37 us
    unnamed x6, local copies, waits for them, and re-layouts  2.82 us
    pallas_call x1, Pallas kernels, local_split(): kernel_call(grads_body, (own,) + (block,) * (members - 1), [pltpu.VMEM((O...  1.92 us
  transfers between devices with their start and end apart: 18, of which 13 were waited for; matrix products, arithmetic and copies ran while one was open for 1% of the time, Pallas kernels for 0%

profile of v2, /device:TPU:0, one launch (start us, length us, event | category | flops | bytes accessed | tf_op | source)
XLA Modules:
  0.0 53.8 jit_solution(11251345284849104813)
XLA Ops:
  0.6 0.0 copy-start
  0.6 1.2 %copy-done = bf16[16,2,64,256]{3,2,1,0:T(8,128)(2,1)S(1)} copy-done((bf16[16,2,64,256]{3,2,1,0:T(8,128)(2,1)S(1)}, bf16[16,2,64,256]{3,2,1,0:T(8,128)(2,1)}, u32[]{:S(2)}) %copy-start) | copy-done | bytes 1048600
  1.9 0.0 copy-start.1
  1.9 0.9 %copy-done.1 = bf16[16,2,16,256]{3,2,1,0:T(8,128)(2,1)S(1)} copy-done((bf16[16,2,16,256]{3,2,1,0:T(8,128)(2,1)S(1)}, bf16[16,2,16,256]{3,2,1,0:T(8,128)(2,1)}, u32[]{:S(2)}) %copy-start.1) | copy-done | bytes 262168
  2.8 1.9 %shard_map.50 = (f32[18,16,128]{2,1,0:T(8,128)S(1)}, f32[312,128]{1,0:T(8,128)S(1)}, f32[312,128]{1,0:T(8,128)S(1)}, f32[312,128]{1,0:T(8,128)S(1)}, f32[312,128...) custom-call(bf16[16,2,64,256]{3,2,1,0:T(8,128)(2,1)S(1)} %copy-done, ...), custom_call_target="tpu_custom_call" | custom-call | tf_op jit(solution)/shard_map/pallas_call | solution.py:275
  4.8 3.1 %collective-permute-start = (f16[312,128]{1,0:T(8,128)(2,1)S(1)}, f16[312,128]{1,0:T(8,128)(2,1)S(1)}, u32[]{:S(2)}, u32[]{:S(2)}) collective-permute-start(f16[312,128]{1,0:T(8,128)(2,1)S(1)} %convert_element_type.42), channel_id=1, source_target_pairs={{0,8},{4,12},{8,0},{12,4},{16,24},{20,28},{24,16},{28,20},{1,9},{5... | collective-permute-start | bytes 239624 | tf_op jit(solution)/shard_map/ppermute | solution.py:37
  7.9 2.7 %collective-permute-start.1 = (f16[312,128]{1,0:T(8,128)(2,1)S(1)}, f16[312,128]{1,0:T(8,128)(2,1)S(1)}, u32[]{:S(2)}, u32[]{:S(2)}) collective-permute-start(f16[312,128]{1,0:T(8,128)(2,1)S(1)} %convert_element_type.44), channel_id=1, source_target_pairs={{0,16},{4,20},{8,24},{12,28},{16,0},{20,4},{24,8},{28,12},{1,17},{... | collective-permute-start | bytes 239624 | tf_op jit(solution)/shard_map/ppermute | solution.py:37
  10.5 0.1 collective-permute-start.2
  10.6 1.7 %collective-permute-start.3 = (f16[312,128]{1,0:T(8,128)(2,1)S(1)}, f16[312,128]{1,0:T(8,128)(2,1)S(1)}, u32[]{:S(2)}, u32[]{:S(2)}) collective-permute-start(f16[312,128]{1,0:T(8,128)(2,1)S(1)} %convert_element_type.48), channel_id=1, source_target_pairs={{0,24},{4,28},{8,16},{12,20},{16,8},{20,12},{24,0},{28,4},{1,25},{... | collective-permute-start | bytes 239624 | tf_op jit(solution)/shard_map/ppermute | solution.py:37
  12.4 2.0 %collective-permute-start.4 = (f16[312,128]{1,0:T(8,128)(2,1)S(1)}, f16[312,128]{1,0:T(8,128)(2,1)S(1)}, u32[]{:S(2)}, u32[]{:S(2)}) collective-permute-start(f16[312,128]{1,0:T(8,128)(2,1)S(1)} %convert_element_type.50), channel_id=1, source_target_pairs={{0,28},{4,24},{8,20},{12,16},{16,12},{20,8},{24,4},{28,0},{1,29},{... | collective-permute-start | bytes 239624 | tf_op jit(solution)/shard_map/ppermute | solution.py:37
  14.4 0.0 copy-start.2
  14.4 0.6 %copy-done.2 = f32[16]{0:T(128)S(1)} copy-done((f32[16]{0:T(128)S(1)}, f32[16]{0:T(128)}, u32[]{:S(2)}) %copy-start.2) | copy-done | bytes 88
  15.1 0.1 tile.10
  15.2 0.0 collective-permute-done
  15.2 0.1 collective-permute-start.5
  15.3 4.2 %collective-permute-done.1 = f16[312,128]{1,0:T(8,128)(2,1)S(1)} collective-permute-done((f16[312,128]{1,0:T(8,128)(2,1)S(1)}, f16[312,128]{1,0:T(8,128)(2,1)S(1)}, u32[]{:S(2)}, u32[]{:S(2)}) %collective-permute-start.1) | collective-permute-done | bytes 79904 | tf_op jit(solution)/shard_map/ppermute | solution.py:37
  19.5 0.0 collective-permute-start.6
  19.5 0.1 broadcast_select_fusion.2.energies_ref
  19.6 1.6 %collective-permute-done.2 = f16[312,128]{1,0:T(8,128)(2,1)S(1)} collective-permute-done((f16[312,128]{1,0:T(8,128)(2,1)S(1)}, f16[312,128]{1,0:T(8,128)(2,1)S(1)}, u32[]{:S(2)}, u32[]{:S(2)}) %collective-permute-start.2) | collective-permute-done | bytes 79904 | tf_op jit(solution)/shard_map/ppermute | solution.py:37
  21.2 0.0 collective-permute-done.3
  21.2 0.0 collective-permute-done.4
  21.2 1.7 %collective-permute-done.5 = f16[312,128]{1,0:T(8,128)(2,1)S(1)} collective-permute-done((f16[312,128]{1,0:T(8,128)(2,1)S(1)}, f16[312,128]{1,0:T(8,128)(2,1)S(1)}, u32[]{:S(2)}, u32[]{:S(2)}) %collective-permute-start.5) | collective-permute-done | bytes 79904 | tf_op jit(solution)/shard_map/ppermute | solution.py:37
  22.9 0.0 collective-permute-done.6
  23.0 0.7 %shard_map.51 = (bf16[18,128,128]{2,1,0:T(8,128)(2,1)S(1)}, f32[72,128]{1,0:T(8,128)S(1)}) custom-call(f32[8,128]{1,0:T(8,128)S(1)} %broadcast_select_fusion.2.energies_ref, f32[18,16,128]{2,1,0:T(8,128)S(1)} %get-tuple-element.14.own_ref, f32[312,128]{1,0:T(8,128)S(1)} %convert_element_type.43.refs_0_, f32[312,128]{1,0:T(8,128)S(1)} %convert_element_type.45.refs_1_, ...), custom_call_target="tpu_custom_call" | custom-call | tf_op jit(solution)/shard_map/pallas_call | solution.py:290
  23.6 0.2 collective-permute-start.7
  23.8 1.1 %collective-permute-done.7 = f32[72,128]{1,0:T(8,128)S(1)} collective-permute-done((f32[72,128]{1,0:T(8,128)S(1)}, f32[72,128]{1,0:T(8,128)S(1)}, u32[]{:S(2)}, u32[]{:S(2)}) %collective-permute-start.7) | collective-permute-done | bytes 36896 | tf_op jit(solution)/shard_map/ppermute | solution.py:37
  24.9 1.5 %collective-permute-start.10 = (f32[72,128]{1,0:T(8,128)S(1)}, f32[72,128]{1,0:T(8,128)S(1)}, u32[]{:S(2)}, u32[]{:S(2)}) collective-permute-start(f32[72,128]{1,0:T(8,128)S(1)} %add.17), channel_id=1, source_target_pairs={{0,1},{1,0},{2,3},{3,2},{4,5},{5,4},{6,7},{7,6},{8,9},{9,8},{10,11... | collective-permute-start | bytes 110600 | tf_op jit(solution)/shard_map/ppermute | solution.py:37
  26.4 1.5 %collective-permute-start.8 = (f32[72,128]{1,0:T(8,128)S(1)}, f32[72,128]{1,0:T(8,128)S(1)}, u32[]{:S(2)}, u32[]{:S(2)}) collective-permute-start(f32[72,128]{1,0:T(8,128)S(1)} %add.17), channel_id=1, source_target_pairs={{0,3},{1,2},{2,1},{3,0},{4,7},{5,6},{6,5},{7,4},{8,11},{9,10},{10,... | collective-permute-start | bytes 110600 | tf_op jit(solution)/shard_map/ppermute | solution.py:37
  27.9 0.5 collective-permute-start.9
  28.4 0.5 collective-permute-done.10
  28.9 2.4 %collective-permute-done.8 = f32[72,128]{1,0:T(8,128)S(1)} collective-permute-done((f32[72,128]{1,0:T(8,128)S(1)}, f32[72,128]{1,0:T(8,128)S(1)}, u32[]{:S(2)}, u32[]{:S(2)}) %collective-permute-start.8) | collective-permute-done | bytes 36896 | tf_op jit(solution)/shard_map/ppermute | solution.py:37
  31.3 0.6 %collective-permute-done.9 = f32[72,128]{1,0:T(8,128)S(1)} collective-permute-done((f32[72,128]{1,0:T(8,128)S(1)}, f32[72,128]{1,0:T(8,128)S(1)}, u32[]{:S(2)}, u32[]{:S(2)}) %collective-permute-start.9) | collective-permute-done | bytes 36896 | tf_op jit(solution)/shard_map/ppermute | solution.py:37
  31.9 2.7 %collective-permute-start.11 = (f32[72,128]{1,0:T(8,128)S(1)}, f32[72,128]{1,0:T(8,128)S(1)}, u32[]{:S(2)}, u32[]{:S(2)}) collective-permute-start(f32[72,128]{1,0:T(8,128)S(1)} %add_add_fusion.refs_0_), channel_id=1, source_target_pairs={{0,24},{4,28},{8,16},{12,20},{16,8},{20,12},{24,0},{28,4},{1,25},{... | collective-permute-start | bytes 110600 | tf_op jit(solution)/shard_map/ppermute | solution.py:37
  34.6 1.0 %collective-permute-start.12 = (f32[72,128]{1,0:T(8,128)S(1)}, f32[72,128]{1,0:T(8,128)S(1)}, u32[]{:S(2)}, u32[]{:S(2)}) collective-permute-start(f32[72,128]{1,0:T(8,128)S(1)} %add_add_fusion.refs_0_), channel_id=1, source_target_pairs={{0,16},{4,20},{8,24},{12,28},{16,0},{20,4},{24,8},{28,12},{1,17},{... | collective-permute-start | bytes 110600 | tf_op jit(solution)/shard_map/ppermute | solution.py:37
  35.6 0.7 %collective-permute-start.13 = (f32[72,128]{1,0:T(8,128)S(1)}, f32[72,128]{1,0:T(8,128)S(1)}, u32[]{:S(2)}, u32[]{:S(2)}) collective-permute-start(f32[72,128]{1,0:T(8,128)S(1)} %add_add_fusion.refs_0_), channel_id=1, source_target_pairs={{0,8},{4,12},{8,0},{12,4},{16,24},{20,28},{24,16},{28,20},{1,9},{5... | collective-permute-start | bytes 110600 | tf_op jit(solution)/shard_map/ppermute | solution.py:37
  36.3 1.5 %collective-permute-done.11.refs_1_ = f32[72,128]{1,0:T(8,128)S(1)} collective-permute-done((f32[72,128]{1,0:T(8,128)S(1)}, f32[72,128]{1,0:T(8,128)S(1)}, u32[]{:S(2)}, u32[]{:S(2)}) %collective-permute-start.11) | collective-permute-done | bytes 36896 | tf_op jit(solution)/shard_map/ppermute | solution.py:37
  37.8 1.7 %collective-permute-done.12.refs_2_ = f32[72,128]{1,0:T(8,128)S(1)} collective-permute-done((f32[72,128]{1,0:T(8,128)S(1)}, f32[72,128]{1,0:T(8,128)S(1)}, u32[]{:S(2)}, u32[]{:S(2)}) %collective-permute-start.12) | collective-permute-done | bytes 36896 | tf_op jit(solution)/shard_map/ppermute | solution.py:37
  39.5 0.4 collective-permute-done.13.refs_3_
  39.9 5.4 %shard_map.52 = (f32[2,1152]{1,0:T(2,128)S(1)}, f32[1,16]{1,0:T(1,128)}) custom-call(bf16[18,128,128]{2,1,0:T(8,128)(2,1)S(1)} %get-tuple-element.22.centered_ref, f32[72,128]{1,0:T(8,128)S(1)} %add_add_fusion.refs_0_, f32[72,128]{1,0:T(8,128)S(1)} %collective-permute-done.11.refs_1_, f32[72,128]{1,0:T(8,128)S(1)} %collective-permute-done.12.refs_2_, ...), custom_call_target="tpu_custom_call" | custom-call | tf_op jit(solution)/shard_map/pallas_call | solution.py:298
  45.2 0.0 collective-permute-start.14
  45.2 1.2 %collective-permute-done.14 = f32[2,1152]{1,0:T(2,128)S(1)} collective-permute-done((f32[2,1152]{1,0:T(2,128)S(1)}, f32[2,1152]{1,0:T(2,128)S(1)}, u32[]{:S(2)}, u32[]{:S(2)}) %collective-permute-start.14) | collective-permute-done | bytes 9248 | tf_op jit(solution)/shard_map/ppermute | solution.py:37
  46.4 2.1 %collective-permute-start.15 = (f32[4,1152]{1,0:T(4,128)S(1)}, f32[4,1152]{1,0:T(4,128)S(1)}, u32[]{:S(2)}, u32[]{:S(2)}) collective-permute-start(f32[4,1152]{1,0:T(4,128)S(1)} %pad_maximum_fusion.1), channel_id=1, source_target_pairs={{0,24},{4,28},{8,16},{12,20},{16,8},{20,12},{24,0},{28,4},{1,25},{... | collective-permute-start | bytes 55304 | tf_op jit(solution)/shard_map/ppermute | solution.py:37
  48.5 0.0 collective-permute-start.16
  48.5 2.4 %collective-permute-start.17 = (f32[4,1152]{1,0:T(4,128)S(1)}, f32[4,1152]{1,0:T(4,128)S(1)}, u32[]{:S(2)}, u32[]{:S(2)}) collective-permute-start(f32[4,1152]{1,0:T(4,128)S(1)} %pad_maximum_fusion.1), channel_id=1, source_target_pairs={{0,8},{4,12},{8,0},{12,4},{16,24},{20,28},{24,16},{28,20},{1,9},{5... | collective-permute-start | bytes 55304 | tf_op jit(solution)/shard_map/ppermute | solution.py:37
  50.9 1.3 %collective-permute-done.15 = f32[4,1152]{1,0:T(4,128)S(1)} collective-permute-done((f32[4,1152]{1,0:T(4,128)S(1)}, f32[4,1152]{1,0:T(4,128)S(1)}, u32[]{:S(2)}, u32[]{:S(2)}) %collective-permute-start.15) | collective-permute-done | bytes 18464 | tf_op jit(solution)/shard_map/ppermute | solution.py:37
  52.2 1.0 %collective-permute-done.16 = f32[4,1152]{1,0:T(4,128)S(1)} collective-permute-done((f32[4,1152]{1,0:T(4,128)S(1)}, f32[4,1152]{1,0:T(4,128)S(1)}, u32[]{:S(2)}, u32[]{:S(2)}) %collective-permute-start.16) | collective-permute-done | bytes 18464 | tf_op jit(solution)/shard_map/ppermute | solution.py:37
  53.2 0.0 collective-permute-done.17
  53.2 0.7 %pad_maximum_fusion = f32[16,1152]{1,0:T(8,128)} fusion(f32[4,1152]{1,0:T(4,128)S(1)} %get-tuple-element.27, f32[4,1152]{1,0:T(4,128)S(1)} %get-tuple-element.28, f32[4,1152]{1,0:T(4,128)S(1)} %get-tuple-element.29, f32[4,1152]{1,0:T(4,128)S(1)} %get-tuple-element.26), kind=kLoop, calls=%fused_computation | loop fusion | flops 55296 | bytes 147456 | tf_op jit(solution)/shard_map/concatenate | solution.py:252
  (22 shorter events, 0.3 us)
Async XLA Ops:
  0.6 1.2 %copy-start = (bf16[16,2,64,256]{3,2,1,0:T(8,128)(2,1)S(1)}, bf16[16,2,64,256]{3,2,1,0:T(8,128)(2,1)}, u32[]{:S(2)}) copy-start(bf16[16,2,64,256]{3,2,1,0:T(8,128)(2,1)} %acts_ref.1) | copy-start | bytes 3145732
  1.9 0.9 %copy-start.1 = (bf16[16,2,16,256]{3,2,1,0:T(8,128)(2,1)S(1)}, bf16[16,2,16,256]{3,2,1,0:T(8,128)(2,1)}, u32[]{:S(2)}) copy-start(bf16[16,2,16,256]{3,2,1,0:T(8,128)(2,1)} %cots_ref.1) | copy-start | bytes 786436
  4.8 10.4 %collective-permute-start = (f16[312,128]{1,0:T(8,128)(2,1)S(1)}, f16[312,128]{1,0:T(8,128)(2,1)S(1)}, u32[]{:S(2)}, u32[]{:S(2)}) collective-permute-start(f16[312,128]{1,0:T(8,128)(2,1)S(1)} %convert_element_type.42), channel_id=1, source_target_pairs={{0,8},{4,12},{8,0},{12,4},{16,24},{20,28},{24,16},{28,20},{1,9},{5... | collective-permute-start | bytes 239624 | tf_op jit(solution)/shard_map/ppermute | solution.py:37
  7.9 11.6 %collective-permute-start.1 = (f16[312,128]{1,0:T(8,128)(2,1)S(1)}, f16[312,128]{1,0:T(8,128)(2,1)S(1)}, u32[]{:S(2)}, u32[]{:S(2)}) collective-permute-start(f16[312,128]{1,0:T(8,128)(2,1)S(1)} %convert_element_type.44), channel_id=1, source_target_pairs={{0,16},{4,20},{8,24},{12,28},{16,0},{20,4},{24,8},{28,12},{1,17},{... | collective-permute-start | bytes 239624 | tf_op jit(solution)/shard_map/ppermute | solution.py:37
  10.5 10.6 %collective-permute-start.2 = (f16[312,128]{1,0:T(8,128)(2,1)S(1)}, f16[312,128]{1,0:T(8,128)(2,1)S(1)}, u32[]{:S(2)}, u32[]{:S(2)}) collective-permute-start(f16[312,128]{1,0:T(8,128)(2,1)S(1)} %convert_element_type.46), channel_id=1, source_target_pairs={{0,20},{4,16},{8,28},{12,24},{16,4},{20,0},{24,12},{28,8},{1,21},{... | collective-permute-start | bytes 239624 | tf_op jit(solution)/shard_map/ppermute | solution.py:37
  10.6 10.5 %collective-permute-start.3 = (f16[312,128]{1,0:T(8,128)(2,1)S(1)}, f16[312,128]{1,0:T(8,128)(2,1)S(1)}, u32[]{:S(2)}, u32[]{:S(2)}) collective-permute-start(f16[312,128]{1,0:T(8,128)(2,1)S(1)} %convert_element_type.48), channel_id=1, source_target_pairs={{0,24},{4,28},{8,16},{12,20},{16,8},{20,12},{24,0},{28,4},{1,25},{... | collective-permute-start | bytes 239624 | tf_op jit(solution)/shard_map/ppermute | solution.py:37
  12.4 8.8 %collective-permute-start.4 = (f16[312,128]{1,0:T(8,128)(2,1)S(1)}, f16[312,128]{1,0:T(8,128)(2,1)S(1)}, u32[]{:S(2)}, u32[]{:S(2)}) collective-permute-start(f16[312,128]{1,0:T(8,128)(2,1)S(1)} %convert_element_type.50), channel_id=1, source_target_pairs={{0,28},{4,24},{8,20},{12,16},{16,12},{20,8},{24,4},{28,0},{1,29},{... | collective-permute-start | bytes 239624 | tf_op jit(solution)/shard_map/ppermute | solution.py:37
  14.4 0.7 %copy-start.2 = (f32[16]{0:T(128)S(1)}, f32[16]{0:T(128)}, u32[]{:S(2)}) copy-start(f32[16]{0:T(128)} %param.5) | copy-start | bytes 196
  15.2 7.7 %collective-permute-start.5 = (f16[312,128]{1,0:T(8,128)(2,1)S(1)}, f16[312,128]{1,0:T(8,128)(2,1)S(1)}, u32[]{:S(2)}, u32[]{:S(2)}) collective-permute-start(f16[312,128]{1,0:T(8,128)(2,1)S(1)} %convert_element_type.52), channel_id=1, source_target_pairs={{0,12},{4,8},{8,4},{12,0},{16,28},{20,24},{24,20},{28,16},{1,13},{... | collective-permute-start | bytes 239624 | tf_op jit(solution)/shard_map/ppermute | solution.py:37
  19.5 3.5 %collective-permute-start.6 = (f16[312,128]{1,0:T(8,128)(2,1)S(1)}, f16[312,128]{1,0:T(8,128)(2,1)S(1)}, u32[]{:S(2)}, u32[]{:S(2)}) collective-permute-start(f16[312,128]{1,0:T(8,128)(2,1)S(1)} %convert_element_type.54), channel_id=1, source_target_pairs={{0,4},{4,0},{8,12},{12,8},{16,20},{20,16},{24,28},{28,24},{1,5},{5... | collective-permute-start | bytes 239624 | tf_op jit(solution)/shard_map/ppermute | solution.py:37
  23.6 1.3 %collective-permute-start.7 = (f32[72,128]{1,0:T(8,128)S(1)}, f32[72,128]{1,0:T(8,128)S(1)}, u32[]{:S(2)}, u32[]{:S(2)}) collective-permute-start(f32[72,128]{1,0:T(8,128)S(1)} %get-tuple-element.23), channel_id=1, source_target_pairs={{0,4},{4,0},{8,12},{12,8},{16,20},{20,16},{24,28},{28,24},{1,5},{5... | collective-permute-start | bytes 110600 | tf_op jit(solution)/shard_map/ppermute | solution.py:37
  24.9 4.0 %collective-permute-start.10 = (f32[72,128]{1,0:T(8,128)S(1)}, f32[72,128]{1,0:T(8,128)S(1)}, u32[]{:S(2)}, u32[]{:S(2)}) collective-permute-start(f32[72,128]{1,0:T(8,128)S(1)} %add.17), channel_id=1, source_target_pairs={{0,1},{1,0},{2,3},{3,2},{4,5},{5,4},{6,7},{7,6},{8,9},{9,8},{10,11... | collective-permute-start | bytes 110600 | tf_op jit(solution)/shard_map/ppermute | solution.py:37
  26.4 4.9 %collective-permute-start.8 = (f32[72,128]{1,0:T(8,128)S(1)}, f32[72,128]{1,0:T(8,128)S(1)}, u32[]{:S(2)}, u32[]{:S(2)}) collective-permute-start(f32[72,128]{1,0:T(8,128)S(1)} %add.17), channel_id=1, source_target_pairs={{0,3},{1,2},{2,1},{3,0},{4,7},{5,6},{6,5},{7,4},{8,11},{9,10},{10,... | collective-permute-start | bytes 110600 | tf_op jit(solution)/shard_map/ppermute | solution.py:37
  27.9 4.0 %collective-permute-start.9 = (f32[72,128]{1,0:T(8,128)S(1)}, f32[72,128]{1,0:T(8,128)S(1)}, u32[]{:S(2)}, u32[]{:S(2)}) collective-permute-start(f32[72,128]{1,0:T(8,128)S(1)} %add.17), channel_id=1, source_target_pairs={{0,2},{1,3},{2,0},{3,1},{4,6},{5,7},{6,4},{7,5},{8,10},{9,11},{10,... | collective-permute-start | bytes 110600 | tf_op jit(solution)/shard_map/ppermute | solution.py:37
  31.9 5.9 %collective-permute-start.11 = (f32[72,128]{1,0:T(8,128)S(1)}, f32[72,128]{1,0:T(8,128)S(1)}, u32[]{:S(2)}, u32[]{:S(2)}) collective-permute-start(f32[72,128]{1,0:T(8,128)S(1)} %add_add_fusion.refs_0_), channel_id=1, source_target_pairs={{0,24},{4,28},{8,16},{12,20},{16,8},{20,12},{24,0},{28,4},{1,25},{... | collective-permute-start | bytes 110600 | tf_op jit(solution)/shard_map/ppermute | solution.py:37
  34.6 4.9 %collective-permute-start.12 = (f32[72,128]{1,0:T(8,128)S(1)}, f32[72,128]{1,0:T(8,128)S(1)}, u32[]{:S(2)}, u32[]{:S(2)}) collective-permute-start(f32[72,128]{1,0:T(8,128)S(1)} %add_add_fusion.refs_0_), channel_id=1, source_target_pairs={{0,16},{4,20},{8,24},{12,28},{16,0},{20,4},{24,8},{28,12},{1,17},{... | collective-permute-start | bytes 110600 | tf_op jit(solution)/shard_map/ppermute | solution.py:37
  35.6 4.3 %collective-permute-start.13 = (f32[72,128]{1,0:T(8,128)S(1)}, f32[72,128]{1,0:T(8,128)S(1)}, u32[]{:S(2)}, u32[]{:S(2)}) collective-permute-start(f32[72,128]{1,0:T(8,128)S(1)} %add_add_fusion.refs_0_), channel_id=1, source_target_pairs={{0,8},{4,12},{8,0},{12,4},{16,24},{20,28},{24,16},{28,20},{1,9},{5... | collective-permute-start | bytes 110600 | tf_op jit(solution)/shard_map/ppermute | solution.py:37
  45.2 1.2 %collective-permute-start.14 = (f32[2,1152]{1,0:T(2,128)S(1)}, f32[2,1152]{1,0:T(2,128)S(1)}, u32[]{:S(2)}, u32[]{:S(2)}) collective-permute-start(f32[2,1152]{1,0:T(2,128)S(1)} %get-tuple-element.24), channel_id=1, source_target_pairs={{0,4},{4,0},{8,12},{12,8},{16,20},{20,16},{24,28},{28,24},{1,5},{5... | collective-permute-start | bytes 27656 | tf_op jit(solution)/shard_map/ppermute | solution.py:37
  46.4 5.7 %collective-permute-start.15 = (f32[4,1152]{1,0:T(4,128)S(1)}, f32[4,1152]{1,0:T(4,128)S(1)}, u32[]{:S(2)}, u32[]{:S(2)}) collective-permute-start(f32[4,1152]{1,0:T(4,128)S(1)} %pad_maximum_fusion.1), channel_id=1, source_target_pairs={{0,24},{4,28},{8,16},{12,20},{16,8},{20,12},{24,0},{28,4},{1,25},{... | collective-permute-start | bytes 55304 | tf_op jit(solution)/shard_map/ppermute | solution.py:37
  48.5 4.7 %collective-permute-start.16 = (f32[4,1152]{1,0:T(4,128)S(1)}, f32[4,1152]{1,0:T(4,128)S(1)}, u32[]{:S(2)}, u32[]{:S(2)}) collective-permute-start(f32[4,1152]{1,0:T(4,128)S(1)} %pad_maximum_fusion.1), channel_id=1, source_target_pairs={{0,16},{4,20},{8,24},{12,28},{16,0},{20,4},{24,8},{28,12},{1,17},{... | collective-permute-start | bytes 55304 | tf_op jit(solution)/shard_map/ppermute | solution.py:37
  48.5 4.6 %collective-permute-start.17 = (f32[4,1152]{1,0:T(4,128)S(1)}, f32[4,1152]{1,0:T(4,128)S(1)}, u32[]{:S(2)}, u32[]{:S(2)}) collective-permute-start(f32[4,1152]{1,0:T(4,128)S(1)} %pad_maximum_fusion.1), channel_id=1, source_target_pairs={{0,8},{4,12},{8,0},{12,4},{16,24},{20,28},{24,16},{28,20},{1,9},{5... | collective-permute-start | bytes 55304 | tf_op jit(solution)/shard_map/ppermute | solution.py:37

commit v3 on v2

--- a/solution.py
+++ b/solution.py
@@ -23,10 +23,11 @@
 VMEM_LIMIT = 48 * 1024 * 1024
 
 
-def kernel_call(body, out_shape, scratch_shapes=()):
+def kernel_call(body, out_shape, scratch_shapes=(), **options):
     return pl.pallas_call(
         body,
         out_shape=out_shape,
+        **options,
         scratch_shapes=scratch_shapes,
         compiler_params=pltpu.CompilerParams(vmem_limit_bytes=VMEM_LIMIT),
     )
@@ -46,49 +47,58 @@
     return -(-(rows * samples + rows + 2) // 8) * 8
 
 
-def grads_body(acts_ref, cots_ref, own_ref, *refs):
+def grads_body(far, acts_hbm, cots_hbm, *refs):
+    *out_refs, acts_ref, cots_ref, shifted_ref, grads_ref, semaphores = refs
+    copies = [
+        pltpu.make_async_copy(cots_hbm, cots_ref, semaphores.at[0]),
+        pltpu.make_async_copy(acts_hbm, acts_ref, semaphores.at[1]),
+    ]
+    for copy in copies:
+        copy.start()
     samples, layers, owned, sites = cots_ref.shape
-    *out_refs, shifted_ref, grads_ref = refs
-    members = len(out_refs) + 1
+    members = len(out_refs)
+    owned = owned // 2
     mine = owned // members
     rows = OFFSETS * mine
-    field = cots_ref[...].reshape(samples * layers * owned, sites)
+    moves = []
     source = lax.broadcasted_iota(jnp.int32, (sites, sites), 0)
     target = lax.broadcasted_iota(jnp.int32, (1, sites), 1)
     for offset in range(OFFSETS):
         row, col = target // SIDE, target % SIDE
         row = (row + SIDE - (offset // 3 - 1)) % SIDE
         col = (col + SIDE - (offset % 3 - 1)) % SIDE
-        move = jnp.where(source == row * SIDE + col, 1.0, 0.0).astype(BF16)
-        shifted_ref[offset] = jnp.dot(field, move, preferred_element_type=F32).astype(BF16)
-    empty = jnp.zeros((C, sites), BF16)
+        moves.append(jnp.where(source == row * SIDE + col, 1.0, 0.0).astype(BF16))
+    position = lax.axis_index("samp")
+    upper = (position // members + int(far)) % 2 == 1
+    copies[0].wait()
+    field = cots_ref[...].astype(F32).reshape(samples * layers, 2, owned, sites)
+    field = jnp.where(upper, field[:, 1], field[:, 0]).reshape(samples * layers * owned, sites).astype(BF16)
+    for offset in range(OFFSETS):
+        shifted_ref[offset] = jnp.dot(field, moves[offset], preferred_element_type=F32).astype(BF16)
+    copies[1].wait()
+    lanes = grads_ref.shape[1]
+    lane = lax.broadcasted_iota(jnp.int32, (OFFSETS, owned, lanes), 2)
     for sample in range(samples):
-        left = []
-        for layer in range(layers):
-            first = (sample * layers + layer) * owned
-            left.append(jnp.concatenate([shifted_ref[k, first : first + owned, :] for k in range(OFFSETS)], axis=0))
-        right = [
-            jnp.concatenate([acts_ref[sample, layer] if layer == other else empty for other in range(layers)], axis=1)
-            for layer in range(layers)
-        ]
-        grads_ref[pl.ds(sample, OFFSETS * owned, stride=samples), :] = lax.dot_general(
-            jnp.concatenate(left, axis=1),
-            jnp.concatenate(right, axis=0),
-            (((1,), (1,)), ((), ())),
-            preferred_element_type=F32,
-        )
-    position = lax.axis_index("samp")
-    lanes = grads_ref.shape[1]
-    for slot in range(members):
-        start = (position ^ slot) * (mine * samples)
+        first = sample * layers * owned
+        left = jnp.concatenate([shifted_ref[k, first : first + layers * owned, :] for k in range(OFFSETS)], axis=0)
+        right = acts_ref[sample].reshape(layers * C, sites)
+        products = lax.dot_general(left, right, (((1,), (1,)), ((), ())), preferred_element_type=F32)
+        products = products.reshape(OFFSETS, layers, owned, lanes)
+        grads = products[:, 0]
+        for layer in range(1, layers):
+            grads = jnp.where(lane >= layer * C, products[:, layer], grads)
+        grads_ref[pl.ds(sample, OFFSETS * owned, stride=samples), :] = grads.reshape(OFFSETS * owned, lanes)
+    for index in range(members):
+        slot = index + members * int(far)
+        start = ((position ^ slot) % members) * (mine * samples)
         pieces = [
             grads_ref[pl.ds(pl.multiple_of(k * owned * samples + start, mine * samples), mine * samples), :] for k in range(OFFSETS)
         ]
         values = jnp.concatenate(pieces, axis=0).reshape(rows, samples, lanes)
+        values_ref = out_refs[index]
         if slot == 0:
-            own_ref[...] = values
+            values_ref[...] = values
             continue
-        values_ref = out_refs[slot - 1]
         reference = (jnp.sum(values, axis=1) * (1.0 / samples)).astype(BF16).astype(F32)
         values = values - reference[:, None, :]
         shift = exponent(jnp.max(jnp.abs(values), axis=0))
@@ -162,32 +172,69 @@
     gram_ref[...] = fold(gram, energies_ref[...])
 
 
+def thirds(values):
+    high = values.astype(BF16).astype(F32)
+    middle = (values - high).astype(BF16).astype(F32)
+    return high, middle, values - high - middle
+
+
+def outer_sum(left, right):
+    a, b, c = thirds(left)
+    d, e, f = thirds(right)
+    lefts = jnp.concatenate([a, a, b, a, b, c], axis=0).astype(BF16)
+    rights = jnp.concatenate([d, e, d, f, e, d], axis=0).astype(BF16)
+    return lax.dot_general(lefts, rights, (((0,), (0,)), ((), ())), preferred_element_type=F32)
+
+
+def spread_lane(rows, lane):
+    return jnp.broadcast_to(rows[:, lane : lane + 1], rows.shape)
+
+
+def eliminate(block, panel, row):
+    block = list(block)
+    for step in range(0, 8, 2):
+        one, two = block[step], block[step + 1]
+        a, b, c = one[step : step + 1], two[step : step + 1], two[step + 1 : step + 2]
+        inverse = 1.0 / (a * c - b * b)
+
+        def reduced(rows):
+            upper, lower = rows[step : step + 1], rows[step + 1 : step + 2]
+            first, second = (c * upper - b * lower) * inverse, (a * lower - b * upper) * inverse
+            rest = rows - (one * first + two * second)
+            return jnp.where(row == step, first, jnp.where(row == step + 1, second, rest))
+
+        panel = reduced(panel)
+        block = [reduced(rows) if c >= step + 2 else rows for c, rows in enumerate(block)]
+    return panel
+
+
 def invert(matrix):
-    size = 8 * len(matrix)
+    matrix = list(matrix)
+    count, size = len(matrix), 8 * len(matrix)
     row = lax.broadcasted_iota(jnp.int32, (8, size), 0)
     lane = lax.broadcasted_iota(jnp.int32, (8, size), 1)
-    matrix = list(matrix)
-    for pivot in range(len(matrix)):
-        first = 8 * pivot
-        spread = [[jnp.broadcast_to(rows[:, first + c : first + c + 1], (8, size)) for c in range(8)] for rows in matrix]
+    pivot = matrix[0]
+    for index in range(count):
+        first = 8 * index
         inside = (lane >= first) & (lane < first + 8)
-        panel = jnp.where(inside, jnp.where(lane == row + first, 1.0, 0.0), matrix[pivot])
-        block = spread[pivot]
-        for step in range(8):
-            inverse = 1.0 / block[step][step : step + 1]
-            column, here = block[step], row == step
-            scaled = panel[step : step + 1] * inverse
-            panel = jnp.where(here, scaled, panel - column * scaled)
-            for c in range(step + 1, 8):
-                scaled = block[c][step : step + 1] * inverse
-                block[c] = jnp.where(here, scaled, block[c] - column * scaled)
-        for other in range(len(matrix)):
-            if other != pivot:
-                rows = jnp.where(inside, 0.0, matrix[other])
-                for c in range(8):
-                    rows = rows - spread[other][c] * panel[c : c + 1]
-                matrix[other] = rows
-        matrix[pivot] = panel
+        unit = jnp.where(lane == row + first, 1.0, 0.0)
+        solved = eliminate([spread_lane(pivot, first + c) for c in range(8)], jnp.where(inside, unit, pivot), row)
+        solved = jnp.where(inside, -solved, solved)
+        update = outer_sum(jnp.where(inside, 0.0, pivot), solved)
+        following = None
+        if index + 1 < count:
+            terms = [spread_lane(matrix[index + 1], first + c) * solved[c : c + 1] for c in range(8)]
+            while len(terms) > 1:
+                terms = [one + two for one, two in zip(terms[::2], terms[1::2])]
+            following = jnp.where(inside, 0.0, matrix[index + 1]) - terms[0]
+        for other in range(count):
+            if other == index:
+                matrix[other] = solved
+            elif other == index + 1:
+                matrix[other] = following
+            else:
+                matrix[other] = jnp.where(inside, 0.0, matrix[other]) - update[8 * other : 8 * other + 8]
+        pivot = following
     return matrix
 
 
@@ -206,7 +253,7 @@
     ]
     energies = summed[total // 2 + 1 : total // 2 + 2]
     deviation = energies - jnp.sum(energies, axis=1, keepdims=True) / total
-    coeffs = jnp.concatenate([jnp.sum(part * deviation, axis=1, keepdims=True) for part in invert(regular)], axis=0)
+    coeffs = jnp.concatenate([-jnp.sum(part * deviation, axis=1, keepdims=True) for part in invert(regular)], axis=0)
 
     position = lax.axis_index("samp")
     sample = lax.broadcasted_iota(jnp.int32, (total, lanes), 0)
@@ -232,8 +279,7 @@
 
 
 def far_first(members):
-    far = range(2 * CORES, members)
-    return [CORES, *far, *range(CORES + 1, 2 * CORES), *range(1, CORES)]
+    return [*range(members // 2, members), *range(CORES, members // 2), *range(1, CORES)]
 
 
 def swaps(x, axis, masks):
@@ -272,14 +318,25 @@
 
     own = jax.ShapeDtypeStruct((rows, samples, LANES), F32)
     block = jax.ShapeDtypeStruct((packed_rows(rows, samples), LANES), F32)
-    own, *blocks = kernel_call(
-        grads_body,
-        (own,) + (block,) * (members - 1),
-        [
-            pltpu.VMEM((OFFSETS, samples * layers * owned, sites), BF16),
-            pltpu.VMEM((OFFSETS * owned * samples, LANES), F32),
-        ],
-    )(activations, cotangents)
+    inputs = [pltpu.with_memory_space_constraint(x, pltpu.HBM) for x in (activations, cotangents)]
+
+    def half(far, out_shape):
+        return kernel_call(
+            functools.partial(grads_body, far),
+            out_shape,
+            [
+                pltpu.VMEM(activations.shape, BF16),
+                pltpu.VMEM(cotangents.shape, BF16),
+                pltpu.VMEM((OFFSETS, samples * layers * owned // 2, sites), BF16),
+                pltpu.VMEM((OFFSETS * owned // 2 * samples, LANES), F32),
+                pltpu.SemaphoreType.DMA((2,)),
+            ],
+            in_specs=[pl.BlockSpec(memory_space=pltpu.HBM)] * 2,
+        )(*inputs)
+
+    far_blocks = half(True, (block,) * (members // 2))
+    own, *near_blocks = half(False, (own,) + (block,) * (members // 2 - 1))
+    blocks = [*near_blocks, *far_blocks]
     order = far_first(members)
     arrived = [swap(blocks[slot - 1].astype(jnp.float16), "samp", slot).astype(F32) for slot in order]
 

time: 54 us -> 51.4 us (0.952)
  waiting for transfers between devices: 19 us -> 16.3 us
  local copies, waits for them, and re-layouts: 2.9 us -> 0.73 us
  Pallas kernels: 7.95 us -> 9.26 us
  starting transfers between devices: 22.2 us -> 23.1 us
    ppermute x18, waiting for transfers between devices: 19 us -> 16.3 us  [swap(): return lax.ppermute(x, axis, [(i, i ^ mask) for i in range(count)])]
    pallas_call x1 -> x2, Pallas kernels: 1.92 us -> 4.3 us  [half(): kernel_call(functools.partial(grads_body, far), out_shape, [pltpu.VMEM(ac...]
    unnamed x6 -> x2, local copies, waits for them, and re-layouts: 2.82 us -> 0.65 us
    pallas_call x1, Pallas kernels: 5.37 us -> 4.3 us  [local_split(): kernel_call(functools.partial(solve_body, -math.sqrt(params_all / total))...]
    ppermute x18, starting transfers between devices: 22.2 us -> 23.1 us  [swap(): return lax.ppermute(x, axis, [(i, i ^ mask) for i in range(count)])]
  transfers between devices with their start and end apart: 18 -> 18, of which waited for: 13 -> 13; matrix products, arithmetic and copies ran while one was open for 1% -> 1% of each run, Pallas kernels for 0% -> 4%
where the time goes in v3:
time: 51.4 us; the launch traced here: 51.2 us
  starting transfers between devices  23.1 us (45%)
  waiting for transfers between devices  16.3 us (32%)
  Pallas kernels  9.26 us (18%)
  other arithmetic  1 us (2%)
  between operations  0.85 us (2%)
  local copies, waits for them, and re-layouts  0.73 us (1%)
    ppermute x18, starting transfers between devices, swap(): return lax.ppermute(x, axis, [(i, i ^ mask) for i in range(count)])  23.1 us
    ppermute x18, waiting for transfers between devices, swap(): return lax.ppermute(x, axis, [(i, i ^ mask) for i in range(count)])  16.3 us
    pallas_call x2, Pallas kernels, half(): kernel_call(functools.partial(grads_body, far), out_shape, [pltpu.VMEM(ac...  4.3 us
    pallas_call x1, Pallas kernels, local_split(): kernel_call(functools.partial(solve_body, -math.sqrt(params_all / total))...  4.3 us
  transfers between devices with their start and end apart: 18, of which 13 were waited for; matrix products, arithmetic and copies ran while one was open for 1% of the time, Pallas kernels for 4%

profile of v3, /device:TPU:0, one launch (start us, length us, event | category | flops | bytes accessed | tf_op | source)
XLA Modules:
  0.0 51.2 jit_solution(3418819093364334958)
XLA Ops:
  0.6 2.2 %shard_map.51 = (f32[312,128]{1,0:T(8,128)S(1)}, f32[312,128]{1,0:T(8,128)S(1)}, f32[312,128]{1,0:T(8,128)S(1)}, f32[312,128]{1,0:T(8,128)S(1)}) custom-call(bf16[16,2,64,256]{3,2,1,0:T(8,128)(2,1)} %acts_hbm.3, bf16[16,2,16,256]{3,2,1,0:T(8,128)(2,1)} %cots_hbm.3), custom_call_target="tpu_custom_call" | custom-call | tf_op jit(solution)/shard_map/pallas_call | solution.py:324
  2.8 4.1 %collective-permute-start = (f16[312,128]{1,0:T(8,128)(2,1)S(1)}, f16[312,128]{1,0:T(8,128)(2,1)S(1)}, u32[]{:S(2)}, u32[]{:S(2)}) collective-permute-start(f16[312,128]{1,0:T(8,128)(2,1)S(1)} %convert_element_type.42), channel_id=1, source_target_pairs={{0,16},{4,20},{8,24},{12,28},{16,0},{20,4},{24,8},{28,12},{1,17},{... | collective-permute-start | bytes 239624 | tf_op jit(solution)/shard_map/ppermute | solution.py:38
  6.9 0.1 collective-permute-start.1
  7.0 3.1 %collective-permute-start.2 = (f16[312,128]{1,0:T(8,128)(2,1)S(1)}, f16[312,128]{1,0:T(8,128)(2,1)S(1)}, u32[]{:S(2)}, u32[]{:S(2)}) collective-permute-start(f16[312,128]{1,0:T(8,128)(2,1)S(1)} %convert_element_type.46), channel_id=1, source_target_pairs={{0,24},{4,28},{8,16},{12,20},{16,8},{20,12},{24,0},{28,4},{1,25},{... | collective-permute-start | bytes 239624 | tf_op jit(solution)/shard_map/ppermute | solution.py:38
  10.2 0.6 %collective-permute-start.3 = (f16[312,128]{1,0:T(8,128)(2,1)S(1)}, f16[312,128]{1,0:T(8,128)(2,1)S(1)}, u32[]{:S(2)}, u32[]{:S(2)}) collective-permute-start(f16[312,128]{1,0:T(8,128)(2,1)S(1)} %convert_element_type.48), channel_id=1, source_target_pairs={{0,28},{4,24},{8,20},{12,16},{16,12},{20,8},{24,4},{28,0},{1,29},{... | collective-permute-start | bytes 239624 | tf_op jit(solution)/shard_map/ppermute | solution.py:38
  10.9 2.1 %shard_map.50 = (f32[18,16,128]{2,1,0:T(8,128)S(1)}, f32[312,128]{1,0:T(8,128)S(1)}, f32[312,128]{1,0:T(8,128)S(1)}, f32[312,128]{1,0:T(8,128)S(1)}) custom-call(bf16[16,2,64,256]{3,2,1,0:T(8,128)(2,1)} %acts_hbm.3, bf16[16,2,16,256]{3,2,1,0:T(8,128)(2,1)} %cots_hbm.3), custom_call_target="tpu_custom_call" | custom-call | tf_op jit(solution)/shard_map/pallas_call | solution.py:324
  13.0 0.1 collective-permute-start.4
  13.1 0.0 copy-start
  13.1 0.6 %copy-done = f32[16]{0:T(128)S(1)} copy-done((f32[16]{0:T(128)S(1)}, f32[16]{0:T(128)}, u32[]{:S(2)}) %copy-start) | copy-done | bytes 88
  13.8 0.1 tile.10
  13.9 0.0 collective-permute-done
  13.9 2.5 %collective-permute-start.5 = (f16[312,128]{1,0:T(8,128)(2,1)S(1)}, f16[312,128]{1,0:T(8,128)(2,1)S(1)}, u32[]{:S(2)}, u32[]{:S(2)}) collective-permute-start(f16[312,128]{1,0:T(8,128)(2,1)S(1)} %convert_element_type.52), channel_id=1, source_target_pairs={{0,12},{4,8},{8,4},{12,0},{16,28},{20,24},{24,20},{28,16},{1,13},{... | collective-permute-start | bytes 239624 | tf_op jit(solution)/shard_map/ppermute | solution.py:38
  16.4 1.5 %collective-permute-done.1 = f16[312,128]{1,0:T(8,128)(2,1)S(1)} collective-permute-done((f16[312,128]{1,0:T(8,128)(2,1)S(1)}, f16[312,128]{1,0:T(8,128)(2,1)S(1)}, u32[]{:S(2)}, u32[]{:S(2)}) %collective-permute-start.1) | collective-permute-done | bytes 79904 | tf_op jit(solution)/shard_map/ppermute | solution.py:38
  17.9 0.1 collective-permute-start.6
  18.0 0.1 broadcast_select_fusion.2.energies_ref
  18.1 0.0 collective-permute-done.2
  18.1 0.0 collective-permute-done.3
  18.1 1.5 %collective-permute-done.4 = f16[312,128]{1,0:T(8,128)(2,1)S(1)} collective-permute-done((f16[312,128]{1,0:T(8,128)(2,1)S(1)}, f16[312,128]{1,0:T(8,128)(2,1)S(1)}, u32[]{:S(2)}, u32[]{:S(2)}) %collective-permute-start.4) | collective-permute-done | bytes 79904 | tf_op jit(solution)/shard_map/ppermute | solution.py:38
  19.7 1.6 %collective-permute-done.5 = f16[312,128]{1,0:T(8,128)(2,1)S(1)} collective-permute-done((f16[312,128]{1,0:T(8,128)(2,1)S(1)}, f16[312,128]{1,0:T(8,128)(2,1)S(1)}, u32[]{:S(2)}, u32[]{:S(2)}) %collective-permute-start.5) | collective-permute-done | bytes 79904 | tf_op jit(solution)/shard_map/ppermute | solution.py:38
  21.3 0.0 collective-permute-done.6
  21.3 0.7 %shard_map.52 = (bf16[18,128,128]{2,1,0:T(8,128)(2,1)S(1)}, f32[72,128]{1,0:T(8,128)S(1)}) custom-call(f32[8,128]{1,0:T(8,128)S(1)} %broadcast_select_fusion.2.energies_ref, f32[18,16,128]{2,1,0:T(8,128)S(1)} %get-tuple-element.14.own_ref, f32[312,128]{1,0:T(8,128)S(1)} %convert_element_type.43.refs_0_, f32[312,128]{1,0:T(8,128)S(1)} %convert_element_type.45.refs_1_, ...), custom_call_target="tpu_custom_call" | custom-call | tf_op jit(solution)/shard_map/pallas_call | solution.py:347
  22.0 0.2 collective-permute-start.7
  22.1 1.1 %collective-permute-done.7 = f32[72,128]{1,0:T(8,128)S(1)} collective-permute-done((f32[72,128]{1,0:T(8,128)S(1)}, f32[72,128]{1,0:T(8,128)S(1)}, u32[]{:S(2)}, u32[]{:S(2)}) %collective-permute-start.7) | collective-permute-done | bytes 36896 | tf_op jit(solution)/shard_map/ppermute | solution.py:38
  23.2 1.7 %collective-permute-start.10 = (f32[72,128]{1,0:T(8,128)S(1)}, f32[72,128]{1,0:T(8,128)S(1)}, u32[]{:S(2)}, u32[]{:S(2)}) collective-permute-start(f32[72,128]{1,0:T(8,128)S(1)} %add.17), channel_id=1, source_target_pairs={{0,1},{1,0},{2,3},{3,2},{4,5},{5,4},{6,7},{7,6},{8,9},{9,8},{10,11... | collective-permute-start | bytes 110600 | tf_op jit(solution)/shard_map/ppermute | solution.py:38
  24.9 1.5 %collective-permute-start.8 = (f32[72,128]{1,0:T(8,128)S(1)}, f32[72,128]{1,0:T(8,128)S(1)}, u32[]{:S(2)}, u32[]{:S(2)}) collective-permute-start(f32[72,128]{1,0:T(8,128)S(1)} %add.17), channel_id=1, source_target_pairs={{0,3},{1,2},{2,1},{3,0},{4,7},{5,6},{6,5},{7,4},{8,11},{9,10},{10,... | collective-permute-start | bytes 110600 | tf_op jit(solution)/shard_map/ppermute | solution.py:38
  26.4 0.3 collective-permute-start.9
  26.7 0.5 collective-permute-done.10
  27.2 2.6 %collective-permute-done.8 = f32[72,128]{1,0:T(8,128)S(1)} collective-permute-done((f32[72,128]{1,0:T(8,128)S(1)}, f32[72,128]{1,0:T(8,128)S(1)}, u32[]{:S(2)}, u32[]{:S(2)}) %collective-permute-start.8) | collective-permute-done | bytes 36896 | tf_op jit(solution)/shard_map/ppermute | solution.py:38
  29.8 0.6 %collective-permute-done.9 = f32[72,128]{1,0:T(8,128)S(1)} collective-permute-done((f32[72,128]{1,0:T(8,128)S(1)}, f32[72,128]{1,0:T(8,128)S(1)}, u32[]{:S(2)}, u32[]{:S(2)}) %collective-permute-start.9) | collective-permute-done | bytes 36896 | tf_op jit(solution)/shard_map/ppermute | solution.py:38
  30.4 3.4 %collective-permute-start.11 = (f32[72,128]{1,0:T(8,128)S(1)}, f32[72,128]{1,0:T(8,128)S(1)}, u32[]{:S(2)}, u32[]{:S(2)}) collective-permute-start(f32[72,128]{1,0:T(8,128)S(1)} %add_add_fusion.refs_0_), channel_id=1, source_target_pairs={{0,24},{4,28},{8,16},{12,20},{16,8},{20,12},{24,0},{28,4},{1,25},{... | collective-permute-start | bytes 110600 | tf_op jit(solution)/shard_map/ppermute | solution.py:38
  33.8 0.0 collective-permute-start.12
  33.8 1.1 %collective-permute-start.13 = (f32[72,128]{1,0:T(8,128)S(1)}, f32[72,128]{1,0:T(8,128)S(1)}, u32[]{:S(2)}, u32[]{:S(2)}) collective-permute-start(f32[72,128]{1,0:T(8,128)S(1)} %add_add_fusion.refs_0_), channel_id=1, source_target_pairs={{0,8},{4,12},{8,0},{12,4},{16,24},{20,28},{24,16},{28,20},{1,9},{5... | collective-permute-start | bytes 110600 | tf_op jit(solution)/shard_map/ppermute | solution.py:38
  34.9 1.5 %collective-permute-done.11.refs_1_ = f32[72,128]{1,0:T(8,128)S(1)} collective-permute-done((f32[72,128]{1,0:T(8,128)S(1)}, f32[72,128]{1,0:T(8,128)S(1)}, u32[]{:S(2)}, u32[]{:S(2)}) %collective-permute-start.11) | collective-permute-done | bytes 36896 | tf_op jit(solution)/shard_map/ppermute | solution.py:38
  36.3 2.3 %collective-permute-done.12.refs_2_ = f32[72,128]{1,0:T(8,128)S(1)} collective-permute-done((f32[72,128]{1,0:T(8,128)S(1)}, f32[72,128]{1,0:T(8,128)S(1)}, u32[]{:S(2)}, u32[]{:S(2)}) %collective-permute-start.12) | collective-permute-done | bytes 36896 | tf_op jit(solution)/shard_map/ppermute | solution.py:38
  38.6 0.0 collective-permute-done.13.refs_3_
  38.6 4.3 %shard_map.53 = (f32[2,1152]{1,0:T(2,128)S(1)}, f32[1,16]{1,0:T(1,128)}) custom-call(bf16[18,128,128]{2,1,0:T(8,128)(2,1)S(1)} %get-tuple-element.22.centered_ref, f32[72,128]{1,0:T(8,128)S(1)} %add_add_fusion.refs_0_, f32[72,128]{1,0:T(8,128)S(1)} %collective-permute-done.11.refs_1_, f32[72,128]{1,0:T(8,128)S(1)} %collective-permute-done.12.refs_2_, ...), custom_call_target="tpu_custom_call" | custom-call | tf_op jit(solution)/shard_map/pallas_call | solution.py:355
  42.9 0.0 collective-permute-start.14
  42.9 1.2 %collective-permute-done.14 = f32[2,1152]{1,0:T(2,128)S(1)} collective-permute-done((f32[2,1152]{1,0:T(2,128)S(1)}, f32[2,1152]{1,0:T(2,128)S(1)}, u32[]{:S(2)}, u32[]{:S(2)}) %collective-permute-start.14) | collective-permute-done | bytes 9248 | tf_op jit(solution)/shard_map/ppermute | solution.py:38
  44.1 1.5 %collective-permute-start.15 = (f32[4,1152]{1,0:T(4,128)S(1)}, f32[4,1152]{1,0:T(4,128)S(1)}, u32[]{:S(2)}, u32[]{:S(2)}) collective-permute-start(f32[4,1152]{1,0:T(4,128)S(1)} %pad_maximum_fusion.1), channel_id=1, source_target_pairs={{0,24},{4,28},{8,16},{12,20},{16,8},{20,12},{24,0},{28,4},{1,25},{... | collective-permute-start | bytes 55304 | tf_op jit(solution)/shard_map/ppermute | solution.py:38
  45.7 0.6 %collective-permute-start.16 = (f32[4,1152]{1,0:T(4,128)S(1)}, f32[4,1152]{1,0:T(4,128)S(1)}, u32[]{:S(2)}, u32[]{:S(2)}) collective-permute-start(f32[4,1152]{1,0:T(4,128)S(1)} %pad_maximum_fusion.1), channel_id=1, source_target_pairs={{0,16},{4,20},{8,24},{12,28},{16,0},{20,4},{24,8},{28,12},{1,17},{... | collective-permute-start | bytes 55304 | tf_op jit(solution)/shard_map/ppermute | solution.py:38
  46.3 2.3 %collective-permute-start.17 = (f32[4,1152]{1,0:T(4,128)S(1)}, f32[4,1152]{1,0:T(4,128)S(1)}, u32[]{:S(2)}, u32[]{:S(2)}) collective-permute-start(f32[4,1152]{1,0:T(4,128)S(1)} %pad_maximum_fusion.1), channel_id=1, source_target_pairs={{0,8},{4,12},{8,0},{12,4},{16,24},{20,28},{24,16},{28,20},{1,9},{5... | collective-permute-start | bytes 55304 | tf_op jit(solution)/shard_map/ppermute | solution.py:38
  48.6 1.3 %collective-permute-done.15 = f32[4,1152]{1,0:T(4,128)S(1)} collective-permute-done((f32[4,1152]{1,0:T(4,128)S(1)}, f32[4,1152]{1,0:T(4,128)S(1)}, u32[]{:S(2)}, u32[]{:S(2)}) %collective-permute-start.15) | collective-permute-done | bytes 18464 | tf_op jit(solution)/shard_map/ppermute | solution.py:38
  49.9 0.4 collective-permute-done.16
  50.3 0.2 collective-permute-done.17
  50.6 0.7 %pad_maximum_fusion = f32[16,1152]{1,0:T(8,128)} fusion(f32[4,1152]{1,0:T(4,128)S(1)} %get-tuple-element.27, f32[4,1152]{1,0:T(4,128)S(1)} %get-tuple-element.28, f32[4,1152]{1,0:T(4,128)S(1)} %get-tuple-element.29, f32[4,1152]{1,0:T(4,128)S(1)} %get-tuple-element.26), kind=kLoop, calls=%fused_computation | loop fusion | flops 55296 | bytes 147456 | tf_op jit(solution)/shard_map/concatenate | solution.py:298
  (22 shorter events, 0.3 us)
Async XLA Ops:
  2.8 11.1 %collective-permute-start = (f16[312,128]{1,0:T(8,128)(2,1)S(1)}, f16[312,128]{1,0:T(8,128)(2,1)S(1)}, u32[]{:S(2)}, u32[]{:S(2)}) collective-permute-start(f16[312,128]{1,0:T(8,128)(2,1)S(1)} %convert_element_type.42), channel_id=1, source_target_pairs={{0,16},{4,20},{8,24},{12,28},{16,0},{20,4},{24,8},{28,12},{1,17},{... | collective-permute-start | bytes 239624 | tf_op jit(solution)/shard_map/ppermute | solution.py:38
  6.9 11.0 %collective-permute-start.1 = (f16[312,128]{1,0:T(8,128)(2,1)S(1)}, f16[312,128]{1,0:T(8,128)(2,1)S(1)}, u32[]{:S(2)}, u32[]{:S(2)}) collective-permute-start(f16[312,128]{1,0:T(8,128)(2,1)S(1)} %convert_element_type.44), channel_id=1, source_target_pairs={{0,20},{4,16},{8,28},{12,24},{16,4},{20,0},{24,12},{28,8},{1,21},{... | collective-permute-start | bytes 239624 | tf_op jit(solution)/shard_map/ppermute | solution.py:38
  7.0 11.0 %collective-permute-start.2 = (f16[312,128]{1,0:T(8,128)(2,1)S(1)}, f16[312,128]{1,0:T(8,128)(2,1)S(1)}, u32[]{:S(2)}, u32[]{:S(2)}) collective-permute-start(f16[312,128]{1,0:T(8,128)(2,1)S(1)} %convert_element_type.46), channel_id=1, source_target_pairs={{0,24},{4,28},{8,16},{12,20},{16,8},{20,12},{24,0},{28,4},{1,25},{... | collective-permute-start | bytes 239624 | tf_op jit(solution)/shard_map/ppermute | solution.py:38
  10.2 7.9 %collective-permute-start.3 = (f16[312,128]{1,0:T(8,128)(2,1)S(1)}, f16[312,128]{1,0:T(8,128)(2,1)S(1)}, u32[]{:S(2)}, u32[]{:S(2)}) collective-permute-start(f16[312,128]{1,0:T(8,128)(2,1)S(1)} %convert_element_type.48), channel_id=1, source_target_pairs={{0,28},{4,24},{8,20},{12,16},{16,12},{20,8},{24,4},{28,0},{1,29},{... | collective-permute-start | bytes 239624 | tf_op jit(solution)/shard_map/ppermute | solution.py:38
  13.0 6.6 %collective-permute-start.4 = (f16[312,128]{1,0:T(8,128)(2,1)S(1)}, f16[312,128]{1,0:T(8,128)(2,1)S(1)}, u32[]{:S(2)}, u32[]{:S(2)}) collective-permute-start(f16[312,128]{1,0:T(8,128)(2,1)S(1)} %convert_element_type.50), channel_id=1, source_target_pairs={{0,8},{4,12},{8,0},{12,4},{16,24},{20,28},{24,16},{28,20},{1,9},{5... | collective-permute-start | bytes 239624 | tf_op jit(solution)/shard_map/ppermute | solution.py:38
  13.1 0.7 %copy-start = (f32[16]{0:T(128)S(1)}, f32[16]{0:T(128)}, u32[]{:S(2)}) copy-start(f32[16]{0:T(128)} %param.5) | copy-start | bytes 196
  13.9 7.3 %collective-permute-start.5 = (f16[312,128]{1,0:T(8,128)(2,1)S(1)}, f16[312,128]{1,0:T(8,128)(2,1)S(1)}, u32[]{:S(2)}, u32[]{:S(2)}) collective-permute-start(f16[312,128]{1,0:T(8,128)(2,1)S(1)} %convert_element_type.52), channel_id=1, source_target_pairs={{0,12},{4,8},{8,4},{12,0},{16,28},{20,24},{24,20},{28,16},{1,13},{... | collective-permute-start | bytes 239624 | tf_op jit(solution)/shard_map/ppermute | solution.py:38
  17.9 3.4 %collective-permute-start.6 = (f16[312,128]{1,0:T(8,128)(2,1)S(1)}, f16[312,128]{1,0:T(8,128)(2,1)S(1)}, u32[]{:S(2)}, u32[]{:S(2)}) collective-permute-start(f16[312,128]{1,0:T(8,128)(2,1)S(1)} %convert_element_type.54), channel_id=1, source_target_pairs={{0,4},{4,0},{8,12},{12,8},{16,20},{20,16},{24,28},{28,24},{1,5},{5... | collective-permute-start | bytes 239624 | tf_op jit(solution)/shard_map/ppermute | solution.py:38
  22.0 1.3 %collective-permute-start.7 = (f32[72,128]{1,0:T(8,128)S(1)}, f32[72,128]{1,0:T(8,128)S(1)}, u32[]{:S(2)}, u32[]{:S(2)}) collective-permute-start(f32[72,128]{1,0:T(8,128)S(1)} %get-tuple-element.23), channel_id=1, source_target_pairs={{0,4},{4,0},{8,12},{12,8},{16,20},{20,16},{24,28},{28,24},{1,5},{5... | collective-permute-start | bytes 110600 | tf_op jit(solution)/shard_map/ppermute | solution.py:38
  23.2 4.0 %collective-permute-start.10 = (f32[72,128]{1,0:T(8,128)S(1)}, f32[72,128]{1,0:T(8,128)S(1)}, u32[]{:S(2)}, u32[]{:S(2)}) collective-permute-start(f32[72,128]{1,0:T(8,128)S(1)} %add.17), channel_id=1, source_target_pairs={{0,1},{1,0},{2,3},{3,2},{4,5},{5,4},{6,7},{7,6},{8,9},{9,8},{10,11... | collective-permute-start | bytes 110600 | tf_op jit(solution)/shard_map/ppermute | solution.py:38
  24.9 4.9 %collective-permute-start.8 = (f32[72,128]{1,0:T(8,128)S(1)}, f32[72,128]{1,0:T(8,128)S(1)}, u32[]{:S(2)}, u32[]{:S(2)}) collective-permute-start(f32[72,128]{1,0:T(8,128)S(1)} %add.17), channel_id=1, source_target_pairs={{0,3},{1,2},{2,1},{3,0},{4,7},{5,6},{6,5},{7,4},{8,11},{9,10},{10,... | collective-permute-start | bytes 110600 | tf_op jit(solution)/shard_map/ppermute | solution.py:38
  26.4 4.0 %collective-permute-start.9 = (f32[72,128]{1,0:T(8,128)S(1)}, f32[72,128]{1,0:T(8,128)S(1)}, u32[]{:S(2)}, u32[]{:S(2)}) collective-permute-start(f32[72,128]{1,0:T(8,128)S(1)} %add.17), channel_id=1, source_target_pairs={{0,2},{1,3},{2,0},{3,1},{4,6},{5,7},{6,4},{7,5},{8,10},{9,11},{10,... | collective-permute-start | bytes 110600 | tf_op jit(solution)/shard_map/ppermute | solution.py:38
  30.4 5.9 %collective-permute-start.11 = (f32[72,128]{1,0:T(8,128)S(1)}, f32[72,128]{1,0:T(8,128)S(1)}, u32[]{:S(2)}, u32[]{:S(2)}) collective-permute-start(f32[72,128]{1,0:T(8,128)S(1)} %add_add_fusion.refs_0_), channel_id=1, source_target_pairs={{0,24},{4,28},{8,16},{12,20},{16,8},{20,12},{24,0},{28,4},{1,25},{... | collective-permute-start | bytes 110600 | tf_op jit(solution)/shard_map/ppermute | solution.py:38
  33.8 4.9 %collective-permute-start.12 = (f32[72,128]{1,0:T(8,128)S(1)}, f32[72,128]{1,0:T(8,128)S(1)}, u32[]{:S(2)}, u32[]{:S(2)}) collective-permute-start(f32[72,128]{1,0:T(8,128)S(1)} %add_add_fusion.refs_0_), channel_id=1, source_target_pairs={{0,16},{4,20},{8,24},{12,28},{16,0},{20,4},{24,8},{28,12},{1,17},{... | collective-permute-start | bytes 110600 | tf_op jit(solution)/shard_map/ppermute | solution.py:38
  33.8 4.9 %collective-permute-start.13 = (f32[72,128]{1,0:T(8,128)S(1)}, f32[72,128]{1,0:T(8,128)S(1)}, u32[]{:S(2)}, u32[]{:S(2)}) collective-permute-start(f32[72,128]{1,0:T(8,128)S(1)} %add_add_fusion.refs_0_), channel_id=1, source_target_pairs={{0,8},{4,12},{8,0},{12,4},{16,24},{20,28},{24,16},{28,20},{1,9},{5... | collective-permute-start | bytes 110600 | tf_op jit(solution)/shard_map/ppermute | solution.py:38
  42.9 1.2 %collective-permute-start.14 = (f32[2,1152]{1,0:T(2,128)S(1)}, f32[2,1152]{1,0:T(2,128)S(1)}, u32[]{:S(2)}, u32[]{:S(2)}) collective-permute-start(f32[2,1152]{1,0:T(2,128)S(1)} %get-tuple-element.24), channel_id=1, source_target_pairs={{0,4},{4,0},{8,12},{12,8},{16,20},{20,16},{24,28},{28,24},{1,5},{5... | collective-permute-start | bytes 27656 | tf_op jit(solution)/shard_map/ppermute | solution.py:38
  44.1 5.8 %collective-permute-start.15 = (f32[4,1152]{1,0:T(4,128)S(1)}, f32[4,1152]{1,0:T(4,128)S(1)}, u32[]{:S(2)}, u32[]{:S(2)}) collective-permute-start(f32[4,1152]{1,0:T(4,128)S(1)} %pad_maximum_fusion.1), channel_id=1, source_target_pairs={{0,24},{4,28},{8,16},{12,20},{16,8},{20,12},{24,0},{28,4},{1,25},{... | collective-permute-start | bytes 55304 | tf_op jit(solution)/shard_map/ppermute | solution.py:38
  45.7 4.7 %collective-permute-start.16 = (f32[4,1152]{1,0:T(4,128)S(1)}, f32[4,1152]{1,0:T(4,128)S(1)}, u32[]{:S(2)}, u32[]{:S(2)}) collective-permute-start(f32[4,1152]{1,0:T(4,128)S(1)} %pad_maximum_fusion.1), channel_id=1, source_target_pairs={{0,16},{4,20},{8,24},{12,28},{16,0},{20,4},{24,8},{28,12},{1,17},{... | collective-permute-start | bytes 55304 | tf_op jit(solution)/shard_map/ppermute | solution.py:38
  46.3 4.2 %collective-permute-start.17 = (f32[4,1152]{1,0:T(4,128)S(1)}, f32[4,1152]{1,0:T(4,128)S(1)}, u32[]{:S(2)}, u32[]{:S(2)}) collective-permute-start(f32[4,1152]{1,0:T(4,128)S(1)} %pad_maximum_fusion.1), channel_id=1, source_target_pairs={{0,8},{4,12},{8,0},{12,4},{16,24},{20,28},{24,16},{28,20},{1,9},{5... | collective-permute-start | bytes 55304 | tf_op jit(solution)/shard_map/ppermute | solution.py:38

commit v4 on v3

--- a/solution.py
+++ b/solution.py
@@ -238,7 +238,25 @@
     return matrix
 
 
-def solve_body(scale, centered_ref, *refs):
+def arrange(terms):
+    rows, lanes = len(terms), terms[0].shape[1]
+    owned = rows // OFFSETS
+    padded = -(-rows // 8) * 8
+    table = jnp.concatenate(terms + [jnp.zeros((padded - rows, lanes), F32)], axis=0)
+    row_index = lax.broadcasted_iota(jnp.int32, (padded, lanes), 0)
+    tiles = []
+    for tile in range(OFFSETS):
+        place = lax.broadcasted_iota(jnp.int32, (padded, lanes), 1) + tile * lanes
+        picked = jnp.take_along_axis(table, place // OFFSETS, axis=1)
+        sums = []
+        for channel in range(owned):
+            mask = row_index == (place % OFFSETS) * owned + channel
+            sums.append(jnp.sum(jnp.where(mask, picked, 0.0), axis=0, keepdims=True))
+        tiles.append(jnp.concatenate(sums, axis=0))
+    return jnp.concatenate(tiles, axis=1)
+
+
+def solve_body(scale, centered_ref, across_ref, *refs):
     *part_refs, update_ref, coeffs_ref = refs
     rows, total, lanes = centered_ref.shape
     samples = coeffs_ref.shape[1]
@@ -263,19 +281,14 @@
     coeffs_ref[...] = own[:, :samples]
 
     spread = spread * scale
-    terms = [jnp.sum(centered_ref[row].astype(F32) * spread, axis=0, keepdims=True) for row in range(rows)]
-    owned = rows // OFFSETS
-    padded = -(-rows // 8) * 8
-    table = jnp.concatenate(terms + [jnp.zeros((padded - rows, lanes), F32)], axis=0)
-    row_index = lax.broadcasted_iota(jnp.int32, (padded, lanes), 0)
-    for tile in range(OFFSETS):
-        place = lax.broadcasted_iota(jnp.int32, (padded, lanes), 1) + tile * lanes
-        picked = jnp.take_along_axis(table, place // OFFSETS, axis=1)
-        for channel in range(owned):
-            mask = row_index == (place % OFFSETS) * owned + channel
-            update_ref[channel : channel + 1, tile * lanes : (tile + 1) * lanes] = jnp.sum(
-                jnp.where(mask, picked, 0.0), axis=0, keepdims=True
-            )
+    own, across = (
+        arrange([jnp.sum(ref[row].astype(F32) * spread, axis=0, keepdims=True) for row in range(rows)])
+        for ref in (centered_ref, across_ref)
+    )
+    even = position % CORES == 0
+    owned = own.shape[0]
+    update_ref[0:owned, :] = jnp.where(even, own, across)
+    update_ref[owned : 2 * owned, :] = jnp.where(even, across, own)
 
 
 def far_first(members):
@@ -350,13 +363,15 @@
     )(spread, own, *arrived)
 
     summed = partial_gram + swap(partial_gram, "samp", 1)
-    summed = summed + sum(swaps(summed, "par", range(1, lax.axis_size("par"))).values())
+    ready, summed = lax.optimization_barrier((centered, summed))
+    across = swap(ready, "samp", 1)
+    masks = [*range(2, lax.axis_size("par")), 1]
+    summed = sum((swap(summed, "par", mask) for mask in masks), start=summed)
     parts = [summed, *swaps(summed, "samp", range(CORES, members, CORES)).values()]
     update, local_coeffs = kernel_call(
         functools.partial(solve_body, -math.sqrt(params_all / total)),
-        (jax.ShapeDtypeStruct((mine, OFFSETS * LANES), F32), jax.ShapeDtypeStruct((1, samples), F32)),
-    )(centered, *parts)
-    update = in_order(update, "samp", range(1, CORES))
+        (jax.ShapeDtypeStruct((CORES * mine, OFFSETS * LANES), F32), jax.ShapeDtypeStruct((1, samples), F32)),
+    )(centered, across, *parts)
     update = in_order(update, "samp", range(CORES, members, CORES))
     return update, local_coeffs[0]
 

time: 51.4 us -> 50.5 us (0.982)
  waiting for transfers between devices: 16.3 us -> 15.1 us
    ppermute x18, waiting for transfers between devices: 16.3 us -> 15.1 us  [swap(): return lax.ppermute(x, axis, [(i, i ^ mask) for i in range(count)])]
  transfers between devices with their start and end apart: 18 -> 18, of which waited for: 13 -> 12; matrix products, arithmetic and copies ran while one was open for 1% -> 1% of each run, Pallas kernels for 4% -> 4%
where the time goes in v4:
time: 50.5 us; the launch traced here: 50.3 us
  starting transfers between devices  23.2 us (46%)
  waiting for transfers between devices  15.1 us (30%)
  Pallas kernels  9.48 us (19%)
  other arithmetic  0.98 us (2%)
  between operations  0.83 us (2%)
  local copies, waits for them, and re-layouts  0.73 us (1%)
    ppermute x18, starting transfers between devices, swap(): return lax.ppermute(x, axis, [(i, i ^ mask) for i in range(count)])  23.2 us
    ppermute x18, waiting for transfers between devices, swap(): return lax.ppermute(x, axis, [(i, i ^ mask) for i in range(count)])  15.1 us
    pallas_call x1, Pallas kernels, local_split(): kernel_call(functools.partial(solve_body, -math.sqrt(params_all / total))...  4.52 us
    pallas_call x2, Pallas kernels, half(): kernel_call(functools.partial(grads_body, far), out_shape, [pltpu.VMEM(ac...  4.3 us
  transfers between devices with their start and end apart: 18, of which 12 were waited for; matrix products, arithmetic and copies ran while one was open for 1% of the time, Pallas kernels for 4%

profile of v4, /device:TPU:0, one launch (start us, length us, event | category | flops | bytes accessed | tf_op | source)
XLA Modules:
  0.0 50.3 jit_solution(3642485034294649697)
XLA Ops:
  0.6 2.2 %shard_map.51 = (f32[312,128]{1,0:T(8,128)S(1)}, f32[312,128]{1,0:T(8,128)S(1)}, f32[312,128]{1,0:T(8,128)S(1)}, f32[312,128]{1,0:T(8,128)S(1)}) custom-call(bf16[16,2,64,256]{3,2,1,0:T(8,128)(2,1)} %acts_hbm.3, bf16[16,2,16,256]{3,2,1,0:T(8,128)(2,1)} %cots_hbm.3), custom_call_target="tpu_custom_call" | custom-call | tf_op jit(solution)/shard_map/pallas_call | solution.py:337
  2.8 4.1 %collective-permute-start = (f16[312,128]{1,0:T(8,128)(2,1)S(1)}, f16[312,128]{1,0:T(8,128)(2,1)S(1)}, u32[]{:S(2)}, u32[]{:S(2)}) collective-permute-start(f16[312,128]{1,0:T(8,128)(2,1)S(1)} %convert_element_type.42), channel_id=1, source_target_pairs={{0,16},{4,20},{8,24},{12,28},{16,0},{20,4},{24,8},{28,12},{1,17},{... | collective-permute-start | bytes 239624 | tf_op jit(solution)/shard_map/ppermute | solution.py:38
  6.9 0.1 collective-permute-start.1
  7.0 3.1 %collective-permute-start.2 = (f16[312,128]{1,0:T(8,128)(2,1)S(1)}, f16[312,128]{1,0:T(8,128)(2,1)S(1)}, u32[]{:S(2)}, u32[]{:S(2)}) collective-permute-start(f16[312,128]{1,0:T(8,128)(2,1)S(1)} %convert_element_type.46), channel_id=1, source_target_pairs={{0,24},{4,28},{8,16},{12,20},{16,8},{20,12},{24,0},{28,4},{1,25},{... | collective-permute-start | bytes 239624 | tf_op jit(solution)/shard_map/ppermute | solution.py:38
  10.2 0.6 %collective-permute-start.3 = (f16[312,128]{1,0:T(8,128)(2,1)S(1)}, f16[312,128]{1,0:T(8,128)(2,1)S(1)}, u32[]{:S(2)}, u32[]{:S(2)}) collective-permute-start(f16[312,128]{1,0:T(8,128)(2,1)S(1)} %convert_element_type.48), channel_id=1, source_target_pairs={{0,28},{4,24},{8,20},{12,16},{16,12},{20,8},{24,4},{28,0},{1,29},{... | collective-permute-start | bytes 239624 | tf_op jit(solution)/shard_map/ppermute | solution.py:38
  10.9 2.1 %shard_map.50 = (f32[18,16,128]{2,1,0:T(8,128)S(1)}, f32[312,128]{1,0:T(8,128)S(1)}, f32[312,128]{1,0:T(8,128)S(1)}, f32[312,128]{1,0:T(8,128)S(1)}) custom-call(bf16[16,2,64,256]{3,2,1,0:T(8,128)(2,1)} %acts_hbm.3, bf16[16,2,16,256]{3,2,1,0:T(8,128)(2,1)} %cots_hbm.3), custom_call_target="tpu_custom_call" | custom-call | tf_op jit(solution)/shard_map/pallas_call | solution.py:337
  13.0 0.1 collective-permute-start.4
  13.1 0.0 copy-start
  13.2 0.6 %copy-done = f32[16]{0:T(128)S(1)} copy-done((f32[16]{0:T(128)S(1)}, f32[16]{0:T(128)}, u32[]{:S(2)}) %copy-start) | copy-done | bytes 88
  13.8 0.1 tile.10
  13.9 0.0 collective-permute-done
  13.9 2.5 %collective-permute-start.5 = (f16[312,128]{1,0:T(8,128)(2,1)S(1)}, f16[312,128]{1,0:T(8,128)(2,1)S(1)}, u32[]{:S(2)}, u32[]{:S(2)}) collective-permute-start(f16[312,128]{1,0:T(8,128)(2,1)S(1)} %convert_element_type.52), channel_id=1, source_target_pairs={{0,12},{4,8},{8,4},{12,0},{16,28},{20,24},{24,20},{28,16},{1,13},{... | collective-permute-start | bytes 239624 | tf_op jit(solution)/shard_map/ppermute | solution.py:38
  16.4 1.5 %collective-permute-done.1 = f16[312,128]{1,0:T(8,128)(2,1)S(1)} collective-permute-done((f16[312,128]{1,0:T(8,128)(2,1)S(1)}, f16[312,128]{1,0:T(8,128)(2,1)S(1)}, u32[]{:S(2)}, u32[]{:S(2)}) %collective-permute-start.1) | collective-permute-done | bytes 79904 | tf_op jit(solution)/shard_map/ppermute | solution.py:38
  17.9 0.1 collective-permute-start.6
  18.0 0.1 broadcast_select_fusion.energies_ref
  18.1 0.0 collective-permute-done.2
  18.1 0.0 collective-permute-done.3
  18.1 1.5 %collective-permute-done.4 = f16[312,128]{1,0:T(8,128)(2,1)S(1)} collective-permute-done((f16[312,128]{1,0:T(8,128)(2,1)S(1)}, f16[312,128]{1,0:T(8,128)(2,1)S(1)}, u32[]{:S(2)}, u32[]{:S(2)}) %collective-permute-start.4) | collective-permute-done | bytes 79904 | tf_op jit(solution)/shard_map/ppermute | solution.py:38
  19.7 1.6 %collective-permute-done.5 = f16[312,128]{1,0:T(8,128)(2,1)S(1)} collective-permute-done((f16[312,128]{1,0:T(8,128)(2,1)S(1)}, f16[312,128]{1,0:T(8,128)(2,1)S(1)}, u32[]{:S(2)}, u32[]{:S(2)}) %collective-permute-start.5) | collective-permute-done | bytes 79904 | tf_op jit(solution)/shard_map/ppermute | solution.py:38
  21.3 0.0 collective-permute-done.6
  21.3 0.7 %shard_map.52 = (bf16[18,128,128]{2,1,0:T(8,128)(2,1)S(1)}, f32[72,128]{1,0:T(8,128)S(1)}) custom-call(f32[8,128]{1,0:T(8,128)S(1)} %broadcast_select_fusion.energies_ref, f32[18,16,128]{2,1,0:T(8,128)S(1)} %get-tuple-element.16.own_ref, f32[312,128]{1,0:T(8,128)S(1)} %convert_element_type.43.refs_0_, f32[312,128]{1,0:T(8,128)S(1)} %convert_element_type.45.refs_1_, ...), custom_call_target="tpu_custom_call" | custom-call | tf_op jit(solution)/shard_map/pallas_call | solution.py:360
  22.0 0.2 collective-permute-start.7
  22.1 1.1 %collective-permute-done.7 = f32[72,128]{1,0:T(8,128)S(1)} collective-permute-done((f32[72,128]{1,0:T(8,128)S(1)}, f32[72,128]{1,0:T(8,128)S(1)}, u32[]{:S(2)}, u32[]{:S(2)}) %collective-permute-start.7) | collective-permute-done | bytes 36896 | tf_op jit(solution)/shard_map/ppermute | solution.py:38
  23.2 0.2 collective-permute-start.8
  23.4 2.7 %collective-permute-start.10 = (f32[72,128]{1,0:T(8,128)S(1)}, f32[72,128]{1,0:T(8,128)S(1)}, u32[]{:S(2)}, u32[]{:S(2)}) collective-permute-start(f32[72,128]{1,0:T(8,128)S(1)} %add.17), channel_id=1, source_target_pairs={{0,3},{1,2},{2,1},{3,0},{4,7},{5,6},{6,5},{7,4},{8,11},{9,10},{10,... | collective-permute-start | bytes 110600 | tf_op jit(solution)/shard_map/ppermute | solution.py:38
  26.1 0.5 %collective-permute-start.11 = (f32[72,128]{1,0:T(8,128)S(1)}, f32[72,128]{1,0:T(8,128)S(1)}, u32[]{:S(2)}, u32[]{:S(2)}) collective-permute-start(f32[72,128]{1,0:T(8,128)S(1)} %add.17), channel_id=1, source_target_pairs={{0,1},{1,0},{2,3},{3,2},{4,5},{5,4},{6,7},{7,6},{8,9},{9,8},{10,11... | collective-permute-start | bytes 110600 | tf_op jit(solution)/shard_map/ppermute | solution.py:38
  26.6 0.3 collective-permute-start.9
  26.9 1.4 %collective-permute-done.10 = f32[72,128]{1,0:T(8,128)S(1)} collective-permute-done((f32[72,128]{1,0:T(8,128)S(1)}, f32[72,128]{1,0:T(8,128)S(1)}, u32[]{:S(2)}, u32[]{:S(2)}) %collective-permute-start.10) | collective-permute-done | bytes 36896 | tf_op jit(solution)/shard_map/ppermute | solution.py:38
  28.3 1.8 %collective-permute-done.11 = f32[72,128]{1,0:T(8,128)S(1)} collective-permute-done((f32[72,128]{1,0:T(8,128)S(1)}, f32[72,128]{1,0:T(8,128)S(1)}, u32[]{:S(2)}, u32[]{:S(2)}) %collective-permute-start.11) | collective-permute-done | bytes 36896 | tf_op jit(solution)/shard_map/ppermute | solution.py:38
  30.0 0.5 %collective-permute-done.9 = f32[72,128]{1,0:T(8,128)S(1)} collective-permute-done((f32[72,128]{1,0:T(8,128)S(1)}, f32[72,128]{1,0:T(8,128)S(1)}, u32[]{:S(2)}, u32[]{:S(2)}) %collective-permute-start.9) | collective-permute-done | bytes 36896 | tf_op jit(solution)/shard_map/ppermute | solution.py:38
  30.6 3.4 %collective-permute-start.12 = (f32[72,128]{1,0:T(8,128)S(1)}, f32[72,128]{1,0:T(8,128)S(1)}, u32[]{:S(2)}, u32[]{:S(2)}) collective-permute-start(f32[72,128]{1,0:T(8,128)S(1)} %add_add_fusion.refs_0_), channel_id=1, source_target_pairs={{0,24},{4,28},{8,16},{12,20},{16,8},{20,12},{24,0},{28,4},{1,25},{... | collective-permute-start | bytes 110600 | tf_op jit(solution)/shard_map/ppermute | solution.py:38
  33.9 0.0 collective-permute-start.13
  33.9 1.1 %collective-permute-start.14 = (f32[72,128]{1,0:T(8,128)S(1)}, f32[72,128]{1,0:T(8,128)S(1)}, u32[]{:S(2)}, u32[]{:S(2)}) collective-permute-start(f32[72,128]{1,0:T(8,128)S(1)} %add_add_fusion.refs_0_), channel_id=1, source_target_pairs={{0,8},{4,12},{8,0},{12,4},{16,24},{20,28},{24,16},{28,20},{1,9},{5... | collective-permute-start | bytes 110600 | tf_op jit(solution)/shard_map/ppermute | solution.py:38
  35.0 1.5 %collective-permute-done.12.refs_1_ = f32[72,128]{1,0:T(8,128)S(1)} collective-permute-done((f32[72,128]{1,0:T(8,128)S(1)}, f32[72,128]{1,0:T(8,128)S(1)}, u32[]{:S(2)}, u32[]{:S(2)}) %collective-permute-start.12) | collective-permute-done | bytes 36896 | tf_op jit(solution)/shard_map/ppermute | solution.py:38
  36.5 2.3 %collective-permute-done.13.refs_2_ = f32[72,128]{1,0:T(8,128)S(1)} collective-permute-done((f32[72,128]{1,0:T(8,128)S(1)}, f32[72,128]{1,0:T(8,128)S(1)}, u32[]{:S(2)}, u32[]{:S(2)}) %collective-permute-start.13) | collective-permute-done | bytes 36896 | tf_op jit(solution)/shard_map/ppermute | solution.py:38
  38.8 0.0 collective-permute-done.14.refs_3_
  38.8 0.0 collective-permute-done.8.across_ref
  38.8 4.5 %shard_map.53 = (f32[4,1152]{1,0:T(4,128)S(1)}, f32[1,16]{1,0:T(1,128)}) custom-call(bf16[18,128,128]{2,1,0:T(8,128)(2,1)S(1)} %get-tuple-element.26.centered_ref, bf16[18,128,128]{2,1,0:T(8,128)(2,1)S(1)} %collective-permute-done.8.across_ref, f32[72,128]{1,0:T(8,128)S(1)} %add_add_fusion.refs_0_, f32[72,128]{1,0:T(8,128)S(1)} %collective-permute-done.12.refs_1_, ...), custom_call_target="tpu_custom_call" | custom-call | tf_op jit(solution)/shard_map/pallas_call | solution.py:371
  43.3 1.5 %collective-permute-start.15 = (f32[4,1152]{1,0:T(4,128)S(1)}, f32[4,1152]{1,0:T(4,128)S(1)}, u32[]{:S(2)}, u32[]{:S(2)}) collective-permute-start(f32[4,1152]{1,0:T(4,128)S(1)} %get-tuple-element.28), channel_id=1, source_target_pairs={{0,24},{4,28},{8,16},{12,20},{16,8},{20,12},{24,0},{28,4},{1,25},{... | collective-permute-start | bytes 55304 | tf_op jit(solution)/shard_map/ppermute | solution.py:38
  44.8 0.6 %collective-permute-start.16 = (f32[4,1152]{1,0:T(4,128)S(1)}, f32[4,1152]{1,0:T(4,128)S(1)}, u32[]{:S(2)}, u32[]{:S(2)}) collective-permute-start(f32[4,1152]{1,0:T(4,128)S(1)} %get-tuple-element.28), channel_id=1, source_target_pairs={{0,16},{4,20},{8,24},{12,28},{16,0},{20,4},{24,8},{28,12},{1,17},{... | collective-permute-start | bytes 55304 | tf_op jit(solution)/shard_map/ppermute | solution.py:38
  45.3 2.4 %collective-permute-start.17 = (f32[4,1152]{1,0:T(4,128)S(1)}, f32[4,1152]{1,0:T(4,128)S(1)}, u32[]{:S(2)}, u32[]{:S(2)}) collective-permute-start(f32[4,1152]{1,0:T(4,128)S(1)} %get-tuple-element.28), channel_id=1, source_target_pairs={{0,8},{4,12},{8,0},{12,4},{16,24},{20,28},{24,16},{28,20},{1,9},{5... | collective-permute-start | bytes 55304 | tf_op jit(solution)/shard_map/ppermute | solution.py:38
  47.7 1.2 %collective-permute-done.15 = f32[4,1152]{1,0:T(4,128)S(1)} collective-permute-done((f32[4,1152]{1,0:T(4,128)S(1)}, f32[4,1152]{1,0:T(4,128)S(1)}, u32[]{:S(2)}, u32[]{:S(2)}) %collective-permute-start.15) | collective-permute-done | bytes 18464 | tf_op jit(solution)/shard_map/ppermute | solution.py:38
  48.9 0.6 %collective-permute-done.16 = f32[4,1152]{1,0:T(4,128)S(1)} collective-permute-done((f32[4,1152]{1,0:T(4,128)S(1)}, f32[4,1152]{1,0:T(4,128)S(1)}, u32[]{:S(2)}, u32[]{:S(2)}) %collective-permute-start.16) | collective-permute-done | bytes 18464 | tf_op jit(solution)/shard_map/ppermute | solution.py:38
  49.5 0.2 collective-permute-done.17
  49.7 0.7 %pad_maximum_fusion = f32[16,1152]{1,0:T(8,128)} fusion(f32[4,1152]{1,0:T(4,128)S(1)} %get-tuple-element.31, f32[4,1152]{1,0:T(4,128)S(1)} %get-tuple-element.32, f32[4,1152]{1,0:T(4,128)S(1)} %get-tuple-element.33, f32[4,1152]{1,0:T(4,128)S(1)} %get-tuple-element.30), kind=kLoop, calls=%fused_computation | loop fusion | flops 55296 | bytes 147456 | tf_op jit(solution)/shard_map/concatenate | solution.py:311
  (20 shorter events, 0.3 us)
Async XLA Ops:
  2.8 11.1 %collective-permute-start = (f16[312,128]{1,0:T(8,128)(2,1)S(1)}, f16[312,128]{1,0:T(8,128)(2,1)S(1)}, u32[]{:S(2)}, u32[]{:S(2)}) collective-permute-start(f16[312,128]{1,0:T(8,128)(2,1)S(1)} %convert_element_type.42), channel_id=1, source_target_pairs={{0,16},{4,20},{8,24},{12,28},{16,0},{20,4},{24,8},{28,12},{1,17},{... | collective-permute-start | bytes 239624 | tf_op jit(solution)/shard_map/ppermute | solution.py:38
  6.9 11.0 %collective-permute-start.1 = (f16[312,128]{1,0:T(8,128)(2,1)S(1)}, f16[312,128]{1,0:T(8,128)(2,1)S(1)}, u32[]{:S(2)}, u32[]{:S(2)}) collective-permute-start(f16[312,128]{1,0:T(8,128)(2,1)S(1)} %convert_element_type.44), channel_id=1, source_target_pairs={{0,20},{4,16},{8,28},{12,24},{16,4},{20,0},{24,12},{28,8},{1,21},{... | collective-permute-start | bytes 239624 | tf_op jit(solution)/shard_map/ppermute | solution.py:38
  7.0 11.0 %collective-permute-start.2 = (f16[312,128]{1,0:T(8,128)(2,1)S(1)}, f16[312,128]{1,0:T(8,128)(2,1)S(1)}, u32[]{:S(2)}, u32[]{:S(2)}) collective-permute-start(f16[312,128]{1,0:T(8,128)(2,1)S(1)} %convert_element_type.46), channel_id=1, source_target_pairs={{0,24},{4,28},{8,16},{12,20},{16,8},{20,12},{24,0},{28,4},{1,25},{... | collective-permute-start | bytes 239624 | tf_op jit(solution)/shard_map/ppermute | solution.py:38
  10.2 7.9 %collective-permute-start.3 = (f16[312,128]{1,0:T(8,128)(2,1)S(1)}, f16[312,128]{1,0:T(8,128)(2,1)S(1)}, u32[]{:S(2)}, u32[]{:S(2)}) collective-permute-start(f16[312,128]{1,0:T(8,128)(2,1)S(1)} %convert_element_type.48), channel_id=1, source_target_pairs={{0,28},{4,24},{8,20},{12,16},{16,12},{20,8},{24,4},{28,0},{1,29},{... | collective-permute-start | bytes 239624 | tf_op jit(solution)/shard_map/ppermute | solution.py:38
  13.0 6.6 %collective-permute-start.4 = (f16[312,128]{1,0:T(8,128)(2,1)S(1)}, f16[312,128]{1,0:T(8,128)(2,1)S(1)}, u32[]{:S(2)}, u32[]{:S(2)}) collective-permute-start(f16[312,128]{1,0:T(8,128)(2,1)S(1)} %convert_element_type.50), channel_id=1, source_target_pairs={{0,8},{4,12},{8,0},{12,4},{16,24},{20,28},{24,16},{28,20},{1,9},{5... | collective-permute-start | bytes 239624 | tf_op jit(solution)/shard_map/ppermute | solution.py:38
  13.1 0.7 %copy-start = (f32[16]{0:T(128)S(1)}, f32[16]{0:T(128)}, u32[]{:S(2)}) copy-start(f32[16]{0:T(128)} %param.5) | copy-start | bytes 196
  13.9 7.3 %collective-permute-start.5 = (f16[312,128]{1,0:T(8,128)(2,1)S(1)}, f16[312,128]{1,0:T(8,128)(2,1)S(1)}, u32[]{:S(2)}, u32[]{:S(2)}) collective-permute-start(f16[312,128]{1,0:T(8,128)(2,1)S(1)} %convert_element_type.52), channel_id=1, source_target_pairs={{0,12},{4,8},{8,4},{12,0},{16,28},{20,24},{24,20},{28,16},{1,13},{... | collective-permute-start | bytes 239624 | tf_op jit(solution)/shard_map/ppermute | solution.py:38
  17.9 3.4 %collective-permute-start.6 = (f16[312,128]{1,0:T(8,128)(2,1)S(1)}, f16[312,128]{1,0:T(8,128)(2,1)S(1)}, u32[]{:S(2)}, u32[]{:S(2)}) collective-permute-start(f16[312,128]{1,0:T(8,128)(2,1)S(1)} %convert_element_type.54), channel_id=1, source_target_pairs={{0,4},{4,0},{8,12},{12,8},{16,20},{20,16},{24,28},{28,24},{1,5},{5... | collective-permute-start | bytes 239624 | tf_op jit(solution)/shard_map/ppermute | solution.py:38
  22.0 1.3 %collective-permute-start.7 = (f32[72,128]{1,0:T(8,128)S(1)}, f32[72,128]{1,0:T(8,128)S(1)}, u32[]{:S(2)}, u32[]{:S(2)}) collective-permute-start(f32[72,128]{1,0:T(8,128)S(1)} %get-tuple-element.25), channel_id=1, source_target_pairs={{0,4},{4,0},{8,12},{12,8},{16,20},{20,16},{24,28},{28,24},{1,5},{5... | collective-permute-start | bytes 110600 | tf_op jit(solution)/shard_map/ppermute | solution.py:38
  23.2 15.6 %collective-permute-start.8 = (bf16[18,128,128]{2,1,0:T(8,128)(2,1)S(1)}, bf16[18,128,128]{2,1,0:T(8,128)(2,1)S(1)}, u32[]{:S(2)}, u32[]{:S(2)}) collective-permute-start(bf16[18,128,128]{2,1,0:T(8,128)(2,1)S(1)} %get-tuple-element.26.centered_ref), channel_id=1, source_target_pairs={{0,4},{4,0},{8,12},{12,8},{16,20},{20,16},{24,28},{28,24},{1,5},{5... | collective-permute-start | bytes 1769480 | tf_op jit(solution)/shard_map/ppermute | solution.py:38
  23.4 4.9 %collective-permute-start.10 = (f32[72,128]{1,0:T(8,128)S(1)}, f32[72,128]{1,0:T(8,128)S(1)}, u32[]{:S(2)}, u32[]{:S(2)}) collective-permute-start(f32[72,128]{1,0:T(8,128)S(1)} %add.17), channel_id=1, source_target_pairs={{0,3},{1,2},{2,1},{3,0},{4,7},{5,6},{6,5},{7,4},{8,11},{9,10},{10,... | collective-permute-start | bytes 110600 | tf_op jit(solution)/shard_map/ppermute | solution.py:38
  26.1 4.0 %collective-permute-start.11 = (f32[72,128]{1,0:T(8,128)S(1)}, f32[72,128]{1,0:T(8,128)S(1)}, u32[]{:S(2)}, u32[]{:S(2)}) collective-permute-start(f32[72,128]{1,0:T(8,128)S(1)} %add.17), channel_id=1, source_target_pairs={{0,1},{1,0},{2,3},{3,2},{4,5},{5,4},{6,7},{7,6},{8,9},{9,8},{10,11... | collective-permute-start | bytes 110600 | tf_op jit(solution)/shard_map/ppermute | solution.py:38
  26.6 4.0 %collective-permute-start.9 = (f32[72,128]{1,0:T(8,128)S(1)}, f32[72,128]{1,0:T(8,128)S(1)}, u32[]{:S(2)}, u32[]{:S(2)}) collective-permute-start(f32[72,128]{1,0:T(8,128)S(1)} %add.17), channel_id=1, source_target_pairs={{0,2},{1,3},{2,0},{3,1},{4,6},{5,7},{6,4},{7,5},{8,10},{9,11},{10,... | collective-permute-start | bytes 110600 | tf_op jit(solution)/shard_map/ppermute | solution.py:38
  30.6 5.9 %collective-permute-start.12 = (f32[72,128]{1,0:T(8,128)S(1)}, f32[72,128]{1,0:T(8,128)S(1)}, u32[]{:S(2)}, u32[]{:S(2)}) collective-permute-start(f32[72,128]{1,0:T(8,128)S(1)} %add_add_fusion.refs_0_), channel_id=1, source_target_pairs={{0,24},{4,28},{8,16},{12,20},{16,8},{20,12},{24,0},{28,4},{1,25},{... | collective-permute-start | bytes 110600 | tf_op jit(solution)/shard_map/ppermute | solution.py:38
  33.9 4.9 %collective-permute-start.13 = (f32[72,128]{1,0:T(8,128)S(1)}, f32[72,128]{1,0:T(8,128)S(1)}, u32[]{:S(2)}, u32[]{:S(2)}) collective-permute-start(f32[72,128]{1,0:T(8,128)S(1)} %add_add_fusion.refs_0_), channel_id=1, source_target_pairs={{0,16},{4,20},{8,24},{12,28},{16,0},{20,4},{24,8},{28,12},{1,17},{... | collective-permute-start | bytes 110600 | tf_op jit(solution)/shard_map/ppermute | solution.py:38
  33.9 4.9 %collective-permute-start.14 = (f32[72,128]{1,0:T(8,128)S(1)}, f32[72,128]{1,0:T(8,128)S(1)}, u32[]{:S(2)}, u32[]{:S(2)}) collective-permute-start(f32[72,128]{1,0:T(8,128)S(1)} %add_add_fusion.refs_0_), channel_id=1, source_target_pairs={{0,8},{4,12},{8,0},{12,4},{16,24},{20,28},{24,16},{28,20},{1,9},{5... | collective-permute-start | bytes 110600 | tf_op jit(solution)/shard_map/ppermute | solution.py:38
  43.3 5.6 %collective-permute-start.15 = (f32[4,1152]{1,0:T(4,128)S(1)}, f32[4,1152]{1,0:T(4,128)S(1)}, u32[]{:S(2)}, u32[]{:S(2)}) collective-permute-start(f32[4,1152]{1,0:T(4,128)S(1)} %get-tuple-element.28), channel_id=1, source_target_pairs={{0,24},{4,28},{8,16},{12,20},{16,8},{20,12},{24,0},{28,4},{1,25},{... | collective-permute-start | bytes 55304 | tf_op jit(solution)/shard_map/ppermute | solution.py:38
  44.8 4.7 %collective-permute-start.16 = (f32[4,1152]{1,0:T(4,128)S(1)}, f32[4,1152]{1,0:T(4,128)S(1)}, u32[]{:S(2)}, u32[]{:S(2)}) collective-permute-start(f32[4,1152]{1,0:T(4,128)S(1)} %get-tuple-element.28), channel_id=1, source_target_pairs={{0,16},{4,20},{8,24},{12,28},{16,0},{20,4},{24,8},{28,12},{1,17},{... | collective-permute-start | bytes 55304 | tf_op jit(solution)/shard_map/ppermute | solution.py:38
  45.3 4.3 %collective-permute-start.17 = (f32[4,1152]{1,0:T(4,128)S(1)}, f32[4,1152]{1,0:T(4,128)S(1)}, u32[]{:S(2)}, u32[]{:S(2)}) collective-permute-start(f32[4,1152]{1,0:T(4,128)S(1)} %get-tuple-element.28), channel_id=1, source_target_pairs={{0,8},{4,12},{8,0},{12,4},{16,24},{20,28},{24,16},{28,20},{1,9},{5... | collective-permute-start | bytes 55304 | tf_op jit(solution)/shard_map/ppermute | solution.py:38

commit v5 on v4

--- a/solution.py
+++ b/solution.py
@@ -172,17 +172,21 @@
     gram_ref[...] = fold(gram, energies_ref[...])
 
 
+WIDTH = 16
+
+
 def thirds(values):
-    high = values.astype(BF16).astype(F32)
-    middle = (values - high).astype(BF16).astype(F32)
-    return high, middle, values - high - middle
+    high = values.astype(BF16)
+    rest = values - high.astype(F32)
+    middle = rest.astype(BF16)
+    return high, middle, (rest - middle.astype(F32)).astype(BF16)
 
 
 def outer_sum(left, right):
     a, b, c = thirds(left)
     d, e, f = thirds(right)
-    lefts = jnp.concatenate([a, a, b, a, b, c], axis=0).astype(BF16)
-    rights = jnp.concatenate([d, e, d, f, e, d], axis=0).astype(BF16)
+    lefts = jnp.concatenate([a, a, b, a, b, c], axis=0)
+    rights = jnp.concatenate([d, e, d, f, e, d], axis=0)
     return lax.dot_general(lefts, rights, (((0,), (0,)), ((), ())), preferred_element_type=F32)
 
 
@@ -192,16 +196,19 @@
 
 def eliminate(block, panel, row):
     block = list(block)
-    for step in range(0, 8, 2):
+    for step in range(0, len(block), 2):
         one, two = block[step], block[step + 1]
         a, b, c = one[step : step + 1], two[step : step + 1], two[step + 1 : step + 2]
         inverse = 1.0 / (a * c - b * b)
+        upper_row, lower_row = row == step, row == step + 1
+        done = upper_row | lower_row
+        one = jnp.where(done, jnp.where(upper_row, -1.0, 0.0), one)
+        two = jnp.where(done, jnp.where(lower_row, -1.0, 0.0), two)
 
         def reduced(rows):
             upper, lower = rows[step : step + 1], rows[step + 1 : step + 2]
             first, second = (c * upper - b * lower) * inverse, (a * lower - b * upper) * inverse
-            rest = rows - (one * first + two * second)
-            return jnp.where(row == step, first, jnp.where(row == step + 1, second, rest))
+            return jnp.where(done, 0.0, rows) - (one * first + two * second)
 
         panel = reduced(panel)
         block = [reduced(rows) if c >= step + 2 else rows for c, rows in enumerate(block)]
@@ -210,30 +217,30 @@
 
 def invert(matrix):
     matrix = list(matrix)
-    count, size = len(matrix), 8 * len(matrix)
-    row = lax.broadcasted_iota(jnp.int32, (8, size), 0)
-    lane = lax.broadcasted_iota(jnp.int32, (8, size), 1)
+    count, size = len(matrix), WIDTH * len(matrix)
+    row = lax.broadcasted_iota(jnp.int32, (WIDTH, size), 0)
+    lane = lax.broadcasted_iota(jnp.int32, (WIDTH, size), 1)
     pivot = matrix[0]
     for index in range(count):
-        first = 8 * index
-        inside = (lane >= first) & (lane < first + 8)
+        first = WIDTH * index
+        inside = (lane >= first) & (lane < first + WIDTH)
         unit = jnp.where(lane == row + first, 1.0, 0.0)
-        solved = eliminate([spread_lane(pivot, first + c) for c in range(8)], jnp.where(inside, unit, pivot), row)
+        solved = eliminate([spread_lane(pivot, first + c) for c in range(WIDTH)], jnp.where(inside, unit, pivot), row)
         solved = jnp.where(inside, -solved, solved)
         update = outer_sum(jnp.where(inside, 0.0, pivot), solved)
         following = None
         if index + 1 < count:
-            terms = [spread_lane(matrix[index + 1], first + c) * solved[c : c + 1] for c in range(8)]
-            while len(terms) > 1:
-                terms = [one + two for one, two in zip(terms[::2], terms[1::2])]
-            following = jnp.where(inside, 0.0, matrix[index + 1]) - terms[0]
+            terms = [spread_lane(matrix[index + 1], first + c) * solved[c : c + 1] for c in range(WIDTH)]
+            following = jnp.where(inside, 0.0, matrix[index + 1])
+            for term in terms:
+                following = following - term
         for other in range(count):
             if other == index:
                 matrix[other] = solved
             elif other == index + 1:
                 matrix[other] = following
             else:
-                matrix[other] = jnp.where(inside, 0.0, matrix[other]) - update[8 * other : 8 * other + 8]
+                matrix[other] = jnp.where(inside, 0.0, matrix[other]) - update[WIDTH * other : WIDTH * (other + 1)]
         pivot = following
     return matrix
 
@@ -264,10 +271,11 @@
     for ref in part_refs[1:]:
         summed = summed + ref[...]
     matrix = unfold(summed)
-    row_index = lax.broadcasted_iota(jnp.int32, (8, total), 0)
-    lane_index = lax.broadcasted_iota(jnp.int32, (8, total), 1)
+    row_index = lax.broadcasted_iota(jnp.int32, (WIDTH, total), 0)
+    lane_index = lax.broadcasted_iota(jnp.int32, (WIDTH, total), 1)
     regular = [
-        matrix[first : first + 8] + jnp.where(lane_index == row_index + first, reg_shift, 0.0) for first in range(0, total, 8)
+        matrix[first : first + WIDTH] + jnp.where(lane_index == row_index + first, reg_shift, 0.0)
+        for first in range(0, total, WIDTH)
     ]
     energies = summed[total // 2 + 1 : total // 2 + 2]
     deviation = energies - jnp.sum(energies, axis=1, keepdims=True) / total

time: 50.5 us -> 50.2 us (level)
  no operation moved by 1% of the time
where the time goes in v5:
time: 50.2 us; the launch traced here: 50 us
  starting transfers between devices  23.2 us (46%)
  waiting for transfers between devices  15.1 us (30%)
  Pallas kernels  9.18 us (18%)
  other arithmetic  0.98 us (2%)
  between operations  0.83 us (2%)
  local copies, waits for them, and re-layouts  0.73 us (1%)
    ppermute x18, starting transfers between devices, swap(): return lax.ppermute(x, axis, [(i, i ^ mask) for i in range(count)])  23.2 us
    ppermute x18, waiting for transfers between devices, swap(): return lax.ppermute(x, axis, [(i, i ^ mask) for i in range(count)])  15.1 us
    pallas_call x2, Pallas kernels, half(): kernel_call(functools.partial(grads_body, far), out_shape, [pltpu.VMEM(ac...  4.3 us
    pallas_call x1, Pallas kernels, local_split(): kernel_call(functools.partial(solve_body, -math.sqrt(params_all / total))...  4.22 us
  transfers between devices with their start and end apart: 18, of which 12 were waited for; matrix products, arithmetic and copies ran while one was open for 1% of the time, Pallas kernels for 4%

profile of v5, /device:TPU:0, one launch (start us, length us, event | category | flops | bytes accessed | tf_op | source)
XLA Modules:
  0.0 50.0 jit_solution(17040214628274552345)
XLA Ops:
  0.6 2.2 %shard_map.51 = (f32[312,128]{1,0:T(8,128)S(1)}, f32[312,128]{1,0:T(8,128)S(1)}, f32[312,128]{1,0:T(8,128)S(1)}, f32[312,128]{1,0:T(8,128)S(1)}) custom-call(bf16[16,2,64,256]{3,2,1,0:T(8,128)(2,1)} %acts_hbm.3, bf16[16,2,16,256]{3,2,1,0:T(8,128)(2,1)} %cots_hbm.3), custom_call_target="tpu_custom_call" | custom-call | tf_op jit(solution)/shard_map/pallas_call | solution.py:345
  2.8 4.1 %collective-permute-start = (f16[312,128]{1,0:T(8,128)(2,1)S(1)}, f16[312,128]{1,0:T(8,128)(2,1)S(1)}, u32[]{:S(2)}, u32[]{:S(2)}) collective-permute-start(f16[312,128]{1,0:T(8,128)(2,1)S(1)} %convert_element_type.42), channel_id=1, source_target_pairs={{0,16},{4,20},{8,24},{12,28},{16,0},{20,4},{24,8},{28,12},{1,17},{... | collective-permute-start | bytes 239624 | tf_op jit(solution)/shard_map/ppermute | solution.py:38
  6.9 0.1 collective-permute-start.1
  7.0 3.1 %collective-permute-start.2 = (f16[312,128]{1,0:T(8,128)(2,1)S(1)}, f16[312,128]{1,0:T(8,128)(2,1)S(1)}, u32[]{:S(2)}, u32[]{:S(2)}) collective-permute-start(f16[312,128]{1,0:T(8,128)(2,1)S(1)} %convert_element_type.46), channel_id=1, source_target_pairs={{0,24},{4,28},{8,16},{12,20},{16,8},{20,12},{24,0},{28,4},{1,25},{... | collective-permute-start | bytes 239624 | tf_op jit(solution)/shard_map/ppermute | solution.py:38
  10.2 0.6 %collective-permute-start.3 = (f16[312,128]{1,0:T(8,128)(2,1)S(1)}, f16[312,128]{1,0:T(8,128)(2,1)S(1)}, u32[]{:S(2)}, u32[]{:S(2)}) collective-permute-start(f16[312,128]{1,0:T(8,128)(2,1)S(1)} %convert_element_type.48), channel_id=1, source_target_pairs={{0,28},{4,24},{8,20},{12,16},{16,12},{20,8},{24,4},{28,0},{1,29},{... | collective-permute-start | bytes 239624 | tf_op jit(solution)/shard_map/ppermute | solution.py:38
  10.9 2.1 %shard_map.50 = (f32[18,16,128]{2,1,0:T(8,128)S(1)}, f32[312,128]{1,0:T(8,128)S(1)}, f32[312,128]{1,0:T(8,128)S(1)}, f32[312,128]{1,0:T(8,128)S(1)}) custom-call(bf16[16,2,64,256]{3,2,1,0:T(8,128)(2,1)} %acts_hbm.3, bf16[16,2,16,256]{3,2,1,0:T(8,128)(2,1)} %cots_hbm.3), custom_call_target="tpu_custom_call" | custom-call | tf_op jit(solution)/shard_map/pallas_call | solution.py:345
  13.0 0.1 collective-permute-start.4
  13.1 0.0 copy-start
  13.2 0.6 %copy-done = f32[16]{0:T(128)S(1)} copy-done((f32[16]{0:T(128)S(1)}, f32[16]{0:T(128)}, u32[]{:S(2)}) %copy-start) | copy-done | bytes 88
  13.8 0.1 tile.10
  13.9 0.0 collective-permute-done
  13.9 2.5 %collective-permute-start.5 = (f16[312,128]{1,0:T(8,128)(2,1)S(1)}, f16[312,128]{1,0:T(8,128)(2,1)S(1)}, u32[]{:S(2)}, u32[]{:S(2)}) collective-permute-start(f16[312,128]{1,0:T(8,128)(2,1)S(1)} %convert_element_type.52), channel_id=1, source_target_pairs={{0,12},{4,8},{8,4},{12,0},{16,28},{20,24},{24,20},{28,16},{1,13},{... | collective-permute-start | bytes 239624 | tf_op jit(solution)/shard_map/ppermute | solution.py:38
  16.4 1.5 %collective-permute-done.1 = f16[312,128]{1,0:T(8,128)(2,1)S(1)} collective-permute-done((f16[312,128]{1,0:T(8,128)(2,1)S(1)}, f16[312,128]{1,0:T(8,128)(2,1)S(1)}, u32[]{:S(2)}, u32[]{:S(2)}) %collective-permute-start.1) | collective-permute-done | bytes 79904 | tf_op jit(solution)/shard_map/ppermute | solution.py:38
  17.9 0.1 collective-permute-start.6
  18.0 0.1 broadcast_select_fusion.energies_ref
  18.1 0.0 collective-permute-done.2
  18.1 0.0 collective-permute-done.3
  18.1 1.5 %collective-permute-done.4 = f16[312,128]{1,0:T(8,128)(2,1)S(1)} collective-permute-done((f16[312,128]{1,0:T(8,128)(2,1)S(1)}, f16[312,128]{1,0:T(8,128)(2,1)S(1)}, u32[]{:S(2)}, u32[]{:S(2)}) %collective-permute-start.4) | collective-permute-done | bytes 79904 | tf_op jit(solution)/shard_map/ppermute | solution.py:38
  19.7 1.6 %collective-permute-done.5 = f16[312,128]{1,0:T(8,128)(2,1)S(1)} collective-permute-done((f16[312,128]{1,0:T(8,128)(2,1)S(1)}, f16[312,128]{1,0:T(8,128)(2,1)S(1)}, u32[]{:S(2)}, u32[]{:S(2)}) %collective-permute-start.5) | collective-permute-done | bytes 79904 | tf_op jit(solution)/shard_map/ppermute | solution.py:38
  21.3 0.0 collective-permute-done.6
  21.3 0.7 %shard_map.52 = (bf16[18,128,128]{2,1,0:T(8,128)(2,1)S(1)}, f32[72,128]{1,0:T(8,128)S(1)}) custom-call(f32[8,128]{1,0:T(8,128)S(1)} %broadcast_select_fusion.energies_ref, f32[18,16,128]{2,1,0:T(8,128)S(1)} %get-tuple-element.16.own_ref, f32[312,128]{1,0:T(8,128)S(1)} %convert_element_type.43.refs_0_, f32[312,128]{1,0:T(8,128)S(1)} %convert_element_type.45.refs_1_, ...), custom_call_target="tpu_custom_call" | custom-call | tf_op jit(solution)/shard_map/pallas_call | solution.py:368
  22.0 0.2 collective-permute-start.7
  22.1 1.1 %collective-permute-done.7 = f32[72,128]{1,0:T(8,128)S(1)} collective-permute-done((f32[72,128]{1,0:T(8,128)S(1)}, f32[72,128]{1,0:T(8,128)S(1)}, u32[]{:S(2)}, u32[]{:S(2)}) %collective-permute-start.7) | collective-permute-done | bytes 36896 | tf_op jit(solution)/shard_map/ppermute | solution.py:38
  23.2 0.2 collective-permute-start.8
  23.4 2.7 %collective-permute-start.10 = (f32[72,128]{1,0:T(8,128)S(1)}, f32[72,128]{1,0:T(8,128)S(1)}, u32[]{:S(2)}, u32[]{:S(2)}) collective-permute-start(f32[72,128]{1,0:T(8,128)S(1)} %add.17), channel_id=1, source_target_pairs={{0,3},{1,2},{2,1},{3,0},{4,7},{5,6},{6,5},{7,4},{8,11},{9,10},{10,... | collective-permute-start | bytes 110600 | tf_op jit(solution)/shard_map/ppermute | solution.py:38
  26.1 0.5 %collective-permute-start.11 = (f32[72,128]{1,0:T(8,128)S(1)}, f32[72,128]{1,0:T(8,128)S(1)}, u32[]{:S(2)}, u32[]{:S(2)}) collective-permute-start(f32[72,128]{1,0:T(8,128)S(1)} %add.17), channel_id=1, source_target_pairs={{0,1},{1,0},{2,3},{3,2},{4,5},{5,4},{6,7},{7,6},{8,9},{9,8},{10,11... | collective-permute-start | bytes 110600 | tf_op jit(solution)/shard_map/ppermute | solution.py:38
  26.6 0.3 collective-permute-start.9
  26.9 1.4 %collective-permute-done.10 = f32[72,128]{1,0:T(8,128)S(1)} collective-permute-done((f32[72,128]{1,0:T(8,128)S(1)}, f32[72,128]{1,0:T(8,128)S(1)}, u32[]{:S(2)}, u32[]{:S(2)}) %collective-permute-start.10) | collective-permute-done | bytes 36896 | tf_op jit(solution)/shard_map/ppermute | solution.py:38
  28.3 1.8 %collective-permute-done.11 = f32[72,128]{1,0:T(8,128)S(1)} collective-permute-done((f32[72,128]{1,0:T(8,128)S(1)}, f32[72,128]{1,0:T(8,128)S(1)}, u32[]{:S(2)}, u32[]{:S(2)}) %collective-permute-start.11) | collective-permute-done | bytes 36896 | tf_op jit(solution)/shard_map/ppermute | solution.py:38
  30.0 0.5 %collective-permute-done.9 = f32[72,128]{1,0:T(8,128)S(1)} collective-permute-done((f32[72,128]{1,0:T(8,128)S(1)}, f32[72,128]{1,0:T(8,128)S(1)}, u32[]{:S(2)}, u32[]{:S(2)}) %collective-permute-start.9) | collective-permute-done | bytes 36896 | tf_op jit(solution)/shard_map/ppermute | solution.py:38
  30.6 3.4 %collective-permute-start.12 = (f32[72,128]{1,0:T(8,128)S(1)}, f32[72,128]{1,0:T(8,128)S(1)}, u32[]{:S(2)}, u32[]{:S(2)}) collective-permute-start(f32[72,128]{1,0:T(8,128)S(1)} %add_add_fusion.refs_0_), channel_id=1, source_target_pairs={{0,24},{4,28},{8,16},{12,20},{16,8},{20,12},{24,0},{28,4},{1,25},{... | collective-permute-start | bytes 110600 | tf_op jit(solution)/shard_map/ppermute | solution.py:38
  33.9 0.0 collective-permute-start.13
  33.9 1.1 %collective-permute-start.14 = (f32[72,128]{1,0:T(8,128)S(1)}, f32[72,128]{1,0:T(8,128)S(1)}, u32[]{:S(2)}, u32[]{:S(2)}) collective-permute-start(f32[72,128]{1,0:T(8,128)S(1)} %add_add_fusion.refs_0_), channel_id=1, source_target_pairs={{0,8},{4,12},{8,0},{12,4},{16,24},{20,28},{24,16},{28,20},{1,9},{5... | collective-permute-start | bytes 110600 | tf_op jit(solution)/shard_map/ppermute | solution.py:38
  35.0 1.5 %collective-permute-done.12.refs_1_ = f32[72,128]{1,0:T(8,128)S(1)} collective-permute-done((f32[72,128]{1,0:T(8,128)S(1)}, f32[72,128]{1,0:T(8,128)S(1)}, u32[]{:S(2)}, u32[]{:S(2)}) %collective-permute-start.12) | collective-permute-done | bytes 36896 | tf_op jit(solution)/shard_map/ppermute | solution.py:38
  36.5 2.3 %collective-permute-done.13.refs_2_ = f32[72,128]{1,0:T(8,128)S(1)} collective-permute-done((f32[72,128]{1,0:T(8,128)S(1)}, f32[72,128]{1,0:T(8,128)S(1)}, u32[]{:S(2)}, u32[]{:S(2)}) %collective-permute-start.13) | collective-permute-done | bytes 36896 | tf_op jit(solution)/shard_map/ppermute | solution.py:38
  38.8 0.0 collective-permute-done.14.refs_3_
  38.8 0.0 collective-permute-done.8.across_ref
  38.8 4.2 %shard_map.53 = (f32[4,1152]{1,0:T(4,128)S(1)}, f32[1,16]{1,0:T(1,128)}) custom-call(bf16[18,128,128]{2,1,0:T(8,128)(2,1)S(1)} %get-tuple-element.26.centered_ref, bf16[18,128,128]{2,1,0:T(8,128)(2,1)S(1)} %collective-permute-done.8.across_ref, f32[72,128]{1,0:T(8,128)S(1)} %add_add_fusion.refs_0_, f32[72,128]{1,0:T(8,128)S(1)} %collective-permute-done.12.refs_1_, ...), custom_call_target="tpu_custom_call" | custom-call | tf_op jit(solution)/shard_map/pallas_call | solution.py:379
  43.0 1.5 %collective-permute-start.15 = (f32[4,1152]{1,0:T(4,128)S(1)}, f32[4,1152]{1,0:T(4,128)S(1)}, u32[]{:S(2)}, u32[]{:S(2)}) collective-permute-start(f32[4,1152]{1,0:T(4,128)S(1)} %get-tuple-element.28), channel_id=1, source_target_pairs={{0,24},{4,28},{8,16},{12,20},{16,8},{20,12},{24,0},{28,4},{1,25},{... | collective-permute-start | bytes 55304 | tf_op jit(solution)/shard_map/ppermute | solution.py:38
  44.5 0.6 %collective-permute-start.16 = (f32[4,1152]{1,0:T(4,128)S(1)}, f32[4,1152]{1,0:T(4,128)S(1)}, u32[]{:S(2)}, u32[]{:S(2)}) collective-permute-start(f32[4,1152]{1,0:T(4,128)S(1)} %get-tuple-element.28), channel_id=1, source_target_pairs={{0,16},{4,20},{8,24},{12,28},{16,0},{20,4},{24,8},{28,12},{1,17},{... | collective-permute-start | bytes 55304 | tf_op jit(solution)/shard_map/ppermute | solution.py:38
  45.0 2.4 %collective-permute-start.17 = (f32[4,1152]{1,0:T(4,128)S(1)}, f32[4,1152]{1,0:T(4,128)S(1)}, u32[]{:S(2)}, u32[]{:S(2)}) collective-permute-start(f32[4,1152]{1,0:T(4,128)S(1)} %get-tuple-element.28), channel_id=1, source_target_pairs={{0,8},{4,12},{8,0},{12,4},{16,24},{20,28},{24,16},{28,20},{1,9},{5... | collective-permute-start | bytes 55304 | tf_op jit(solution)/shard_map/ppermute | solution.py:38
  47.4 1.2 %collective-permute-done.15 = f32[4,1152]{1,0:T(4,128)S(1)} collective-permute-done((f32[4,1152]{1,0:T(4,128)S(1)}, f32[4,1152]{1,0:T(4,128)S(1)}, u32[]{:S(2)}, u32[]{:S(2)}) %collective-permute-start.15) | collective-permute-done | bytes 18464 | tf_op jit(solution)/shard_map/ppermute | solution.py:38
  48.6 0.6 %collective-permute-done.16 = f32[4,1152]{1,0:T(4,128)S(1)} collective-permute-done((f32[4,1152]{1,0:T(4,128)S(1)}, f32[4,1152]{1,0:T(4,128)S(1)}, u32[]{:S(2)}, u32[]{:S(2)}) %collective-permute-start.16) | collective-permute-done | bytes 18464 | tf_op jit(solution)/shard_map/ppermute | solution.py:38
  49.2 0.2 collective-permute-done.17
  49.4 0.7 %pad_maximum_fusion = f32[16,1152]{1,0:T(8,128)} fusion(f32[4,1152]{1,0:T(4,128)S(1)} %get-tuple-element.31, f32[4,1152]{1,0:T(4,128)S(1)} %get-tuple-element.32, f32[4,1152]{1,0:T(4,128)S(1)} %get-tuple-element.33, f32[4,1152]{1,0:T(4,128)S(1)} %get-tuple-element.30), kind=kLoop, calls=%fused_computation | loop fusion | flops 55296 | bytes 147456 | tf_op jit(solution)/shard_map/concatenate | solution.py:319
  (20 shorter events, 0.3 us)
Async XLA Ops:
  2.8 11.1 %collective-permute-start = (f16[312,128]{1,0:T(8,128)(2,1)S(1)}, f16[312,128]{1,0:T(8,128)(2,1)S(1)}, u32[]{:S(2)}, u32[]{:S(2)}) collective-permute-start(f16[312,128]{1,0:T(8,128)(2,1)S(1)} %convert_element_type.42), channel_id=1, source_target_pairs={{0,16},{4,20},{8,24},{12,28},{16,0},{20,4},{24,8},{28,12},{1,17},{... | collective-permute-start | bytes 239624 | tf_op jit(solution)/shard_map/ppermute | solution.py:38
  6.9 11.0 %collective-permute-start.1 = (f16[312,128]{1,0:T(8,128)(2,1)S(1)}, f16[312,128]{1,0:T(8,128)(2,1)S(1)}, u32[]{:S(2)}, u32[]{:S(2)}) collective-permute-start(f16[312,128]{1,0:T(8,128)(2,1)S(1)} %convert_element_type.44), channel_id=1, source_target_pairs={{0,20},{4,16},{8,28},{12,24},{16,4},{20,0},{24,12},{28,8},{1,21},{... | collective-permute-start | bytes 239624 | tf_op jit(solution)/shard_map/ppermute | solution.py:38
  7.0 11.0 %collective-permute-start.2 = (f16[312,128]{1,0:T(8,128)(2,1)S(1)}, f16[312,128]{1,0:T(8,128)(2,1)S(1)}, u32[]{:S(2)}, u32[]{:S(2)}) collective-permute-start(f16[312,128]{1,0:T(8,128)(2,1)S(1)} %convert_element_type.46), channel_id=1, source_target_pairs={{0,24},{4,28},{8,16},{12,20},{16,8},{20,12},{24,0},{28,4},{1,25},{... | collective-permute-start | bytes 239624 | tf_op jit(solution)/shard_map/ppermute | solution.py:38
  10.2 7.9 %collective-permute-start.3 = (f16[312,128]{1,0:T(8,128)(2,1)S(1)}, f16[312,128]{1,0:T(8,128)(2,1)S(1)}, u32[]{:S(2)}, u32[]{:S(2)}) collective-permute-start(f16[312,128]{1,0:T(8,128)(2,1)S(1)} %convert_element_type.48), channel_id=1, source_target_pairs={{0,28},{4,24},{8,20},{12,16},{16,12},{20,8},{24,4},{28,0},{1,29},{... | collective-permute-start | bytes 239624 | tf_op jit(solution)/shard_map/ppermute | solution.py:38
  13.0 6.6 %collective-permute-start.4 = (f16[312,128]{1,0:T(8,128)(2,1)S(1)}, f16[312,128]{1,0:T(8,128)(2,1)S(1)}, u32[]{:S(2)}, u32[]{:S(2)}) collective-permute-start(f16[312,128]{1,0:T(8,128)(2,1)S(1)} %convert_element_type.50), channel_id=1, source_target_pairs={{0,8},{4,12},{8,0},{12,4},{16,24},{20,28},{24,16},{28,20},{1,9},{5... | collective-permute-start | bytes 239624 | tf_op jit(solution)/shard_map/ppermute | solution.py:38
  13.1 0.7 %copy-start = (f32[16]{0:T(128)S(1)}, f32[16]{0:T(128)}, u32[]{:S(2)}) copy-start(f32[16]{0:T(128)} %param.5) | copy-start | bytes 196
  13.9 7.3 %collective-permute-start.5 = (f16[312,128]{1,0:T(8,128)(2,1)S(1)}, f16[312,128]{1,0:T(8,128)(2,1)S(1)}, u32[]{:S(2)}, u32[]{:S(2)}) collective-permute-start(f16[312,128]{1,0:T(8,128)(2,1)S(1)} %convert_element_type.52), channel_id=1, source_target_pairs={{0,12},{4,8},{8,4},{12,0},{16,28},{20,24},{24,20},{28,16},{1,13},{... | collective-permute-start | bytes 239624 | tf_op jit(solution)/shard_map/ppermute | solution.py:38
  17.9 3.4 %collective-permute-start.6 = (f16[312,128]{1,0:T(8,128)(2,1)S(1)}, f16[312,128]{1,0:T(8,128)(2,1)S(1)}, u32[]{:S(2)}, u32[]{:S(2)}) collective-permute-start(f16[312,128]{1,0:T(8,128)(2,1)S(1)} %convert_element_type.54), channel_id=1, source_target_pairs={{0,4},{4,0},{8,12},{12,8},{16,20},{20,16},{24,28},{28,24},{1,5},{5... | collective-permute-start | bytes 239624 | tf_op jit(solution)/shard_map/ppermute | solution.py:38
  22.0 1.3 %collective-permute-start.7 = (f32[72,128]{1,0:T(8,128)S(1)}, f32[72,128]{1,0:T(8,128)S(1)}, u32[]{:S(2)}, u32[]{:S(2)}) collective-permute-start(f32[72,128]{1,0:T(8,128)S(1)} %get-tuple-element.25), channel_id=1, source_target_pairs={{0,4},{4,0},{8,12},{12,8},{16,20},{20,16},{24,28},{28,24},{1,5},{5... | collective-permute-start | bytes 110600 | tf_op jit(solution)/shard_map/ppermute | solution.py:38
  23.2 15.6 %collective-permute-start.8 = (bf16[18,128,128]{2,1,0:T(8,128)(2,1)S(1)}, bf16[18,128,128]{2,1,0:T(8,128)(2,1)S(1)}, u32[]{:S(2)}, u32[]{:S(2)}) collective-permute-start(bf16[18,128,128]{2,1,0:T(8,128)(2,1)S(1)} %get-tuple-element.26.centered_ref), channel_id=1, source_target_pairs={{0,4},{4,0},{8,12},{12,8},{16,20},{20,16},{24,28},{28,24},{1,5},{5... | collective-permute-start | bytes 1769480 | tf_op jit(solution)/shard_map/ppermute | solution.py:38
  23.4 4.9 %collective-permute-start.10 = (f32[72,128]{1,0:T(8,128)S(1)}, f32[72,128]{1,0:T(8,128)S(1)}, u32[]{:S(2)}, u32[]{:S(2)}) collective-permute-start(f32[72,128]{1,0:T(8,128)S(1)} %add.17), channel_id=1, source_target_pairs={{0,3},{1,2},{2,1},{3,0},{4,7},{5,6},{6,5},{7,4},{8,11},{9,10},{10,... | collective-permute-start | bytes 110600 | tf_op jit(solution)/shard_map/ppermute | solution.py:38
  26.1 4.0 %collective-permute-start.11 = (f32[72,128]{1,0:T(8,128)S(1)}, f32[72,128]{1,0:T(8,128)S(1)}, u32[]{:S(2)}, u32[]{:S(2)}) collective-permute-start(f32[72,128]{1,0:T(8,128)S(1)} %add.17), channel_id=1, source_target_pairs={{0,1},{1,0},{2,3},{3,2},{4,5},{5,4},{6,7},{7,6},{8,9},{9,8},{10,11... | collective-permute-start | bytes 110600 | tf_op jit(solution)/shard_map/ppermute | solution.py:38
  26.6 4.0 %collective-permute-start.9 = (f32[72,128]{1,0:T(8,128)S(1)}, f32[72,128]{1,0:T(8,128)S(1)}, u32[]{:S(2)}, u32[]{:S(2)}) collective-permute-start(f32[72,128]{1,0:T(8,128)S(1)} %add.17), channel_id=1, source_target_pairs={{0,2},{1,3},{2,0},{3,1},{4,6},{5,7},{6,4},{7,5},{8,10},{9,11},{10,... | collective-permute-start | bytes 110600 | tf_op jit(solution)/shard_map/ppermute | solution.py:38
  30.6 5.9 %collective-permute-start.12 = (f32[72,128]{1,0:T(8,128)S(1)}, f32[72,128]{1,0:T(8,128)S(1)}, u32[]{:S(2)}, u32[]{:S(2)}) collective-permute-start(f32[72,128]{1,0:T(8,128)S(1)} %add_add_fusion.refs_0_), channel_id=1, source_target_pairs={{0,24},{4,28},{8,16},{12,20},{16,8},{20,12},{24,0},{28,4},{1,25},{... | collective-permute-start | bytes 110600 | tf_op jit(solution)/shard_map/ppermute | solution.py:38
  33.9 4.9 %collective-permute-start.13 = (f32[72,128]{1,0:T(8,128)S(1)}, f32[72,128]{1,0:T(8,128)S(1)}, u32[]{:S(2)}, u32[]{:S(2)}) collective-permute-start(f32[72,128]{1,0:T(8,128)S(1)} %add_add_fusion.refs_0_), channel_id=1, source_target_pairs={{0,16},{4,20},{8,24},{12,28},{16,0},{20,4},{24,8},{28,12},{1,17},{... | collective-permute-start | bytes 110600 | tf_op jit(solution)/shard_map/ppermute | solution.py:38
  33.9 4.9 %collective-permute-start.14 = (f32[72,128]{1,0:T(8,128)S(1)}, f32[72,128]{1,0:T(8,128)S(1)}, u32[]{:S(2)}, u32[]{:S(2)}) collective-permute-start(f32[72,128]{1,0:T(8,128)S(1)} %add_add_fusion.refs_0_), channel_id=1, source_target_pairs={{0,8},{4,12},{8,0},{12,4},{16,24},{20,28},{24,16},{28,20},{1,9},{5... | collective-permute-start | bytes 110600 | tf_op jit(solution)/shard_map/ppermute | solution.py:38
  43.0 5.6 %collective-permute-start.15 = (f32[4,1152]{1,0:T(4,128)S(1)}, f32[4,1152]{1,0:T(4,128)S(1)}, u32[]{:S(2)}, u32[]{:S(2)}) collective-permute-start(f32[4,1152]{1,0:T(4,128)S(1)} %get-tuple-element.28), channel_id=1, source_target_pairs={{0,24},{4,28},{8,16},{12,20},{16,8},{20,12},{24,0},{28,4},{1,25},{... | collective-permute-start | bytes 55304 | tf_op jit(solution)/shard_map/ppermute | solution.py:38
  44.5 4.7 %collective-permute-start.16 = (f32[4,1152]{1,0:T(4,128)S(1)}, f32[4,1152]{1,0:T(4,128)S(1)}, u32[]{:S(2)}, u32[]{:S(2)}) collective-permute-start(f32[4,1152]{1,0:T(4,128)S(1)} %get-tuple-element.28), channel_id=1, source_target_pairs={{0,16},{4,20},{8,24},{12,28},{16,0},{20,4},{24,8},{28,12},{1,17},{... | collective-permute-start | bytes 55304 | tf_op jit(solution)/shard_map/ppermute | solution.py:38
  45.0 4.3 %collective-permute-start.17 = (f32[4,1152]{1,0:T(4,128)S(1)}, f32[4,1152]{1,0:T(4,128)S(1)}, u32[]{:S(2)}, u32[]{:S(2)}) collective-permute-start(f32[4,1152]{1,0:T(4,128)S(1)} %get-tuple-element.28), channel_id=1, source_target_pairs={{0,8},{4,12},{8,0},{12,4},{16,24},{20,28},{24,16},{28,20},{1,9},{5... | collective-permute-start | bytes 55304 | tf_op jit(solution)/shard_map/ppermute | solution.py:38

commit v6 on v5

--- a/solution.py
+++ b/solution.py
@@ -349,7 +349,7 @@
                 pltpu.VMEM(activations.shape, BF16),
                 pltpu.VMEM(cotangents.shape, BF16),
                 pltpu.VMEM((OFFSETS, samples * layers * owned // 2, sites), BF16),
-                pltpu.VMEM((OFFSETS * owned // 2 * samples, LANES), F32),
+                pltpu.VMEM(((OFFSETS * owned // 2 + 1) * samples, LANES), F32),
                 pltpu.SemaphoreType.DMA((2,)),
             ],
             in_specs=[pl.BlockSpec(memory_space=pltpu.HBM)] * 2,

time: 50.2 us -> 50.2 us (level)
  no operation moved by 1% of the time
where the time goes in v6:
time: 50.2 us; the launch traced here: 50 us
  starting transfers between devices  23.2 us (46%)
  waiting for transfers between devices  15.1 us (30%)
  Pallas kernels  9.2 us (18%)
  other arithmetic  0.98 us (2%)
  between operations  0.83 us (2%)
  local copies, waits for them, and re-layouts  0.73 us (1%)
    ppermute x18, starting transfers between devices, swap(): return lax.ppermute(x, axis, [(i, i ^ mask) for i in range(count)])  23.2 us
    ppermute x18, waiting for transfers between devices, swap(): return lax.ppermute(x, axis, [(i, i ^ mask) for i in range(count)])  15.1 us
    pallas_call x2, Pallas kernels, half(): kernel_call(functools.partial(grads_body, far), out_shape, [pltpu.VMEM(ac...  4.31 us
    pallas_call x1, Pallas kernels, local_split(): kernel_call(functools.partial(solve_body, -math.sqrt(params_all / total))...  4.23 us
  transfers between devices with their start and end apart: 18, of which 12 were waited for; matrix products, arithmetic and copies ran while one was open for 1% of the time, Pallas kernels for 4%

profile of v6, /device:TPU:0, one launch (start us, length us, event | category | flops | bytes accessed | tf_op | source)
XLA Modules:
  0.0 50.0 jit_solution(2565999372959273436)
XLA Ops:
  0.6 2.2 %shard_map.51 = (f32[312,128]{1,0:T(8,128)S(1)}, f32[312,128]{1,0:T(8,128)S(1)}, f32[312,128]{1,0:T(8,128)S(1)}, f32[312,128]{1,0:T(8,128)S(1)}) custom-call(bf16[16,2,64,256]{3,2,1,0:T(8,128)(2,1)} %acts_hbm.3, bf16[16,2,16,256]{3,2,1,0:T(8,128)(2,1)} %cots_hbm.3), custom_call_target="tpu_custom_call" | custom-call | tf_op jit(solution)/shard_map/pallas_call | solution.py:345
  2.8 4.1 %collective-permute-start = (f16[312,128]{1,0:T(8,128)(2,1)S(1)}, f16[312,128]{1,0:T(8,128)(2,1)S(1)}, u32[]{:S(2)}, u32[]{:S(2)}) collective-permute-start(f16[312,128]{1,0:T(8,128)(2,1)S(1)} %convert_element_type.42), channel_id=1, source_target_pairs={{0,16},{4,20},{8,24},{12,28},{16,0},{20,4},{24,8},{28,12},{1,17},{... | collective-permute-start | bytes 239624 | tf_op jit(solution)/shard_map/ppermute | solution.py:38
  6.9 0.1 collective-permute-start.1
  7.1 3.1 %collective-permute-start.2 = (f16[312,128]{1,0:T(8,128)(2,1)S(1)}, f16[312,128]{1,0:T(8,128)(2,1)S(1)}, u32[]{:S(2)}, u32[]{:S(2)}) collective-permute-start(f16[312,128]{1,0:T(8,128)(2,1)S(1)} %convert_element_type.46), channel_id=1, source_target_pairs={{0,24},{4,28},{8,16},{12,20},{16,8},{20,12},{24,0},{28,4},{1,25},{... | collective-permute-start | bytes 239624 | tf_op jit(solution)/shard_map/ppermute | solution.py:38
  10.2 0.6 %collective-permute-start.3 = (f16[312,128]{1,0:T(8,128)(2,1)S(1)}, f16[312,128]{1,0:T(8,128)(2,1)S(1)}, u32[]{:S(2)}, u32[]{:S(2)}) collective-permute-start(f16[312,128]{1,0:T(8,128)(2,1)S(1)} %convert_element_type.48), channel_id=1, source_target_pairs={{0,28},{4,24},{8,20},{12,16},{16,12},{20,8},{24,4},{28,0},{1,29},{... | collective-permute-start | bytes 239624 | tf_op jit(solution)/shard_map/ppermute | solution.py:38
  10.9 2.1 %shard_map.50 = (f32[18,16,128]{2,1,0:T(8,128)S(1)}, f32[312,128]{1,0:T(8,128)S(1)}, f32[312,128]{1,0:T(8,128)S(1)}, f32[312,128]{1,0:T(8,128)S(1)}) custom-call(bf16[16,2,64,256]{3,2,1,0:T(8,128)(2,1)} %acts_hbm.3, bf16[16,2,16,256]{3,2,1,0:T(8,128)(2,1)} %cots_hbm.3), custom_call_target="tpu_custom_call" | custom-call | tf_op jit(solution)/shard_map/pallas_call | solution.py:345
  13.0 0.1 collective-permute-start.4
  13.2 0.0 copy-start
  13.2 0.6 %copy-done = f32[16]{0:T(128)S(1)} copy-done((f32[16]{0:T(128)S(1)}, f32[16]{0:T(128)}, u32[]{:S(2)}) %copy-start) | copy-done | bytes 88
  13.8 0.1 tile.10
  13.9 0.0 collective-permute-done
  13.9 2.4 %collective-permute-start.5 = (f16[312,128]{1,0:T(8,128)(2,1)S(1)}, f16[312,128]{1,0:T(8,128)(2,1)S(1)}, u32[]{:S(2)}, u32[]{:S(2)}) collective-permute-start(f16[312,128]{1,0:T(8,128)(2,1)S(1)} %convert_element_type.52), channel_id=1, source_target_pairs={{0,12},{4,8},{8,4},{12,0},{16,28},{20,24},{24,20},{28,16},{1,13},{... | collective-permute-start | bytes 239624 | tf_op jit(solution)/shard_map/ppermute | solution.py:38
  16.4 1.5 %collective-permute-done.1 = f16[312,128]{1,0:T(8,128)(2,1)S(1)} collective-permute-done((f16[312,128]{1,0:T(8,128)(2,1)S(1)}, f16[312,128]{1,0:T(8,128)(2,1)S(1)}, u32[]{:S(2)}, u32[]{:S(2)}) %collective-permute-start.1) | collective-permute-done | bytes 79904 | tf_op jit(solution)/shard_map/ppermute | solution.py:38
  17.9 0.1 collective-permute-start.6
  18.0 0.1 broadcast_select_fusion.energies_ref
  18.1 0.0 collective-permute-done.2
  18.1 0.0 collective-permute-done.3
  18.1 1.5 %collective-permute-done.4 = f16[312,128]{1,0:T(8,128)(2,1)S(1)} collective-permute-done((f16[312,128]{1,0:T(8,128)(2,1)S(1)}, f16[312,128]{1,0:T(8,128)(2,1)S(1)}, u32[]{:S(2)}, u32[]{:S(2)}) %collective-permute-start.4) | collective-permute-done | bytes 79904 | tf_op jit(solution)/shard_map/ppermute | solution.py:38
  19.7 1.6 %collective-permute-done.5 = f16[312,128]{1,0:T(8,128)(2,1)S(1)} collective-permute-done((f16[312,128]{1,0:T(8,128)(2,1)S(1)}, f16[312,128]{1,0:T(8,128)(2,1)S(1)}, u32[]{:S(2)}, u32[]{:S(2)}) %collective-permute-start.5) | collective-permute-done | bytes 79904 | tf_op jit(solution)/shard_map/ppermute | solution.py:38
  21.3 0.0 collective-permute-done.6
  21.3 0.7 %shard_map.52 = (bf16[18,128,128]{2,1,0:T(8,128)(2,1)S(1)}, f32[72,128]{1,0:T(8,128)S(1)}) custom-call(f32[8,128]{1,0:T(8,128)S(1)} %broadcast_select_fusion.energies_ref, f32[18,16,128]{2,1,0:T(8,128)S(1)} %get-tuple-element.16.own_ref, f32[312,128]{1,0:T(8,128)S(1)} %convert_element_type.43.refs_0_, f32[312,128]{1,0:T(8,128)S(1)} %convert_element_type.45.refs_1_, ...), custom_call_target="tpu_custom_call" | custom-call | tf_op jit(solution)/shard_map/pallas_call | solution.py:368
  22.0 0.2 collective-permute-start.7
  22.1 1.1 %collective-permute-done.7 = f32[72,128]{1,0:T(8,128)S(1)} collective-permute-done((f32[72,128]{1,0:T(8,128)S(1)}, f32[72,128]{1,0:T(8,128)S(1)}, u32[]{:S(2)}, u32[]{:S(2)}) %collective-permute-start.7) | collective-permute-done | bytes 36896 | tf_op jit(solution)/shard_map/ppermute | solution.py:38
  23.2 0.2 collective-permute-start.8
  23.4 2.7 %collective-permute-start.10 = (f32[72,128]{1,0:T(8,128)S(1)}, f32[72,128]{1,0:T(8,128)S(1)}, u32[]{:S(2)}, u32[]{:S(2)}) collective-permute-start(f32[72,128]{1,0:T(8,128)S(1)} %add.17), channel_id=1, source_target_pairs={{0,3},{1,2},{2,1},{3,0},{4,7},{5,6},{6,5},{7,4},{8,11},{9,10},{10,... | collective-permute-start | bytes 110600 | tf_op jit(solution)/shard_map/ppermute | solution.py:38
  26.1 0.5 %collective-permute-start.11 = (f32[72,128]{1,0:T(8,128)S(1)}, f32[72,128]{1,0:T(8,128)S(1)}, u32[]{:S(2)}, u32[]{:S(2)}) collective-permute-start(f32[72,128]{1,0:T(8,128)S(1)} %add.17), channel_id=1, source_target_pairs={{0,1},{1,0},{2,3},{3,2},{4,5},{5,4},{6,7},{7,6},{8,9},{9,8},{10,11... | collective-permute-start | bytes 110600 | tf_op jit(solution)/shard_map/ppermute | solution.py:38
  26.6 0.3 collective-permute-start.9
  26.9 1.4 %collective-permute-done.10 = f32[72,128]{1,0:T(8,128)S(1)} collective-permute-done((f32[72,128]{1,0:T(8,128)S(1)}, f32[72,128]{1,0:T(8,128)S(1)}, u32[]{:S(2)}, u32[]{:S(2)}) %collective-permute-start.10) | collective-permute-done | bytes 36896 | tf_op jit(solution)/shard_map/ppermute | solution.py:38
  28.3 1.8 %collective-permute-done.11 = f32[72,128]{1,0:T(8,128)S(1)} collective-permute-done((f32[72,128]{1,0:T(8,128)S(1)}, f32[72,128]{1,0:T(8,128)S(1)}, u32[]{:S(2)}, u32[]{:S(2)}) %collective-permute-start.11) | collective-permute-done | bytes 36896 | tf_op jit(solution)/shard_map/ppermute | solution.py:38
  30.0 0.5 %collective-permute-done.9 = f32[72,128]{1,0:T(8,128)S(1)} collective-permute-done((f32[72,128]{1,0:T(8,128)S(1)}, f32[72,128]{1,0:T(8,128)S(1)}, u32[]{:S(2)}, u32[]{:S(2)}) %collective-permute-start.9) | collective-permute-done | bytes 36896 | tf_op jit(solution)/shard_map/ppermute | solution.py:38
  30.6 3.4 %collective-permute-start.12 = (f32[72,128]{1,0:T(8,128)S(1)}, f32[72,128]{1,0:T(8,128)S(1)}, u32[]{:S(2)}, u32[]{:S(2)}) collective-permute-start(f32[72,128]{1,0:T(8,128)S(1)} %add_add_fusion.refs_0_), channel_id=1, source_target_pairs={{0,24},{4,28},{8,16},{12,20},{16,8},{20,12},{24,0},{28,4},{1,25},{... | collective-permute-start | bytes 110600 | tf_op jit(solution)/shard_map/ppermute | solution.py:38
  33.9 0.0 collective-permute-start.13
  33.9 1.1 %collective-permute-start.14 = (f32[72,128]{1,0:T(8,128)S(1)}, f32[72,128]{1,0:T(8,128)S(1)}, u32[]{:S(2)}, u32[]{:S(2)}) collective-permute-start(f32[72,128]{1,0:T(8,128)S(1)} %add_add_fusion.refs_0_), channel_id=1, source_target_pairs={{0,8},{4,12},{8,0},{12,4},{16,24},{20,28},{24,16},{28,20},{1,9},{5... | collective-permute-start | bytes 110600 | tf_op jit(solution)/shard_map/ppermute | solution.py:38
  35.0 1.5 %collective-permute-done.12.refs_1_ = f32[72,128]{1,0:T(8,128)S(1)} collective-permute-done((f32[72,128]{1,0:T(8,128)S(1)}, f32[72,128]{1,0:T(8,128)S(1)}, u32[]{:S(2)}, u32[]{:S(2)}) %collective-permute-start.12) | collective-permute-done | bytes 36896 | tf_op jit(solution)/shard_map/ppermute | solution.py:38
  36.5 2.3 %collective-permute-done.13.refs_2_ = f32[72,128]{1,0:T(8,128)S(1)} collective-permute-done((f32[72,128]{1,0:T(8,128)S(1)}, f32[72,128]{1,0:T(8,128)S(1)}, u32[]{:S(2)}, u32[]{:S(2)}) %collective-permute-start.13) | collective-permute-done | bytes 36896 | tf_op jit(solution)/shard_map/ppermute | solution.py:38
  38.8 0.0 collective-permute-done.14.refs_3_
  38.8 0.0 collective-permute-done.8.across_ref
  38.8 4.2 %shard_map.53 = (f32[4,1152]{1,0:T(4,128)S(1)}, f32[1,16]{1,0:T(1,128)}) custom-call(bf16[18,128,128]{2,1,0:T(8,128)(2,1)S(1)} %get-tuple-element.26.centered_ref, bf16[18,128,128]{2,1,0:T(8,128)(2,1)S(1)} %collective-permute-done.8.across_ref, f32[72,128]{1,0:T(8,128)S(1)} %add_add_fusion.refs_0_, f32[72,128]{1,0:T(8,128)S(1)} %collective-permute-done.12.refs_1_, ...), custom_call_target="tpu_custom_call" | custom-call | tf_op jit(solution)/shard_map/pallas_call | solution.py:379
  43.0 1.5 %collective-permute-start.15 = (f32[4,1152]{1,0:T(4,128)S(1)}, f32[4,1152]{1,0:T(4,128)S(1)}, u32[]{:S(2)}, u32[]{:S(2)}) collective-permute-start(f32[4,1152]{1,0:T(4,128)S(1)} %get-tuple-element.28), channel_id=1, source_target_pairs={{0,24},{4,28},{8,16},{12,20},{16,8},{20,12},{24,0},{28,4},{1,25},{... | collective-permute-start | bytes 55304 | tf_op jit(solution)/shard_map/ppermute | solution.py:38
  44.5 0.6 %collective-permute-start.16 = (f32[4,1152]{1,0:T(4,128)S(1)}, f32[4,1152]{1,0:T(4,128)S(1)}, u32[]{:S(2)}, u32[]{:S(2)}) collective-permute-start(f32[4,1152]{1,0:T(4,128)S(1)} %get-tuple-element.28), channel_id=1, source_target_pairs={{0,16},{4,20},{8,24},{12,28},{16,0},{20,4},{24,8},{28,12},{1,17},{... | collective-permute-start | bytes 55304 | tf_op jit(solution)/shard_map/ppermute | solution.py:38
  45.1 2.4 %collective-permute-start.17 = (f32[4,1152]{1,0:T(4,128)S(1)}, f32[4,1152]{1,0:T(4,128)S(1)}, u32[]{:S(2)}, u32[]{:S(2)}) collective-permute-start(f32[4,1152]{1,0:T(4,128)S(1)} %get-tuple-element.28), channel_id=1, source_target_pairs={{0,8},{4,12},{8,0},{12,4},{16,24},{20,28},{24,16},{28,20},{1,9},{5... | collective-permute-start | bytes 55304 | tf_op jit(solution)/shard_map/ppermute | solution.py:38
  47.4 1.2 %collective-permute-done.15 = f32[4,1152]{1,0:T(4,128)S(1)} collective-permute-done((f32[4,1152]{1,0:T(4,128)S(1)}, f32[4,1152]{1,0:T(4,128)S(1)}, u32[]{:S(2)}, u32[]{:S(2)}) %collective-permute-start.15) | collective-permute-done | bytes 18464 | tf_op jit(solution)/shard_map/ppermute | solution.py:38
  48.6 0.6 %collective-permute-done.16 = f32[4,1152]{1,0:T(4,128)S(1)} collective-permute-done((f32[4,1152]{1,0:T(4,128)S(1)}, f32[4,1152]{1,0:T(4,128)S(1)}, u32[]{:S(2)}, u32[]{:S(2)}) %collective-permute-start.16) | collective-permute-done | bytes 18464 | tf_op jit(solution)/shard_map/ppermute | solution.py:38
  49.2 0.2 collective-permute-done.17
  49.4 0.7 %pad_maximum_fusion = f32[16,1152]{1,0:T(8,128)} fusion(f32[4,1152]{1,0:T(4,128)S(1)} %get-tuple-element.31, f32[4,1152]{1,0:T(4,128)S(1)} %get-tuple-element.32, f32[4,1152]{1,0:T(4,128)S(1)} %get-tuple-element.33, f32[4,1152]{1,0:T(4,128)S(1)} %get-tuple-element.30), kind=kLoop, calls=%fused_computation | loop fusion | flops 55296 | bytes 147456 | tf_op jit(solution)/shard_map/concatenate | solution.py:319
  (20 shorter events, 0.3 us)
Async XLA Ops:
  2.8 11.1 %collective-permute-start = (f16[312,128]{1,0:T(8,128)(2,1)S(1)}, f16[312,128]{1,0:T(8,128)(2,1)S(1)}, u32[]{:S(2)}, u32[]{:S(2)}) collective-permute-start(f16[312,128]{1,0:T(8,128)(2,1)S(1)} %convert_element_type.42), channel_id=1, source_target_pairs={{0,16},{4,20},{8,24},{12,28},{16,0},{20,4},{24,8},{28,12},{1,17},{... | collective-permute-start | bytes 239624 | tf_op jit(solution)/shard_map/ppermute | solution.py:38
  6.9 11.0 %collective-permute-start.1 = (f16[312,128]{1,0:T(8,128)(2,1)S(1)}, f16[312,128]{1,0:T(8,128)(2,1)S(1)}, u32[]{:S(2)}, u32[]{:S(2)}) collective-permute-start(f16[312,128]{1,0:T(8,128)(2,1)S(1)} %convert_element_type.44), channel_id=1, source_target_pairs={{0,20},{4,16},{8,28},{12,24},{16,4},{20,0},{24,12},{28,8},{1,21},{... | collective-permute-start | bytes 239624 | tf_op jit(solution)/shard_map/ppermute | solution.py:38
  7.1 11.0 %collective-permute-start.2 = (f16[312,128]{1,0:T(8,128)(2,1)S(1)}, f16[312,128]{1,0:T(8,128)(2,1)S(1)}, u32[]{:S(2)}, u32[]{:S(2)}) collective-permute-start(f16[312,128]{1,0:T(8,128)(2,1)S(1)} %convert_element_type.46), channel_id=1, source_target_pairs={{0,24},{4,28},{8,16},{12,20},{16,8},{20,12},{24,0},{28,4},{1,25},{... | collective-permute-start | bytes 239624 | tf_op jit(solution)/shard_map/ppermute | solution.py:38
  10.2 7.9 %collective-permute-start.3 = (f16[312,128]{1,0:T(8,128)(2,1)S(1)}, f16[312,128]{1,0:T(8,128)(2,1)S(1)}, u32[]{:S(2)}, u32[]{:S(2)}) collective-permute-start(f16[312,128]{1,0:T(8,128)(2,1)S(1)} %convert_element_type.48), channel_id=1, source_target_pairs={{0,28},{4,24},{8,20},{12,16},{16,12},{20,8},{24,4},{28,0},{1,29},{... | collective-permute-start | bytes 239624 | tf_op jit(solution)/shard_map/ppermute | solution.py:38
  13.0 6.6 %collective-permute-start.4 = (f16[312,128]{1,0:T(8,128)(2,1)S(1)}, f16[312,128]{1,0:T(8,128)(2,1)S(1)}, u32[]{:S(2)}, u32[]{:S(2)}) collective-permute-start(f16[312,128]{1,0:T(8,128)(2,1)S(1)} %convert_element_type.50), channel_id=1, source_target_pairs={{0,8},{4,12},{8,0},{12,4},{16,24},{20,28},{24,16},{28,20},{1,9},{5... | collective-permute-start | bytes 239624 | tf_op jit(solution)/shard_map/ppermute | solution.py:38
  13.2 0.7 %copy-start = (f32[16]{0:T(128)S(1)}, f32[16]{0:T(128)}, u32[]{:S(2)}) copy-start(f32[16]{0:T(128)} %param.5) | copy-start | bytes 196
  13.9 7.3 %collective-permute-start.5 = (f16[312,128]{1,0:T(8,128)(2,1)S(1)}, f16[312,128]{1,0:T(8,128)(2,1)S(1)}, u32[]{:S(2)}, u32[]{:S(2)}) collective-permute-start(f16[312,128]{1,0:T(8,128)(2,1)S(1)} %convert_element_type.52), channel_id=1, source_target_pairs={{0,12},{4,8},{8,4},{12,0},{16,28},{20,24},{24,20},{28,16},{1,13},{... | collective-permute-start | bytes 239624 | tf_op jit(solution)/shard_map/ppermute | solution.py:38
  17.9 3.4 %collective-permute-start.6 = (f16[312,128]{1,0:T(8,128)(2,1)S(1)}, f16[312,128]{1,0:T(8,128)(2,1)S(1)}, u32[]{:S(2)}, u32[]{:S(2)}) collective-permute-start(f16[312,128]{1,0:T(8,128)(2,1)S(1)} %convert_element_type.54), channel_id=1, source_target_pairs={{0,4},{4,0},{8,12},{12,8},{16,20},{20,16},{24,28},{28,24},{1,5},{5... | collective-permute-start | bytes 239624 | tf_op jit(solution)/shard_map/ppermute | solution.py:38
  22.0 1.3 %collective-permute-start.7 = (f32[72,128]{1,0:T(8,128)S(1)}, f32[72,128]{1,0:T(8,128)S(1)}, u32[]{:S(2)}, u32[]{:S(2)}) collective-permute-start(f32[72,128]{1,0:T(8,128)S(1)} %get-tuple-element.25), channel_id=1, source_target_pairs={{0,4},{4,0},{8,12},{12,8},{16,20},{20,16},{24,28},{28,24},{1,5},{5... | collective-permute-start | bytes 110600 | tf_op jit(solution)/shard_map/ppermute | solution.py:38
  23.2 15.6 %collective-permute-start.8 = (bf16[18,128,128]{2,1,0:T(8,128)(2,1)S(1)}, bf16[18,128,128]{2,1,0:T(8,128)(2,1)S(1)}, u32[]{:S(2)}, u32[]{:S(2)}) collective-permute-start(bf16[18,128,128]{2,1,0:T(8,128)(2,1)S(1)} %get-tuple-element.26.centered_ref), channel_id=1, source_target_pairs={{0,4},{4,0},{8,12},{12,8},{16,20},{20,16},{24,28},{28,24},{1,5},{5... | collective-permute-start | bytes 1769480 | tf_op jit(solution)/shard_map/ppermute | solution.py:38
  23.4 4.9 %collective-permute-start.10 = (f32[72,128]{1,0:T(8,128)S(1)}, f32[72,128]{1,0:T(8,128)S(1)}, u32[]{:S(2)}, u32[]{:S(2)}) collective-permute-start(f32[72,128]{1,0:T(8,128)S(1)} %add.17), channel_id=1, source_target_pairs={{0,3},{1,2},{2,1},{3,0},{4,7},{5,6},{6,5},{7,4},{8,11},{9,10},{10,... | collective-permute-start | bytes 110600 | tf_op jit(solution)/shard_map/ppermute | solution.py:38
  26.1 4.0 %collective-permute-start.11 = (f32[72,128]{1,0:T(8,128)S(1)}, f32[72,128]{1,0:T(8,128)S(1)}, u32[]{:S(2)}, u32[]{:S(2)}) collective-permute-start(f32[72,128]{1,0:T(8,128)S(1)} %add.17), channel_id=1, source_target_pairs={{0,1},{1,0},{2,3},{3,2},{4,5},{5,4},{6,7},{7,6},{8,9},{9,8},{10,11... | collective-permute-start | bytes 110600 | tf_op jit(solution)/shard_map/ppermute | solution.py:38
  26.6 4.0 %collective-permute-start.9 = (f32[72,128]{1,0:T(8,128)S(1)}, f32[72,128]{1,0:T(8,128)S(1)}, u32[]{:S(2)}, u32[]{:S(2)}) collective-permute-start(f32[72,128]{1,0:T(8,128)S(1)} %add.17), channel_id=1, source_target_pairs={{0,2},{1,3},{2,0},{3,1},{4,6},{5,7},{6,4},{7,5},{8,10},{9,11},{10,... | collective-permute-start | bytes 110600 | tf_op jit(solution)/shard_map/ppermute | solution.py:38
  30.6 5.9 %collective-permute-start.12 = (f32[72,128]{1,0:T(8,128)S(1)}, f32[72,128]{1,0:T(8,128)S(1)}, u32[]{:S(2)}, u32[]{:S(2)}) collective-permute-start(f32[72,128]{1,0:T(8,128)S(1)} %add_add_fusion.refs_0_), channel_id=1, source_target_pairs={{0,24},{4,28},{8,16},{12,20},{16,8},{20,12},{24,0},{28,4},{1,25},{... | collective-permute-start | bytes 110600 | tf_op jit(solution)/shard_map/ppermute | solution.py:38
  33.9 4.9 %collective-permute-start.13 = (f32[72,128]{1,0:T(8,128)S(1)}, f32[72,128]{1,0:T(8,128)S(1)}, u32[]{:S(2)}, u32[]{:S(2)}) collective-permute-start(f32[72,128]{1,0:T(8,128)S(1)} %add_add_fusion.refs_0_), channel_id=1, source_target_pairs={{0,16},{4,20},{8,24},{12,28},{16,0},{20,4},{24,8},{28,12},{1,17},{... | collective-permute-start | bytes 110600 | tf_op jit(solution)/shard_map/ppermute | solution.py:38
  33.9 4.9 %collective-permute-start.14 = (f32[72,128]{1,0:T(8,128)S(1)}, f32[72,128]{1,0:T(8,128)S(1)}, u32[]{:S(2)}, u32[]{:S(2)}) collective-permute-start(f32[72,128]{1,0:T(8,128)S(1)} %add_add_fusion.refs_0_), channel_id=1, source_target_pairs={{0,8},{4,12},{8,0},{12,4},{16,24},{20,28},{24,16},{28,20},{1,9},{5... | collective-permute-start | bytes 110600 | tf_op jit(solution)/shard_map/ppermute | solution.py:38
  43.0 5.6 %collective-permute-start.15 = (f32[4,1152]{1,0:T(4,128)S(1)}, f32[4,1152]{1,0:T(4,128)S(1)}, u32[]{:S(2)}, u32[]{:S(2)}) collective-permute-start(f32[4,1152]{1,0:T(4,128)S(1)} %get-tuple-element.28), channel_id=1, source_target_pairs={{0,24},{4,28},{8,16},{12,20},{16,8},{20,12},{24,0},{28,4},{1,25},{... | collective-permute-start | bytes 55304 | tf_op jit(solution)/shard_map/ppermute | solution.py:38
  44.5 4.7 %collective-permute-start.16 = (f32[4,1152]{1,0:T(4,128)S(1)}, f32[4,1152]{1,0:T(4,128)S(1)}, u32[]{:S(2)}, u32[]{:S(2)}) collective-permute-start(f32[4,1152]{1,0:T(4,128)S(1)} %get-tuple-element.28), channel_id=1, source_target_pairs={{0,16},{4,20},{8,24},{12,28},{16,0},{20,4},{24,8},{28,12},{1,17},{... | collective-permute-start | bytes 55304 | tf_op jit(solution)/shard_map/ppermute | solution.py:38
  45.1 4.3 %collective-permute-start.17 = (f32[4,1152]{1,0:T(4,128)S(1)}, f32[4,1152]{1,0:T(4,128)S(1)}, u32[]{:S(2)}, u32[]{:S(2)}) collective-permute-start(f32[4,1152]{1,0:T(4,128)S(1)} %get-tuple-element.28), channel_id=1, source_target_pairs={{0,8},{4,12},{8,0},{12,4},{16,24},{20,28},{24,16},{28,20},{1,9},{5... | collective-permute-start | bytes 55304 | tf_op jit(solution)/shard_map/ppermute | solution.py:38

commit v7 on v6

--- a/solution.py
+++ b/solution.py
@@ -215,11 +215,18 @@
     return panel
 
 
-def invert(matrix):
+def as_column(values, rows, first):
+    row = lax.broadcasted_iota(jnp.int32, (rows, values.shape[1]), 0)
+    lane = lax.broadcasted_iota(jnp.int32, (rows, values.shape[1]), 1)
+    return jnp.sum(jnp.where(lane == row + first, values, 0.0), axis=1, keepdims=True)
+
+
+def solve_symmetric(matrix, right):
     matrix = list(matrix)
     count, size = len(matrix), WIDTH * len(matrix)
     row = lax.broadcasted_iota(jnp.int32, (WIDTH, size), 0)
     lane = lax.broadcasted_iota(jnp.int32, (WIDTH, size), 1)
+    columns = [as_column(right, WIDTH, WIDTH * index) for index in range(count)]
     pivot = matrix[0]
     for index in range(count):
         first = WIDTH * index
@@ -227,13 +234,15 @@
         unit = jnp.where(lane == row + first, 1.0, 0.0)
         solved = eliminate([spread_lane(pivot, first + c) for c in range(WIDTH)], jnp.where(inside, unit, pivot), row)
         solved = jnp.where(inside, -solved, solved)
-        update = outer_sum(jnp.where(inside, 0.0, pivot), solved)
-        following = None
-        if index + 1 < count:
-            terms = [spread_lane(matrix[index + 1], first + c) * solved[c : c + 1] for c in range(WIDTH)]
-            following = jnp.where(inside, 0.0, matrix[index + 1])
-            for term in terms:
-                following = following - term
+        held = jnp.where(inside, 0.0, pivot)
+        if index + 1 == count:
+            weights = columns[index] - jnp.sum(held * right, axis=1, keepdims=True)
+            terms = [jnp.where(inside, 0.0, matrix[other]) * columns[other] for other in range(index)]
+            return -jnp.sum(sum(terms) + solved * weights, axis=0, keepdims=True)
+        update = outer_sum(held, solved)
+        following = jnp.where(inside, 0.0, matrix[index + 1])
+        for c in range(WIDTH):
+            following = following - spread_lane(matrix[index + 1], first + c) * solved[c : c + 1]
         for other in range(count):
             if other == index:
                 matrix[other] = solved
@@ -242,7 +251,6 @@
             else:
                 matrix[other] = jnp.where(inside, 0.0, matrix[other]) - update[WIDTH * other : WIDTH * (other + 1)]
         pivot = following
-    return matrix
 
 
 def arrange(terms):
@@ -279,7 +287,7 @@
     ]
     energies = summed[total // 2 + 1 : total // 2 + 2]
     deviation = energies - jnp.sum(energies, axis=1, keepdims=True) / total
-    coeffs = jnp.concatenate([-jnp.sum(part * deviation, axis=1, keepdims=True) for part in invert(regular)], axis=0)
+    coeffs = as_column(solve_symmetric(regular, deviation), total, 0)
 
     position = lax.axis_index("samp")
     sample = lax.broadcasted_iota(jnp.int32, (total, lanes), 0)

time: 50.2 us -> 50 us (level)
  no operation moved by 1% of the time
where the time goes in v7:
time: 50 us; the launch traced here: 49.8 us
  starting transfers between devices  23.2 us (46%)
  waiting for transfers between devices  15.1 us (30%)
  Pallas kernels  9 us (18%)
  other arithmetic  0.98 us (2%)
  between operations  0.83 us (2%)
  local copies, waits for them, and re-layouts  0.73 us (1%)
    ppermute x18, starting transfers between devices, swap(): return lax.ppermute(x, axis, [(i, i ^ mask) for i in range(count)])  23.2 us
    ppermute x18, waiting for transfers between devices, swap(): return lax.ppermute(x, axis, [(i, i ^ mask) for i in range(count)])  15.1 us
    pallas_call x2, Pallas kernels, half(): kernel_call(functools.partial(grads_body, far), out_shape, [pltpu.VMEM(ac...  4.31 us
    pallas_call x1, Pallas kernels, local_split(): kernel_call(functools.partial(solve_body, -math.sqrt(params_all / total))...  4.03 us
  transfers between devices with their start and end apart: 18, of which 12 were waited for; matrix products, arithmetic and copies ran while one was open for 1% of the time, Pallas kernels for 4%

profile of v7, /device:TPU:0, one launch (start us, length us, event | category | flops | bytes accessed | tf_op | source)
XLA Modules:
  0.0 49.8 jit_solution(10157571383001578629)
XLA Ops:
  0.6 2.2 %shard_map.51 = (f32[312,128]{1,0:T(8,128)S(1)}, f32[312,128]{1,0:T(8,128)S(1)}, f32[312,128]{1,0:T(8,128)S(1)}, f32[312,128]{1,0:T(8,128)S(1)}) custom-call(bf16[16,2,64,256]{3,2,1,0:T(8,128)(2,1)} %acts_hbm.3, bf16[16,2,16,256]{3,2,1,0:T(8,128)(2,1)} %cots_hbm.3), custom_call_target="tpu_custom_call" | custom-call | tf_op jit(solution)/shard_map/pallas_call | solution.py:353
  2.8 4.1 %collective-permute-start = (f16[312,128]{1,0:T(8,128)(2,1)S(1)}, f16[312,128]{1,0:T(8,128)(2,1)S(1)}, u32[]{:S(2)}, u32[]{:S(2)}) collective-permute-start(f16[312,128]{1,0:T(8,128)(2,1)S(1)} %convert_element_type.42), channel_id=1, source_target_pairs={{0,16},{4,20},{8,24},{12,28},{16,0},{20,4},{24,8},{28,12},{1,17},{... | collective-permute-start | bytes 239624 | tf_op jit(solution)/shard_map/ppermute | solution.py:38
  6.9 0.1 collective-permute-start.1
  7.1 3.1 %collective-permute-start.2 = (f16[312,128]{1,0:T(8,128)(2,1)S(1)}, f16[312,128]{1,0:T(8,128)(2,1)S(1)}, u32[]{:S(2)}, u32[]{:S(2)}) collective-permute-start(f16[312,128]{1,0:T(8,128)(2,1)S(1)} %convert_element_type.46), channel_id=1, source_target_pairs={{0,24},{4,28},{8,16},{12,20},{16,8},{20,12},{24,0},{28,4},{1,25},{... | collective-permute-start | bytes 239624 | tf_op jit(solution)/shard_map/ppermute | solution.py:38
  10.2 0.6 %collective-permute-start.3 = (f16[312,128]{1,0:T(8,128)(2,1)S(1)}, f16[312,128]{1,0:T(8,128)(2,1)S(1)}, u32[]{:S(2)}, u32[]{:S(2)}) collective-permute-start(f16[312,128]{1,0:T(8,128)(2,1)S(1)} %convert_element_type.48), channel_id=1, source_target_pairs={{0,28},{4,24},{8,20},{12,16},{16,12},{20,8},{24,4},{28,0},{1,29},{... | collective-permute-start | bytes 239624 | tf_op jit(solution)/shard_map/ppermute | solution.py:38
  10.9 2.1 %shard_map.50 = (f32[18,16,128]{2,1,0:T(8,128)S(1)}, f32[312,128]{1,0:T(8,128)S(1)}, f32[312,128]{1,0:T(8,128)S(1)}, f32[312,128]{1,0:T(8,128)S(1)}) custom-call(bf16[16,2,64,256]{3,2,1,0:T(8,128)(2,1)} %acts_hbm.3, bf16[16,2,16,256]{3,2,1,0:T(8,128)(2,1)} %cots_hbm.3), custom_call_target="tpu_custom_call" | custom-call | tf_op jit(solution)/shard_map/pallas_call | solution.py:353
  13.0 0.1 collective-permute-start.4
  13.2 0.0 copy-start
  13.2 0.6 %copy-done = f32[16]{0:T(128)S(1)} copy-done((f32[16]{0:T(128)S(1)}, f32[16]{0:T(128)}, u32[]{:S(2)}) %copy-start) | copy-done | bytes 88
  13.8 0.1 tile.10
  13.9 0.0 collective-permute-done
  13.9 2.4 %collective-permute-start.5 = (f16[312,128]{1,0:T(8,128)(2,1)S(1)}, f16[312,128]{1,0:T(8,128)(2,1)S(1)}, u32[]{:S(2)}, u32[]{:S(2)}) collective-permute-start(f16[312,128]{1,0:T(8,128)(2,1)S(1)} %convert_element_type.52), channel_id=1, source_target_pairs={{0,12},{4,8},{8,4},{12,0},{16,28},{20,24},{24,20},{28,16},{1,13},{... | collective-permute-start | bytes 239624 | tf_op jit(solution)/shard_map/ppermute | solution.py:38
  16.4 1.5 %collective-permute-done.1 = f16[312,128]{1,0:T(8,128)(2,1)S(1)} collective-permute-done((f16[312,128]{1,0:T(8,128)(2,1)S(1)}, f16[312,128]{1,0:T(8,128)(2,1)S(1)}, u32[]{:S(2)}, u32[]{:S(2)}) %collective-permute-start.1) | collective-permute-done | bytes 79904 | tf_op jit(solution)/shard_map/ppermute | solution.py:38
  17.9 0.1 collective-permute-start.6
  18.0 0.1 broadcast_select_fusion.energies_ref
  18.1 0.0 collective-permute-done.2
  18.1 0.0 collective-permute-done.3
  18.1 1.5 %collective-permute-done.4 = f16[312,128]{1,0:T(8,128)(2,1)S(1)} collective-permute-done((f16[312,128]{1,0:T(8,128)(2,1)S(1)}, f16[312,128]{1,0:T(8,128)(2,1)S(1)}, u32[]{:S(2)}, u32[]{:S(2)}) %collective-permute-start.4) | collective-permute-done | bytes 79904 | tf_op jit(solution)/shard_map/ppermute | solution.py:38
  19.7 1.6 %collective-permute-done.5 = f16[312,128]{1,0:T(8,128)(2,1)S(1)} collective-permute-done((f16[312,128]{1,0:T(8,128)(2,1)S(1)}, f16[312,128]{1,0:T(8,128)(2,1)S(1)}, u32[]{:S(2)}, u32[]{:S(2)}) %collective-permute-start.5) | collective-permute-done | bytes 79904 | tf_op jit(solution)/shard_map/ppermute | solution.py:38
  21.3 0.0 collective-permute-done.6
  21.3 0.7 %shard_map.52 = (bf16[18,128,128]{2,1,0:T(8,128)(2,1)S(1)}, f32[72,128]{1,0:T(8,128)S(1)}) custom-call(f32[8,128]{1,0:T(8,128)S(1)} %broadcast_select_fusion.energies_ref, f32[18,16,128]{2,1,0:T(8,128)S(1)} %get-tuple-element.16.own_ref, f32[312,128]{1,0:T(8,128)S(1)} %convert_element_type.43.refs_0_, f32[312,128]{1,0:T(8,128)S(1)} %convert_element_type.45.refs_1_, ...), custom_call_target="tpu_custom_call" | custom-call | tf_op jit(solution)/shard_map/pallas_call | solution.py:376
  22.0 0.2 collective-permute-start.7
  22.1 1.1 %collective-permute-done.7 = f32[72,128]{1,0:T(8,128)S(1)} collective-permute-done((f32[72,128]{1,0:T(8,128)S(1)}, f32[72,128]{1,0:T(8,128)S(1)}, u32[]{:S(2)}, u32[]{:S(2)}) %collective-permute-start.7) | collective-permute-done | bytes 36896 | tf_op jit(solution)/shard_map/ppermute | solution.py:38
  23.2 0.2 collective-permute-start.8
  23.4 2.7 %collective-permute-start.10 = (f32[72,128]{1,0:T(8,128)S(1)}, f32[72,128]{1,0:T(8,128)S(1)}, u32[]{:S(2)}, u32[]{:S(2)}) collective-permute-start(f32[72,128]{1,0:T(8,128)S(1)} %add.17), channel_id=1, source_target_pairs={{0,3},{1,2},{2,1},{3,0},{4,7},{5,6},{6,5},{7,4},{8,11},{9,10},{10,... | collective-permute-start | bytes 110600 | tf_op jit(solution)/shard_map/ppermute | solution.py:38
  26.1 0.5 %collective-permute-start.11 = (f32[72,128]{1,0:T(8,128)S(1)}, f32[72,128]{1,0:T(8,128)S(1)}, u32[]{:S(2)}, u32[]{:S(2)}) collective-permute-start(f32[72,128]{1,0:T(8,128)S(1)} %add.17), channel_id=1, source_target_pairs={{0,1},{1,0},{2,3},{3,2},{4,5},{5,4},{6,7},{7,6},{8,9},{9,8},{10,11... | collective-permute-start | bytes 110600 | tf_op jit(solution)/shard_map/ppermute | solution.py:38
  26.6 0.3 collective-permute-start.9
  26.9 1.4 %collective-permute-done.10 = f32[72,128]{1,0:T(8,128)S(1)} collective-permute-done((f32[72,128]{1,0:T(8,128)S(1)}, f32[72,128]{1,0:T(8,128)S(1)}, u32[]{:S(2)}, u32[]{:S(2)}) %collective-permute-start.10) | collective-permute-done | bytes 36896 | tf_op jit(solution)/shard_map/ppermute | solution.py:38
  28.3 1.8 %collective-permute-done.11 = f32[72,128]{1,0:T(8,128)S(1)} collective-permute-done((f32[72,128]{1,0:T(8,128)S(1)}, f32[72,128]{1,0:T(8,128)S(1)}, u32[]{:S(2)}, u32[]{:S(2)}) %collective-permute-start.11) | collective-permute-done | bytes 36896 | tf_op jit(solution)/shard_map/ppermute | solution.py:38
  30.0 0.5 %collective-permute-done.9 = f32[72,128]{1,0:T(8,128)S(1)} collective-permute-done((f32[72,128]{1,0:T(8,128)S(1)}, f32[72,128]{1,0:T(8,128)S(1)}, u32[]{:S(2)}, u32[]{:S(2)}) %collective-permute-start.9) | collective-permute-done | bytes 36896 | tf_op jit(solution)/shard_map/ppermute | solution.py:38
  30.6 3.4 %collective-permute-start.12 = (f32[72,128]{1,0:T(8,128)S(1)}, f32[72,128]{1,0:T(8,128)S(1)}, u32[]{:S(2)}, u32[]{:S(2)}) collective-permute-start(f32[72,128]{1,0:T(8,128)S(1)} %add_add_fusion.refs_0_), channel_id=1, source_target_pairs={{0,24},{4,28},{8,16},{12,20},{16,8},{20,12},{24,0},{28,4},{1,25},{... | collective-permute-start | bytes 110600 | tf_op jit(solution)/shard_map/ppermute | solution.py:38
  33.9 0.0 collective-permute-start.13
  33.9 1.1 %collective-permute-start.14 = (f32[72,128]{1,0:T(8,128)S(1)}, f32[72,128]{1,0:T(8,128)S(1)}, u32[]{:S(2)}, u32[]{:S(2)}) collective-permute-start(f32[72,128]{1,0:T(8,128)S(1)} %add_add_fusion.refs_0_), channel_id=1, source_target_pairs={{0,8},{4,12},{8,0},{12,4},{16,24},{20,28},{24,16},{28,20},{1,9},{5... | collective-permute-start | bytes 110600 | tf_op jit(solution)/shard_map/ppermute | solution.py:38
  35.0 1.5 %collective-permute-done.12.refs_1_ = f32[72,128]{1,0:T(8,128)S(1)} collective-permute-done((f32[72,128]{1,0:T(8,128)S(1)}, f32[72,128]{1,0:T(8,128)S(1)}, u32[]{:S(2)}, u32[]{:S(2)}) %collective-permute-start.12) | collective-permute-done | bytes 36896 | tf_op jit(solution)/shard_map/ppermute | solution.py:38
  36.5 2.3 %collective-permute-done.13.refs_2_ = f32[72,128]{1,0:T(8,128)S(1)} collective-permute-done((f32[72,128]{1,0:T(8,128)S(1)}, f32[72,128]{1,0:T(8,128)S(1)}, u32[]{:S(2)}, u32[]{:S(2)}) %collective-permute-start.13) | collective-permute-done | bytes 36896 | tf_op jit(solution)/shard_map/ppermute | solution.py:38
  38.8 0.0 collective-permute-done.14.refs_3_
  38.8 0.0 collective-permute-done.8.across_ref
  38.8 4.0 %shard_map.53 = (f32[4,1152]{1,0:T(4,128)S(1)}, f32[1,16]{1,0:T(1,128)}) custom-call(bf16[18,128,128]{2,1,0:T(8,128)(2,1)S(1)} %get-tuple-element.26.centered_ref, bf16[18,128,128]{2,1,0:T(8,128)(2,1)S(1)} %collective-permute-done.8.across_ref, f32[72,128]{1,0:T(8,128)S(1)} %add_add_fusion.refs_0_, f32[72,128]{1,0:T(8,128)S(1)} %collective-permute-done.12.refs_1_, ...), custom_call_target="tpu_custom_call" | custom-call | tf_op jit(solution)/shard_map/pallas_call | solution.py:387
  42.8 1.5 %collective-permute-start.15 = (f32[4,1152]{1,0:T(4,128)S(1)}, f32[4,1152]{1,0:T(4,128)S(1)}, u32[]{:S(2)}, u32[]{:S(2)}) collective-permute-start(f32[4,1152]{1,0:T(4,128)S(1)} %get-tuple-element.28), channel_id=1, source_target_pairs={{0,24},{4,28},{8,16},{12,20},{16,8},{20,12},{24,0},{28,4},{1,25},{... | collective-permute-start | bytes 55304 | tf_op jit(solution)/shard_map/ppermute | solution.py:38
  44.3 0.6 %collective-permute-start.16 = (f32[4,1152]{1,0:T(4,128)S(1)}, f32[4,1152]{1,0:T(4,128)S(1)}, u32[]{:S(2)}, u32[]{:S(2)}) collective-permute-start(f32[4,1152]{1,0:T(4,128)S(1)} %get-tuple-element.28), channel_id=1, source_target_pairs={{0,16},{4,20},{8,24},{12,28},{16,0},{20,4},{24,8},{28,12},{1,17},{... | collective-permute-start | bytes 55304 | tf_op jit(solution)/shard_map/ppermute | solution.py:38
  44.9 2.4 %collective-permute-start.17 = (f32[4,1152]{1,0:T(4,128)S(1)}, f32[4,1152]{1,0:T(4,128)S(1)}, u32[]{:S(2)}, u32[]{:S(2)}) collective-permute-start(f32[4,1152]{1,0:T(4,128)S(1)} %get-tuple-element.28), channel_id=1, source_target_pairs={{0,8},{4,12},{8,0},{12,4},{16,24},{20,28},{24,16},{28,20},{1,9},{5... | collective-permute-start | bytes 55304 | tf_op jit(solution)/shard_map/ppermute | solution.py:38
  47.2 1.2 %collective-permute-done.15 = f32[4,1152]{1,0:T(4,128)S(1)} collective-permute-done((f32[4,1152]{1,0:T(4,128)S(1)}, f32[4,1152]{1,0:T(4,128)S(1)}, u32[]{:S(2)}, u32[]{:S(2)}) %collective-permute-start.15) | collective-permute-done | bytes 18464 | tf_op jit(solution)/shard_map/ppermute | solution.py:38
  48.4 0.6 %collective-permute-done.16 = f32[4,1152]{1,0:T(4,128)S(1)} collective-permute-done((f32[4,1152]{1,0:T(4,128)S(1)}, f32[4,1152]{1,0:T(4,128)S(1)}, u32[]{:S(2)}, u32[]{:S(2)}) %collective-permute-start.16) | collective-permute-done | bytes 18464 | tf_op jit(solution)/shard_map/ppermute | solution.py:38
  49.0 0.2 collective-permute-done.17
  49.2 0.7 %pad_maximum_fusion = f32[16,1152]{1,0:T(8,128)} fusion(f32[4,1152]{1,0:T(4,128)S(1)} %get-tuple-element.31, f32[4,1152]{1,0:T(4,128)S(1)} %get-tuple-element.32, f32[4,1152]{1,0:T(4,128)S(1)} %get-tuple-element.33, f32[4,1152]{1,0:T(4,128)S(1)} %get-tuple-element.30), kind=kLoop, calls=%fused_computation | loop fusion | flops 55296 | bytes 147456 | tf_op jit(solution)/shard_map/concatenate | solution.py:327
  (20 shorter events, 0.3 us)
Async XLA Ops:
  2.8 11.1 %collective-permute-start = (f16[312,128]{1,0:T(8,128)(2,1)S(1)}, f16[312,128]{1,0:T(8,128)(2,1)S(1)}, u32[]{:S(2)}, u32[]{:S(2)}) collective-permute-start(f16[312,128]{1,0:T(8,128)(2,1)S(1)} %convert_element_type.42), channel_id=1, source_target_pairs={{0,16},{4,20},{8,24},{12,28},{16,0},{20,4},{24,8},{28,12},{1,17},{... | collective-permute-start | bytes 239624 | tf_op jit(solution)/shard_map/ppermute | solution.py:38
  6.9 11.0 %collective-permute-start.1 = (f16[312,128]{1,0:T(8,128)(2,1)S(1)}, f16[312,128]{1,0:T(8,128)(2,1)S(1)}, u32[]{:S(2)}, u32[]{:S(2)}) collective-permute-start(f16[312,128]{1,0:T(8,128)(2,1)S(1)} %convert_element_type.44), channel_id=1, source_target_pairs={{0,20},{4,16},{8,28},{12,24},{16,4},{20,0},{24,12},{28,8},{1,21},{... | collective-permute-start | bytes 239624 | tf_op jit(solution)/shard_map/ppermute | solution.py:38
  7.1 11.0 %collective-permute-start.2 = (f16[312,128]{1,0:T(8,128)(2,1)S(1)}, f16[312,128]{1,0:T(8,128)(2,1)S(1)}, u32[]{:S(2)}, u32[]{:S(2)}) collective-permute-start(f16[312,128]{1,0:T(8,128)(2,1)S(1)} %convert_element_type.46), channel_id=1, source_target_pairs={{0,24},{4,28},{8,16},{12,20},{16,8},{20,12},{24,0},{28,4},{1,25},{... | collective-permute-start | bytes 239624 | tf_op jit(solution)/shard_map/ppermute | solution.py:38
  10.2 7.9 %collective-permute-start.3 = (f16[312,128]{1,0:T(8,128)(2,1)S(1)}, f16[312,128]{1,0:T(8,128)(2,1)S(1)}, u32[]{:S(2)}, u32[]{:S(2)}) collective-permute-start(f16[312,128]{1,0:T(8,128)(2,1)S(1)} %convert_element_type.48), channel_id=1, source_target_pairs={{0,28},{4,24},{8,20},{12,16},{16,12},{20,8},{24,4},{28,0},{1,29},{... | collective-permute-start | bytes 239624 | tf_op jit(solution)/shard_map/ppermute | solution.py:38
  13.0 6.6 %collective-permute-start.4 = (f16[312,128]{1,0:T(8,128)(2,1)S(1)}, f16[312,128]{1,0:T(8,128)(2,1)S(1)}, u32[]{:S(2)}, u32[]{:S(2)}) collective-permute-start(f16[312,128]{1,0:T(8,128)(2,1)S(1)} %convert_element_type.50), channel_id=1, source_target_pairs={{0,8},{4,12},{8,0},{12,4},{16,24},{20,28},{24,16},{28,20},{1,9},{5... | collective-permute-start | bytes 239624 | tf_op jit(solution)/shard_map/ppermute | solution.py:38
  13.2 0.7 %copy-start = (f32[16]{0:T(128)S(1)}, f32[16]{0:T(128)}, u32[]{:S(2)}) copy-start(f32[16]{0:T(128)} %param.5) | copy-start | bytes 196
  13.9 7.3 %collective-permute-start.5 = (f16[312,128]{1,0:T(8,128)(2,1)S(1)}, f16[312,128]{1,0:T(8,128)(2,1)S(1)}, u32[]{:S(2)}, u32[]{:S(2)}) collective-permute-start(f16[312,128]{1,0:T(8,128)(2,1)S(1)} %convert_element_type.52), channel_id=1, source_target_pairs={{0,12},{4,8},{8,4},{12,0},{16,28},{20,24},{24,20},{28,16},{1,13},{... | collective-permute-start | bytes 239624 | tf_op jit(solution)/shard_map/ppermute | solution.py:38
  17.9 3.4 %collective-permute-start.6 = (f16[312,128]{1,0:T(8,128)(2,1)S(1)}, f16[312,128]{1,0:T(8,128)(2,1)S(1)}, u32[]{:S(2)}, u32[]{:S(2)}) collective-permute-start(f16[312,128]{1,0:T(8,128)(2,1)S(1)} %convert_element_type.54), channel_id=1, source_target_pairs={{0,4},{4,0},{8,12},{12,8},{16,20},{20,16},{24,28},{28,24},{1,5},{5... | collective-permute-start | bytes 239624 | tf_op jit(solution)/shard_map/ppermute | solution.py:38
  22.0 1.3 %collective-permute-start.7 = (f32[72,128]{1,0:T(8,128)S(1)}, f32[72,128]{1,0:T(8,128)S(1)}, u32[]{:S(2)}, u32[]{:S(2)}) collective-permute-start(f32[72,128]{1,0:T(8,128)S(1)} %get-tuple-element.25), channel_id=1, source_target_pairs={{0,4},{4,0},{8,12},{12,8},{16,20},{20,16},{24,28},{28,24},{1,5},{5... | collective-permute-start | bytes 110600 | tf_op jit(solution)/shard_map/ppermute | solution.py:38
  23.2 15.6 %collective-permute-start.8 = (bf16[18,128,128]{2,1,0:T(8,128)(2,1)S(1)}, bf16[18,128,128]{2,1,0:T(8,128)(2,1)S(1)}, u32[]{:S(2)}, u32[]{:S(2)}) collective-permute-start(bf16[18,128,128]{2,1,0:T(8,128)(2,1)S(1)} %get-tuple-element.26.centered_ref), channel_id=1, source_target_pairs={{0,4},{4,0},{8,12},{12,8},{16,20},{20,16},{24,28},{28,24},{1,5},{5... | collective-permute-start | bytes 1769480 | tf_op jit(solution)/shard_map/ppermute | solution.py:38
  23.4 4.9 %collective-permute-start.10 = (f32[72,128]{1,0:T(8,128)S(1)}, f32[72,128]{1,0:T(8,128)S(1)}, u32[]{:S(2)}, u32[]{:S(2)}) collective-permute-start(f32[72,128]{1,0:T(8,128)S(1)} %add.17), channel_id=1, source_target_pairs={{0,3},{1,2},{2,1},{3,0},{4,7},{5,6},{6,5},{7,4},{8,11},{9,10},{10,... | collective-permute-start | bytes 110600 | tf_op jit(solution)/shard_map/ppermute | solution.py:38
  26.1 4.0 %collective-permute-start.11 = (f32[72,128]{1,0:T(8,128)S(1)}, f32[72,128]{1,0:T(8,128)S(1)}, u32[]{:S(2)}, u32[]{:S(2)}) collective-permute-start(f32[72,128]{1,0:T(8,128)S(1)} %add.17), channel_id=1, source_target_pairs={{0,1},{1,0},{2,3},{3,2},{4,5},{5,4},{6,7},{7,6},{8,9},{9,8},{10,11... | collective-permute-start | bytes 110600 | tf_op jit(solution)/shard_map/ppermute | solution.py:38
  26.6 4.0 %collective-permute-start.9 = (f32[72,128]{1,0:T(8,128)S(1)}, f32[72,128]{1,0:T(8,128)S(1)}, u32[]{:S(2)}, u32[]{:S(2)}) collective-permute-start(f32[72,128]{1,0:T(8,128)S(1)} %add.17), channel_id=1, source_target_pairs={{0,2},{1,3},{2,0},{3,1},{4,6},{5,7},{6,4},{7,5},{8,10},{9,11},{10,... | collective-permute-start | bytes 110600 | tf_op jit(solution)/shard_map/ppermute | solution.py:38
  30.6 5.9 %collective-permute-start.12 = (f32[72,128]{1,0:T(8,128)S(1)}, f32[72,128]{1,0:T(8,128)S(1)}, u32[]{:S(2)}, u32[]{:S(2)}) collective-permute-start(f32[72,128]{1,0:T(8,128)S(1)} %add_add_fusion.refs_0_), channel_id=1, source_target_pairs={{0,24},{4,28},{8,16},{12,20},{16,8},{20,12},{24,0},{28,4},{1,25},{... | collective-permute-start | bytes 110600 | tf_op jit(solution)/shard_map/ppermute | solution.py:38
  33.9 4.9 %collective-permute-start.13 = (f32[72,128]{1,0:T(8,128)S(1)}, f32[72,128]{1,0:T(8,128)S(1)}, u32[]{:S(2)}, u32[]{:S(2)}) collective-permute-start(f32[72,128]{1,0:T(8,128)S(1)} %add_add_fusion.refs_0_), channel_id=1, source_target_pairs={{0,16},{4,20},{8,24},{12,28},{16,0},{20,4},{24,8},{28,12},{1,17},{... | collective-permute-start | bytes 110600 | tf_op jit(solution)/shard_map/ppermute | solution.py:38
  33.9 4.9 %collective-permute-start.14 = (f32[72,128]{1,0:T(8,128)S(1)}, f32[72,128]{1,0:T(8,128)S(1)}, u32[]{:S(2)}, u32[]{:S(2)}) collective-permute-start(f32[72,128]{1,0:T(8,128)S(1)} %add_add_fusion.refs_0_), channel_id=1, source_target_pairs={{0,8},{4,12},{8,0},{12,4},{16,24},{20,28},{24,16},{28,20},{1,9},{5... | collective-permute-start | bytes 110600 | tf_op jit(solution)/shard_map/ppermute | solution.py:38
  42.8 5.6 %collective-permute-start.15 = (f32[4,1152]{1,0:T(4,128)S(1)}, f32[4,1152]{1,0:T(4,128)S(1)}, u32[]{:S(2)}, u32[]{:S(2)}) collective-permute-start(f32[4,1152]{1,0:T(4,128)S(1)} %get-tuple-element.28), channel_id=1, source_target_pairs={{0,24},{4,28},{8,16},{12,20},{16,8},{20,12},{24,0},{28,4},{1,25},{... | collective-permute-start | bytes 55304 | tf_op jit(solution)/shard_map/ppermute | solution.py:38
  44.3 4.7 %collective-permute-start.16 = (f32[4,1152]{1,0:T(4,128)S(1)}, f32[4,1152]{1,0:T(4,128)S(1)}, u32[]{:S(2)}, u32[]{:S(2)}) collective-permute-start(f32[4,1152]{1,0:T(4,128)S(1)} %get-tuple-element.28), channel_id=1, source_target_pairs={{0,16},{4,20},{8,24},{12,28},{16,0},{20,4},{24,8},{28,12},{1,17},{... | collective-permute-start | bytes 55304 | tf_op jit(solution)/shard_map/ppermute | solution.py:38
  44.9 4.3 %collective-permute-start.17 = (f32[4,1152]{1,0:T(4,128)S(1)}, f32[4,1152]{1,0:T(4,128)S(1)}, u32[]{:S(2)}, u32[]{:S(2)}) collective-permute-start(f32[4,1152]{1,0:T(4,128)S(1)} %get-tuple-element.28), channel_id=1, source_target_pairs={{0,8},{4,12},{8,0},{12,4},{16,24},{20,28},{24,16},{28,20},{1,9},{5... | collective-permute-start | bytes 55304 | tf_op jit(solution)/shard_map/ppermute | solution.py:38

commit v8 on v7

--- a/solution.py
+++ b/solution.py
@@ -287,12 +287,12 @@
     ]
     energies = summed[total // 2 + 1 : total // 2 + 2]
     deviation = energies - jnp.sum(energies, axis=1, keepdims=True) / total
-    coeffs = as_column(solve_symmetric(regular, deviation), total, 0)
+    coeffs = solve_symmetric(regular, deviation)
 
     position = lax.axis_index("samp")
     sample = lax.broadcasted_iota(jnp.int32, (total, lanes), 0)
     lane = lax.broadcasted_iota(jnp.int32, (total, lanes), 1)
-    spread = jnp.broadcast_to(coeffs, (total, lanes))
+    spread = jnp.broadcast_to(coeffs, (lanes, total)).T
     own = jnp.sum(jnp.where(sample == lane + position * samples, spread, 0.0), axis=0, keepdims=True)
     coeffs_ref[...] = own[:, :samples]
 

time: 50 us -> 49.9 us (level)
  no operation moved by 1% of the time
where the time goes in v8:
time: 49.9 us; the launch traced here: 49.8 us
  starting transfers between devices  23.2 us (46%)
  waiting for transfers between devices  15.1 us (30%)
  Pallas kernels  8.95 us (18%)
  other arithmetic  0.98 us (2%)
  between operations  0.83 us (2%)
  local copies, waits for them, and re-layouts  0.73 us (1%)
    ppermute x18, starting transfers between devices, swap(): return lax.ppermute(x, axis, [(i, i ^ mask) for i in range(count)])  23.2 us
    ppermute x18, waiting for transfers between devices, swap(): return lax.ppermute(x, axis, [(i, i ^ mask) for i in range(count)])  15.1 us
    pallas_call x2, Pallas kernels, half(): kernel_call(functools.partial(grads_body, far), out_shape, [pltpu.VMEM(ac...  4.31 us
    pallas_call x1, Pallas kernels, local_split(): kernel_call(functools.partial(solve_body, -math.sqrt(params_all / total))...  3.98 us
  transfers between devices with their start and end apart: 18, of which 12 were waited for; matrix products, arithmetic and copies ran while one was open for 1% of the time, Pallas kernels for 4%

profile of v8, /device:TPU:0, one launch (start us, length us, event | category | flops | bytes accessed | tf_op | source)
XLA Modules:
  0.0 49.8 jit_solution(651610609585118566)
XLA Ops:
  0.6 2.2 %shard_map.51 = (f32[312,128]{1,0:T(8,128)S(1)}, f32[312,128]{1,0:T(8,128)S(1)}, f32[312,128]{1,0:T(8,128)S(1)}, f32[312,128]{1,0:T(8,128)S(1)}) custom-call(bf16[16,2,64,256]{3,2,1,0:T(8,128)(2,1)} %acts_hbm.3, bf16[16,2,16,256]{3,2,1,0:T(8,128)(2,1)} %cots_hbm.3), custom_call_target="tpu_custom_call" | custom-call | tf_op jit(solution)/shard_map/pallas_call | solution.py:353
  2.8 4.1 %collective-permute-start = (f16[312,128]{1,0:T(8,128)(2,1)S(1)}, f16[312,128]{1,0:T(8,128)(2,1)S(1)}, u32[]{:S(2)}, u32[]{:S(2)}) collective-permute-start(f16[312,128]{1,0:T(8,128)(2,1)S(1)} %convert_element_type.42), channel_id=1, source_target_pairs={{0,16},{4,20},{8,24},{12,28},{16,0},{20,4},{24,8},{28,12},{1,17},{... | collective-permute-start | bytes 239624 | tf_op jit(solution)/shard_map/ppermute | solution.py:38
  6.9 0.1 collective-permute-start.1
  7.1 3.1 %collective-permute-start.2 = (f16[312,128]{1,0:T(8,128)(2,1)S(1)}, f16[312,128]{1,0:T(8,128)(2,1)S(1)}, u32[]{:S(2)}, u32[]{:S(2)}) collective-permute-start(f16[312,128]{1,0:T(8,128)(2,1)S(1)} %convert_element_type.46), channel_id=1, source_target_pairs={{0,24},{4,28},{8,16},{12,20},{16,8},{20,12},{24,0},{28,4},{1,25},{... | collective-permute-start | bytes 239624 | tf_op jit(solution)/shard_map/ppermute | solution.py:38
  10.2 0.6 %collective-permute-start.3 = (f16[312,128]{1,0:T(8,128)(2,1)S(1)}, f16[312,128]{1,0:T(8,128)(2,1)S(1)}, u32[]{:S(2)}, u32[]{:S(2)}) collective-permute-start(f16[312,128]{1,0:T(8,128)(2,1)S(1)} %convert_element_type.48), channel_id=1, source_target_pairs={{0,28},{4,24},{8,20},{12,16},{16,12},{20,8},{24,4},{28,0},{1,29},{... | collective-permute-start | bytes 239624 | tf_op jit(solution)/shard_map/ppermute | solution.py:38
  10.9 2.1 %shard_map.50 = (f32[18,16,128]{2,1,0:T(8,128)S(1)}, f32[312,128]{1,0:T(8,128)S(1)}, f32[312,128]{1,0:T(8,128)S(1)}, f32[312,128]{1,0:T(8,128)S(1)}) custom-call(bf16[16,2,64,256]{3,2,1,0:T(8,128)(2,1)} %acts_hbm.3, bf16[16,2,16,256]{3,2,1,0:T(8,128)(2,1)} %cots_hbm.3), custom_call_target="tpu_custom_call" | custom-call | tf_op jit(solution)/shard_map/pallas_call | solution.py:353
  13.0 0.1 collective-permute-start.4
  13.2 0.0 copy-start
  13.2 0.6 %copy-done = f32[16]{0:T(128)S(1)} copy-done((f32[16]{0:T(128)S(1)}, f32[16]{0:T(128)}, u32[]{:S(2)}) %copy-start) | copy-done | bytes 88
  13.8 0.1 tile.10
  13.9 0.0 collective-permute-done
  13.9 2.4 %collective-permute-start.5 = (f16[312,128]{1,0:T(8,128)(2,1)S(1)}, f16[312,128]{1,0:T(8,128)(2,1)S(1)}, u32[]{:S(2)}, u32[]{:S(2)}) collective-permute-start(f16[312,128]{1,0:T(8,128)(2,1)S(1)} %convert_element_type.52), channel_id=1, source_target_pairs={{0,12},{4,8},{8,4},{12,0},{16,28},{20,24},{24,20},{28,16},{1,13},{... | collective-permute-start | bytes 239624 | tf_op jit(solution)/shard_map/ppermute | solution.py:38
  16.4 1.5 %collective-permute-done.1 = f16[312,128]{1,0:T(8,128)(2,1)S(1)} collective-permute-done((f16[312,128]{1,0:T(8,128)(2,1)S(1)}, f16[312,128]{1,0:T(8,128)(2,1)S(1)}, u32[]{:S(2)}, u32[]{:S(2)}) %collective-permute-start.1) | collective-permute-done | bytes 79904 | tf_op jit(solution)/shard_map/ppermute | solution.py:38
  17.9 0.1 collective-permute-start.6
  18.0 0.1 broadcast_select_fusion.energies_ref
  18.1 0.0 collective-permute-done.2
  18.1 0.0 collective-permute-done.3
  18.1 1.5 %collective-permute-done.4 = f16[312,128]{1,0:T(8,128)(2,1)S(1)} collective-permute-done((f16[312,128]{1,0:T(8,128)(2,1)S(1)}, f16[312,128]{1,0:T(8,128)(2,1)S(1)}, u32[]{:S(2)}, u32[]{:S(2)}) %collective-permute-start.4) | collective-permute-done | bytes 79904 | tf_op jit(solution)/shard_map/ppermute | solution.py:38
  19.7 1.6 %collective-permute-done.5 = f16[312,128]{1,0:T(8,128)(2,1)S(1)} collective-permute-done((f16[312,128]{1,0:T(8,128)(2,1)S(1)}, f16[312,128]{1,0:T(8,128)(2,1)S(1)}, u32[]{:S(2)}, u32[]{:S(2)}) %collective-permute-start.5) | collective-permute-done | bytes 79904 | tf_op jit(solution)/shard_map/ppermute | solution.py:38
  21.3 0.0 collective-permute-done.6
  21.3 0.7 %shard_map.52 = (bf16[18,128,128]{2,1,0:T(8,128)(2,1)S(1)}, f32[72,128]{1,0:T(8,128)S(1)}) custom-call(f32[8,128]{1,0:T(8,128)S(1)} %broadcast_select_fusion.energies_ref, f32[18,16,128]{2,1,0:T(8,128)S(1)} %get-tuple-element.16.own_ref, f32[312,128]{1,0:T(8,128)S(1)} %convert_element_type.43.refs_0_, f32[312,128]{1,0:T(8,128)S(1)} %convert_element_type.45.refs_1_, ...), custom_call_target="tpu_custom_call" | custom-call | tf_op jit(solution)/shard_map/pallas_call | solution.py:376
  22.0 0.2 collective-permute-start.7
  22.1 1.1 %collective-permute-done.7 = f32[72,128]{1,0:T(8,128)S(1)} collective-permute-done((f32[72,128]{1,0:T(8,128)S(1)}, f32[72,128]{1,0:T(8,128)S(1)}, u32[]{:S(2)}, u32[]{:S(2)}) %collective-permute-start.7) | collective-permute-done | bytes 36896 | tf_op jit(solution)/shard_map/ppermute | solution.py:38
  23.2 0.2 collective-permute-start.8
  23.4 2.7 %collective-permute-start.10 = (f32[72,128]{1,0:T(8,128)S(1)}, f32[72,128]{1,0:T(8,128)S(1)}, u32[]{:S(2)}, u32[]{:S(2)}) collective-permute-start(f32[72,128]{1,0:T(8,128)S(1)} %add.17), channel_id=1, source_target_pairs={{0,3},{1,2},{2,1},{3,0},{4,7},{5,6},{6,5},{7,4},{8,11},{9,10},{10,... | collective-permute-start | bytes 110600 | tf_op jit(solution)/shard_map/ppermute | solution.py:38
  26.1 0.5 %collective-permute-start.11 = (f32[72,128]{1,0:T(8,128)S(1)}, f32[72,128]{1,0:T(8,128)S(1)}, u32[]{:S(2)}, u32[]{:S(2)}) collective-permute-start(f32[72,128]{1,0:T(8,128)S(1)} %add.17), channel_id=1, source_target_pairs={{0,1},{1,0},{2,3},{3,2},{4,5},{5,4},{6,7},{7,6},{8,9},{9,8},{10,11... | collective-permute-start | bytes 110600 | tf_op jit(solution)/shard_map/ppermute | solution.py:38
  26.6 0.3 collective-permute-start.9
  26.9 1.4 %collective-permute-done.10 = f32[72,128]{1,0:T(8,128)S(1)} collective-permute-done((f32[72,128]{1,0:T(8,128)S(1)}, f32[72,128]{1,0:T(8,128)S(1)}, u32[]{:S(2)}, u32[]{:S(2)}) %collective-permute-start.10) | collective-permute-done | bytes 36896 | tf_op jit(solution)/shard_map/ppermute | solution.py:38
  28.3 1.8 %collective-permute-done.11 = f32[72,128]{1,0:T(8,128)S(1)} collective-permute-done((f32[72,128]{1,0:T(8,128)S(1)}, f32[72,128]{1,0:T(8,128)S(1)}, u32[]{:S(2)}, u32[]{:S(2)}) %collective-permute-start.11) | collective-permute-done | bytes 36896 | tf_op jit(solution)/shard_map/ppermute | solution.py:38
  30.0 0.5 %collective-permute-done.9 = f32[72,128]{1,0:T(8,128)S(1)} collective-permute-done((f32[72,128]{1,0:T(8,128)S(1)}, f32[72,128]{1,0:T(8,128)S(1)}, u32[]{:S(2)}, u32[]{:S(2)}) %collective-permute-start.9) | collective-permute-done | bytes 36896 | tf_op jit(solution)/shard_map/ppermute | solution.py:38
  30.6 3.4 %collective-permute-start.12 = (f32[72,128]{1,0:T(8,128)S(1)}, f32[72,128]{1,0:T(8,128)S(1)}, u32[]{:S(2)}, u32[]{:S(2)}) collective-permute-start(f32[72,128]{1,0:T(8,128)S(1)} %add_add_fusion.refs_0_), channel_id=1, source_target_pairs={{0,24},{4,28},{8,16},{12,20},{16,8},{20,12},{24,0},{28,4},{1,25},{... | collective-permute-start | bytes 110600 | tf_op jit(solution)/shard_map/ppermute | solution.py:38
  33.9 0.0 collective-permute-start.13
  33.9 1.1 %collective-permute-start.14 = (f32[72,128]{1,0:T(8,128)S(1)}, f32[72,128]{1,0:T(8,128)S(1)}, u32[]{:S(2)}, u32[]{:S(2)}) collective-permute-start(f32[72,128]{1,0:T(8,128)S(1)} %add_add_fusion.refs_0_), channel_id=1, source_target_pairs={{0,8},{4,12},{8,0},{12,4},{16,24},{20,28},{24,16},{28,20},{1,9},{5... | collective-permute-start | bytes 110600 | tf_op jit(solution)/shard_map/ppermute | solution.py:38
  35.0 1.5 %collective-permute-done.12.refs_1_ = f32[72,128]{1,0:T(8,128)S(1)} collective-permute-done((f32[72,128]{1,0:T(8,128)S(1)}, f32[72,128]{1,0:T(8,128)S(1)}, u32[]{:S(2)}, u32[]{:S(2)}) %collective-permute-start.12) | collective-permute-done | bytes 36896 | tf_op jit(solution)/shard_map/ppermute | solution.py:38
  36.5 2.3 %collective-permute-done.13.refs_2_ = f32[72,128]{1,0:T(8,128)S(1)} collective-permute-done((f32[72,128]{1,0:T(8,128)S(1)}, f32[72,128]{1,0:T(8,128)S(1)}, u32[]{:S(2)}, u32[]{:S(2)}) %collective-permute-start.13) | collective-permute-done | bytes 36896 | tf_op jit(solution)/shard_map/ppermute | solution.py:38
  38.8 0.0 collective-permute-done.14.refs_3_
  38.8 0.0 collective-permute-done.8.across_ref
  38.8 4.0 %shard_map.53 = (f32[4,1152]{1,0:T(4,128)S(1)}, f32[1,16]{1,0:T(1,128)}) custom-call(bf16[18,128,128]{2,1,0:T(8,128)(2,1)S(1)} %get-tuple-element.26.centered_ref, bf16[18,128,128]{2,1,0:T(8,128)(2,1)S(1)} %collective-permute-done.8.across_ref, f32[72,128]{1,0:T(8,128)S(1)} %add_add_fusion.refs_0_, f32[72,128]{1,0:T(8,128)S(1)} %collective-permute-done.12.refs_1_, ...), custom_call_target="tpu_custom_call" | custom-call | tf_op jit(solution)/shard_map/pallas_call | solution.py:387
  42.8 1.5 %collective-permute-start.15 = (f32[4,1152]{1,0:T(4,128)S(1)}, f32[4,1152]{1,0:T(4,128)S(1)}, u32[]{:S(2)}, u32[]{:S(2)}) collective-permute-start(f32[4,1152]{1,0:T(4,128)S(1)} %get-tuple-element.28), channel_id=1, source_target_pairs={{0,24},{4,28},{8,16},{12,20},{16,8},{20,12},{24,0},{28,4},{1,25},{... | collective-permute-start | bytes 55304 | tf_op jit(solution)/shard_map/ppermute | solution.py:38
  44.2 0.6 %collective-permute-start.16 = (f32[4,1152]{1,0:T(4,128)S(1)}, f32[4,1152]{1,0:T(4,128)S(1)}, u32[]{:S(2)}, u32[]{:S(2)}) collective-permute-start(f32[4,1152]{1,0:T(4,128)S(1)} %get-tuple-element.28), channel_id=1, source_target_pairs={{0,16},{4,20},{8,24},{12,28},{16,0},{20,4},{24,8},{28,12},{1,17},{... | collective-permute-start | bytes 55304 | tf_op jit(solution)/shard_map/ppermute | solution.py:38
  44.8 2.4 %collective-permute-start.17 = (f32[4,1152]{1,0:T(4,128)S(1)}, f32[4,1152]{1,0:T(4,128)S(1)}, u32[]{:S(2)}, u32[]{:S(2)}) collective-permute-start(f32[4,1152]{1,0:T(4,128)S(1)} %get-tuple-element.28), channel_id=1, source_target_pairs={{0,8},{4,12},{8,0},{12,4},{16,24},{20,28},{24,16},{28,20},{1,9},{5... | collective-permute-start | bytes 55304 | tf_op jit(solution)/shard_map/ppermute | solution.py:38
  47.2 1.2 %collective-permute-done.15 = f32[4,1152]{1,0:T(4,128)S(1)} collective-permute-done((f32[4,1152]{1,0:T(4,128)S(1)}, f32[4,1152]{1,0:T(4,128)S(1)}, u32[]{:S(2)}, u32[]{:S(2)}) %collective-permute-start.15) | collective-permute-done | bytes 18464 | tf_op jit(solution)/shard_map/ppermute | solution.py:38
  48.3 0.6 %collective-permute-done.16 = f32[4,1152]{1,0:T(4,128)S(1)} collective-permute-done((f32[4,1152]{1,0:T(4,128)S(1)}, f32[4,1152]{1,0:T(4,128)S(1)}, u32[]{:S(2)}, u32[]{:S(2)}) %collective-permute-start.16) | collective-permute-done | bytes 18464 | tf_op jit(solution)/shard_map/ppermute | solution.py:38
  48.9 0.2 collective-permute-done.17
  49.1 0.7 %pad_maximum_fusion = f32[16,1152]{1,0:T(8,128)} fusion(f32[4,1152]{1,0:T(4,128)S(1)} %get-tuple-element.31, f32[4,1152]{1,0:T(4,128)S(1)} %get-tuple-element.32, f32[4,1152]{1,0:T(4,128)S(1)} %get-tuple-element.33, f32[4,1152]{1,0:T(4,128)S(1)} %get-tuple-element.30), kind=kLoop, calls=%fused_computation | loop fusion | flops 55296 | bytes 147456 | tf_op jit(solution)/shard_map/concatenate | solution.py:327
  (20 shorter events, 0.3 us)
Async XLA Ops:
  2.8 11.1 %collective-permute-start = (f16[312,128]{1,0:T(8,128)(2,1)S(1)}, f16[312,128]{1,0:T(8,128)(2,1)S(1)}, u32[]{:S(2)}, u32[]{:S(2)}) collective-permute-start(f16[312,128]{1,0:T(8,128)(2,1)S(1)} %convert_element_type.42), channel_id=1, source_target_pairs={{0,16},{4,20},{8,24},{12,28},{16,0},{20,4},{24,8},{28,12},{1,17},{... | collective-permute-start | bytes 239624 | tf_op jit(solution)/shard_map/ppermute | solution.py:38
  6.9 11.0 %collective-permute-start.1 = (f16[312,128]{1,0:T(8,128)(2,1)S(1)}, f16[312,128]{1,0:T(8,128)(2,1)S(1)}, u32[]{:S(2)}, u32[]{:S(2)}) collective-permute-start(f16[312,128]{1,0:T(8,128)(2,1)S(1)} %convert_element_type.44), channel_id=1, source_target_pairs={{0,20},{4,16},{8,28},{12,24},{16,4},{20,0},{24,12},{28,8},{1,21},{... | collective-permute-start | bytes 239624 | tf_op jit(solution)/shard_map/ppermute | solution.py:38
  7.1 11.0 %collective-permute-start.2 = (f16[312,128]{1,0:T(8,128)(2,1)S(1)}, f16[312,128]{1,0:T(8,128)(2,1)S(1)}, u32[]{:S(2)}, u32[]{:S(2)}) collective-permute-start(f16[312,128]{1,0:T(8,128)(2,1)S(1)} %convert_element_type.46), channel_id=1, source_target_pairs={{0,24},{4,28},{8,16},{12,20},{16,8},{20,12},{24,0},{28,4},{1,25},{... | collective-permute-start | bytes 239624 | tf_op jit(solution)/shard_map/ppermute | solution.py:38
  10.2 7.9 %collective-permute-start.3 = (f16[312,128]{1,0:T(8,128)(2,1)S(1)}, f16[312,128]{1,0:T(8,128)(2,1)S(1)}, u32[]{:S(2)}, u32[]{:S(2)}) collective-permute-start(f16[312,128]{1,0:T(8,128)(2,1)S(1)} %convert_element_type.48), channel_id=1, source_target_pairs={{0,28},{4,24},{8,20},{12,16},{16,12},{20,8},{24,4},{28,0},{1,29},{... | collective-permute-start | bytes 239624 | tf_op jit(solution)/shard_map/ppermute | solution.py:38
  13.0 6.6 %collective-permute-start.4 = (f16[312,128]{1,0:T(8,128)(2,1)S(1)}, f16[312,128]{1,0:T(8,128)(2,1)S(1)}, u32[]{:S(2)}, u32[]{:S(2)}) collective-permute-start(f16[312,128]{1,0:T(8,128)(2,1)S(1)} %convert_element_type.50), channel_id=1, source_target_pairs={{0,8},{4,12},{8,0},{12,4},{16,24},{20,28},{24,16},{28,20},{1,9},{5... | collective-permute-start | bytes 239624 | tf_op jit(solution)/shard_map/ppermute | solution.py:38
  13.2 0.7 %copy-start = (f32[16]{0:T(128)S(1)}, f32[16]{0:T(128)}, u32[]{:S(2)}) copy-start(f32[16]{0:T(128)} %param.5) | copy-start | bytes 196
  13.9 7.3 %collective-permute-start.5 = (f16[312,128]{1,0:T(8,128)(2,1)S(1)}, f16[312,128]{1,0:T(8,128)(2,1)S(1)}, u32[]{:S(2)}, u32[]{:S(2)}) collective-permute-start(f16[312,128]{1,0:T(8,128)(2,1)S(1)} %convert_element_type.52), channel_id=1, source_target_pairs={{0,12},{4,8},{8,4},{12,0},{16,28},{20,24},{24,20},{28,16},{1,13},{... | collective-permute-start | bytes 239624 | tf_op jit(solution)/shard_map/ppermute | solution.py:38
  17.9 3.4 %collective-permute-start.6 = (f16[312,128]{1,0:T(8,128)(2,1)S(1)}, f16[312,128]{1,0:T(8,128)(2,1)S(1)}, u32[]{:S(2)}, u32[]{:S(2)}) collective-permute-start(f16[312,128]{1,0:T(8,128)(2,1)S(1)} %convert_element_type.54), channel_id=1, source_target_pairs={{0,4},{4,0},{8,12},{12,8},{16,20},{20,16},{24,28},{28,24},{1,5},{5... | collective-permute-start | bytes 239624 | tf_op jit(solution)/shard_map/ppermute | solution.py:38
  22.0 1.3 %collective-permute-start.7 = (f32[72,128]{1,0:T(8,128)S(1)}, f32[72,128]{1,0:T(8,128)S(1)}, u32[]{:S(2)}, u32[]{:S(2)}) collective-permute-start(f32[72,128]{1,0:T(8,128)S(1)} %get-tuple-element.25), channel_id=1, source_target_pairs={{0,4},{4,0},{8,12},{12,8},{16,20},{20,16},{24,28},{28,24},{1,5},{5... | collective-permute-start | bytes 110600 | tf_op jit(solution)/shard_map/ppermute | solution.py:38
  23.2 15.6 %collective-permute-start.8 = (bf16[18,128,128]{2,1,0:T(8,128)(2,1)S(1)}, bf16[18,128,128]{2,1,0:T(8,128)(2,1)S(1)}, u32[]{:S(2)}, u32[]{:S(2)}) collective-permute-start(bf16[18,128,128]{2,1,0:T(8,128)(2,1)S(1)} %get-tuple-element.26.centered_ref), channel_id=1, source_target_pairs={{0,4},{4,0},{8,12},{12,8},{16,20},{20,16},{24,28},{28,24},{1,5},{5... | collective-permute-start | bytes 1769480 | tf_op jit(solution)/shard_map/ppermute | solution.py:38
  23.4 4.9 %collective-permute-start.10 = (f32[72,128]{1,0:T(8,128)S(1)}, f32[72,128]{1,0:T(8,128)S(1)}, u32[]{:S(2)}, u32[]{:S(2)}) collective-permute-start(f32[72,128]{1,0:T(8,128)S(1)} %add.17), channel_id=1, source_target_pairs={{0,3},{1,2},{2,1},{3,0},{4,7},{5,6},{6,5},{7,4},{8,11},{9,10},{10,... | collective-permute-start | bytes 110600 | tf_op jit(solution)/shard_map/ppermute | solution.py:38
  26.1 4.0 %collective-permute-start.11 = (f32[72,128]{1,0:T(8,128)S(1)}, f32[72,128]{1,0:T(8,128)S(1)}, u32[]{:S(2)}, u32[]{:S(2)}) collective-permute-start(f32[72,128]{1,0:T(8,128)S(1)} %add.17), channel_id=1, source_target_pairs={{0,1},{1,0},{2,3},{3,2},{4,5},{5,4},{6,7},{7,6},{8,9},{9,8},{10,11... | collective-permute-start | bytes 110600 | tf_op jit(solution)/shard_map/ppermute | solution.py:38
  26.6 4.0 %collective-permute-start.9 = (f32[72,128]{1,0:T(8,128)S(1)}, f32[72,128]{1,0:T(8,128)S(1)}, u32[]{:S(2)}, u32[]{:S(2)}) collective-permute-start(f32[72,128]{1,0:T(8,128)S(1)} %add.17), channel_id=1, source_target_pairs={{0,2},{1,3},{2,0},{3,1},{4,6},{5,7},{6,4},{7,5},{8,10},{9,11},{10,... | collective-permute-start | bytes 110600 | tf_op jit(solution)/shard_map/ppermute | solution.py:38
  30.6 5.9 %collective-permute-start.12 = (f32[72,128]{1,0:T(8,128)S(1)}, f32[72,128]{1,0:T(8,128)S(1)}, u32[]{:S(2)}, u32[]{:S(2)}) collective-permute-start(f32[72,128]{1,0:T(8,128)S(1)} %add_add_fusion.refs_0_), channel_id=1, source_target_pairs={{0,24},{4,28},{8,16},{12,20},{16,8},{20,12},{24,0},{28,4},{1,25},{... | collective-permute-start | bytes 110600 | tf_op jit(solution)/shard_map/ppermute | solution.py:38
  33.9 4.9 %collective-permute-start.13 = (f32[72,128]{1,0:T(8,128)S(1)}, f32[72,128]{1,0:T(8,128)S(1)}, u32[]{:S(2)}, u32[]{:S(2)}) collective-permute-start(f32[72,128]{1,0:T(8,128)S(1)} %add_add_fusion.refs_0_), channel_id=1, source_target_pairs={{0,16},{4,20},{8,24},{12,28},{16,0},{20,4},{24,8},{28,12},{1,17},{... | collective-permute-start | bytes 110600 | tf_op jit(solution)/shard_map/ppermute | solution.py:38
  33.9 4.9 %collective-permute-start.14 = (f32[72,128]{1,0:T(8,128)S(1)}, f32[72,128]{1,0:T(8,128)S(1)}, u32[]{:S(2)}, u32[]{:S(2)}) collective-permute-start(f32[72,128]{1,0:T(8,128)S(1)} %add_add_fusion.refs_0_), channel_id=1, source_target_pairs={{0,8},{4,12},{8,0},{12,4},{16,24},{20,28},{24,16},{28,20},{1,9},{5... | collective-permute-start | bytes 110600 | tf_op jit(solution)/shard_map/ppermute | solution.py:38
  42.8 5.6 %collective-permute-start.15 = (f32[4,1152]{1,0:T(4,128)S(1)}, f32[4,1152]{1,0:T(4,128)S(1)}, u32[]{:S(2)}, u32[]{:S(2)}) collective-permute-start(f32[4,1152]{1,0:T(4,128)S(1)} %get-tuple-element.28), channel_id=1, source_target_pairs={{0,24},{4,28},{8,16},{12,20},{16,8},{20,12},{24,0},{28,4},{1,25},{... | collective-permute-start | bytes 55304 | tf_op jit(solution)/shard_map/ppermute | solution.py:38
  44.2 4.7 %collective-permute-start.16 = (f32[4,1152]{1,0:T(4,128)S(1)}, f32[4,1152]{1,0:T(4,128)S(1)}, u32[]{:S(2)}, u32[]{:S(2)}) collective-permute-start(f32[4,1152]{1,0:T(4,128)S(1)} %get-tuple-element.28), channel_id=1, source_target_pairs={{0,16},{4,20},{8,24},{12,28},{16,0},{20,4},{24,8},{28,12},{1,17},{... | collective-permute-start | bytes 55304 | tf_op jit(solution)/shard_map/ppermute | solution.py:38
  44.8 4.3 %collective-permute-start.17 = (f32[4,1152]{1,0:T(4,128)S(1)}, f32[4,1152]{1,0:T(4,128)S(1)}, u32[]{:S(2)}, u32[]{:S(2)}) collective-permute-start(f32[4,1152]{1,0:T(4,128)S(1)} %get-tuple-element.28), channel_id=1, source_target_pairs={{0,8},{4,12},{8,0},{12,4},{16,24},{20,28},{24,16},{28,20},{1,9},{5... | collective-permute-start | bytes 55304 | tf_op jit(solution)/shard_map/ppermute | solution.py:38

commit v9 on v8

--- a/solution.py
+++ b/solution.py
@@ -290,11 +290,9 @@
     coeffs = solve_symmetric(regular, deviation)
 
     position = lax.axis_index("samp")
-    sample = lax.broadcasted_iota(jnp.int32, (total, lanes), 0)
-    lane = lax.broadcasted_iota(jnp.int32, (total, lanes), 1)
     spread = jnp.broadcast_to(coeffs, (lanes, total)).T
-    own = jnp.sum(jnp.where(sample == lane + position * samples, spread, 0.0), axis=0, keepdims=True)
-    coeffs_ref[...] = own[:, :samples]
+    turned = pltpu.roll(jnp.broadcast_to(coeffs, (8, total)), (total - position * samples) % total, 1)
+    coeffs_ref[...] = turned[:1, :samples]
 
     spread = spread * scale
     own, across = (

time: 49.9 us -> 49.7 us (level)
  no operation moved by 1% of the time
where the time goes in v9:
time: 49.7 us; the launch traced here: 49.5 us
  starting transfers between devices  23.2 us (47%)
  waiting for transfers between devices  15.1 us (30%)
  Pallas kernels  8.64 us (17%)
  other arithmetic  0.98 us (2%)
  between operations  0.83 us (2%)
  local copies, waits for them, and re-layouts  0.73 us (1%)
    ppermute x18, starting transfers between devices, swap(): return lax.ppermute(x, axis, [(i, i ^ mask) for i in range(count)])  23.2 us
    ppermute x18, waiting for transfers between devices, swap(): return lax.ppermute(x, axis, [(i, i ^ mask) for i in range(count)])  15.1 us
    pallas_call x2, Pallas kernels, half(): kernel_call(functools.partial(grads_body, far), out_shape, [pltpu.VMEM(ac...  4.31 us
    pallas_call x1, Pallas kernels, local_split(): kernel_call(functools.partial(solve_body, -math.sqrt(params_all / total))...  3.67 us
  transfers between devices with their start and end apart: 18, of which 12 were waited for; matrix products, arithmetic and copies ran while one was open for 1% of the time, Pallas kernels for 4%

profile of v9, /device:TPU:0, one launch (start us, length us, event | category | flops | bytes accessed | tf_op | source)
XLA Modules:
  0.0 49.5 jit_solution(14351504578052698380)
XLA Ops:
  0.6 2.2 %shard_map.51 = (f32[312,128]{1,0:T(8,128)S(1)}, f32[312,128]{1,0:T(8,128)S(1)}, f32[312,128]{1,0:T(8,128)S(1)}, f32[312,128]{1,0:T(8,128)S(1)}) custom-call(bf16[16,2,64,256]{3,2,1,0:T(8,128)(2,1)} %acts_hbm.3, bf16[16,2,16,256]{3,2,1,0:T(8,128)(2,1)} %cots_hbm.3), custom_call_target="tpu_custom_call" | custom-call | tf_op jit(solution)/shard_map/pallas_call | solution.py:351
  2.8 4.1 %collective-permute-start = (f16[312,128]{1,0:T(8,128)(2,1)S(1)}, f16[312,128]{1,0:T(8,128)(2,1)S(1)}, u32[]{:S(2)}, u32[]{:S(2)}) collective-permute-start(f16[312,128]{1,0:T(8,128)(2,1)S(1)} %convert_element_type.42), channel_id=1, source_target_pairs={{0,16},{4,20},{8,24},{12,28},{16,0},{20,4},{24,8},{28,12},{1,17},{... | collective-permute-start | bytes 239624 | tf_op jit(solution)/shard_map/ppermute | solution.py:38
  6.9 0.1 collective-permute-start.1
  7.1 3.1 %collective-permute-start.2 = (f16[312,128]{1,0:T(8,128)(2,1)S(1)}, f16[312,128]{1,0:T(8,128)(2,1)S(1)}, u32[]{:S(2)}, u32[]{:S(2)}) collective-permute-start(f16[312,128]{1,0:T(8,128)(2,1)S(1)} %convert_element_type.46), channel_id=1, source_target_pairs={{0,24},{4,28},{8,16},{12,20},{16,8},{20,12},{24,0},{28,4},{1,25},{... | collective-permute-start | bytes 239624 | tf_op jit(solution)/shard_map/ppermute | solution.py:38
  10.2 0.6 %collective-permute-start.3 = (f16[312,128]{1,0:T(8,128)(2,1)S(1)}, f16[312,128]{1,0:T(8,128)(2,1)S(1)}, u32[]{:S(2)}, u32[]{:S(2)}) collective-permute-start(f16[312,128]{1,0:T(8,128)(2,1)S(1)} %convert_element_type.48), channel_id=1, source_target_pairs={{0,28},{4,24},{8,20},{12,16},{16,12},{20,8},{24,4},{28,0},{1,29},{... | collective-permute-start | bytes 239624 | tf_op jit(solution)/shard_map/ppermute | solution.py:38
  10.9 2.1 %shard_map.50 = (f32[18,16,128]{2,1,0:T(8,128)S(1)}, f32[312,128]{1,0:T(8,128)S(1)}, f32[312,128]{1,0:T(8,128)S(1)}, f32[312,128]{1,0:T(8,128)S(1)}) custom-call(bf16[16,2,64,256]{3,2,1,0:T(8,128)(2,1)} %acts_hbm.3, bf16[16,2,16,256]{3,2,1,0:T(8,128)(2,1)} %cots_hbm.3), custom_call_target="tpu_custom_call" | custom-call | tf_op jit(solution)/shard_map/pallas_call | solution.py:351
  13.0 0.1 collective-permute-start.4
  13.2 0.0 copy-start
  13.2 0.6 %copy-done = f32[16]{0:T(128)S(1)} copy-done((f32[16]{0:T(128)S(1)}, f32[16]{0:T(128)}, u32[]{:S(2)}) %copy-start) | copy-done | bytes 88
  13.8 0.1 tile.10
  13.9 0.0 collective-permute-done
  13.9 2.4 %collective-permute-start.5 = (f16[312,128]{1,0:T(8,128)(2,1)S(1)}, f16[312,128]{1,0:T(8,128)(2,1)S(1)}, u32[]{:S(2)}, u32[]{:S(2)}) collective-permute-start(f16[312,128]{1,0:T(8,128)(2,1)S(1)} %convert_element_type.52), channel_id=1, source_target_pairs={{0,12},{4,8},{8,4},{12,0},{16,28},{20,24},{24,20},{28,16},{1,13},{... | collective-permute-start | bytes 239624 | tf_op jit(solution)/shard_map/ppermute | solution.py:38
  16.4 1.5 %collective-permute-done.1 = f16[312,128]{1,0:T(8,128)(2,1)S(1)} collective-permute-done((f16[312,128]{1,0:T(8,128)(2,1)S(1)}, f16[312,128]{1,0:T(8,128)(2,1)S(1)}, u32[]{:S(2)}, u32[]{:S(2)}) %collective-permute-start.1) | collective-permute-done | bytes 79904 | tf_op jit(solution)/shard_map/ppermute | solution.py:38
  17.9 0.1 collective-permute-start.6
  18.0 0.1 broadcast_select_fusion.energies_ref
  18.1 0.0 collective-permute-done.2
  18.1 0.0 collective-permute-done.3
  18.1 1.5 %collective-permute-done.4 = f16[312,128]{1,0:T(8,128)(2,1)S(1)} collective-permute-done((f16[312,128]{1,0:T(8,128)(2,1)S(1)}, f16[312,128]{1,0:T(8,128)(2,1)S(1)}, u32[]{:S(2)}, u32[]{:S(2)}) %collective-permute-start.4) | collective-permute-done | bytes 79904 | tf_op jit(solution)/shard_map/ppermute | solution.py:38
  19.7 1.6 %collective-permute-done.5 = f16[312,128]{1,0:T(8,128)(2,1)S(1)} collective-permute-done((f16[312,128]{1,0:T(8,128)(2,1)S(1)}, f16[312,128]{1,0:T(8,128)(2,1)S(1)}, u32[]{:S(2)}, u32[]{:S(2)}) %collective-permute-start.5) | collective-permute-done | bytes 79904 | tf_op jit(solution)/shard_map/ppermute | solution.py:38
  21.3 0.0 collective-permute-done.6
  21.3 0.7 %shard_map.52 = (bf16[18,128,128]{2,1,0:T(8,128)(2,1)S(1)}, f32[72,128]{1,0:T(8,128)S(1)}) custom-call(f32[8,128]{1,0:T(8,128)S(1)} %broadcast_select_fusion.energies_ref, f32[18,16,128]{2,1,0:T(8,128)S(1)} %get-tuple-element.16.own_ref, f32[312,128]{1,0:T(8,128)S(1)} %convert_element_type.43.refs_0_, f32[312,128]{1,0:T(8,128)S(1)} %convert_element_type.45.refs_1_, ...), custom_call_target="tpu_custom_call" | custom-call | tf_op jit(solution)/shard_map/pallas_call | solution.py:374
  22.0 0.2 collective-permute-start.7
  22.1 1.1 %collective-permute-done.7 = f32[72,128]{1,0:T(8,128)S(1)} collective-permute-done((f32[72,128]{1,0:T(8,128)S(1)}, f32[72,128]{1,0:T(8,128)S(1)}, u32[]{:S(2)}, u32[]{:S(2)}) %collective-permute-start.7) | collective-permute-done | bytes 36896 | tf_op jit(solution)/shard_map/ppermute | solution.py:38
  23.2 0.2 collective-permute-start.8
  23.4 2.7 %collective-permute-start.10 = (f32[72,128]{1,0:T(8,128)S(1)}, f32[72,128]{1,0:T(8,128)S(1)}, u32[]{:S(2)}, u32[]{:S(2)}) collective-permute-start(f32[72,128]{1,0:T(8,128)S(1)} %add.17), channel_id=1, source_target_pairs={{0,3},{1,2},{2,1},{3,0},{4,7},{5,6},{6,5},{7,4},{8,11},{9,10},{10,... | collective-permute-start | bytes 110600 | tf_op jit(solution)/shard_map/ppermute | solution.py:38
  26.1 0.5 %collective-permute-start.11 = (f32[72,128]{1,0:T(8,128)S(1)}, f32[72,128]{1,0:T(8,128)S(1)}, u32[]{:S(2)}, u32[]{:S(2)}) collective-permute-start(f32[72,128]{1,0:T(8,128)S(1)} %add.17), channel_id=1, source_target_pairs={{0,1},{1,0},{2,3},{3,2},{4,5},{5,4},{6,7},{7,6},{8,9},{9,8},{10,11... | collective-permute-start | bytes 110600 | tf_op jit(solution)/shard_map/ppermute | solution.py:38
  26.6 0.3 collective-permute-start.9
  26.9 1.4 %collective-permute-done.10 = f32[72,128]{1,0:T(8,128)S(1)} collective-permute-done((f32[72,128]{1,0:T(8,128)S(1)}, f32[72,128]{1,0:T(8,128)S(1)}, u32[]{:S(2)}, u32[]{:S(2)}) %collective-permute-start.10) | collective-permute-done | bytes 36896 | tf_op jit(solution)/shard_map/ppermute | solution.py:38
  28.3 1.8 %collective-permute-done.11 = f32[72,128]{1,0:T(8,128)S(1)} collective-permute-done((f32[72,128]{1,0:T(8,128)S(1)}, f32[72,128]{1,0:T(8,128)S(1)}, u32[]{:S(2)}, u32[]{:S(2)}) %collective-permute-start.11) | collective-permute-done | bytes 36896 | tf_op jit(solution)/shard_map/ppermute | solution.py:38
  30.0 0.5 %collective-permute-done.9 = f32[72,128]{1,0:T(8,128)S(1)} collective-permute-done((f32[72,128]{1,0:T(8,128)S(1)}, f32[72,128]{1,0:T(8,128)S(1)}, u32[]{:S(2)}, u32[]{:S(2)}) %collective-permute-start.9) | collective-permute-done | bytes 36896 | tf_op jit(solution)/shard_map/ppermute | solution.py:38
  30.6 3.4 %collective-permute-start.12 = (f32[72,128]{1,0:T(8,128)S(1)}, f32[72,128]{1,0:T(8,128)S(1)}, u32[]{:S(2)}, u32[]{:S(2)}) collective-permute-start(f32[72,128]{1,0:T(8,128)S(1)} %add_add_fusion.refs_0_), channel_id=1, source_target_pairs={{0,24},{4,28},{8,16},{12,20},{16,8},{20,12},{24,0},{28,4},{1,25},{... | collective-permute-start | bytes 110600 | tf_op jit(solution)/shard_map/ppermute | solution.py:38
  33.9 0.0 collective-permute-start.13
  33.9 1.1 %collective-permute-start.14 = (f32[72,128]{1,0:T(8,128)S(1)}, f32[72,128]{1,0:T(8,128)S(1)}, u32[]{:S(2)}, u32[]{:S(2)}) collective-permute-start(f32[72,128]{1,0:T(8,128)S(1)} %add_add_fusion.refs_0_), channel_id=1, source_target_pairs={{0,8},{4,12},{8,0},{12,4},{16,24},{20,28},{24,16},{28,20},{1,9},{5... | collective-permute-start | bytes 110600 | tf_op jit(solution)/shard_map/ppermute | solution.py:38
  35.0 1.5 %collective-permute-done.12.refs_1_ = f32[72,128]{1,0:T(8,128)S(1)} collective-permute-done((f32[72,128]{1,0:T(8,128)S(1)}, f32[72,128]{1,0:T(8,128)S(1)}, u32[]{:S(2)}, u32[]{:S(2)}) %collective-permute-start.12) | collective-permute-done | bytes 36896 | tf_op jit(solution)/shard_map/ppermute | solution.py:38
  36.5 2.3 %collective-permute-done.13.refs_2_ = f32[72,128]{1,0:T(8,128)S(1)} collective-permute-done((f32[72,128]{1,0:T(8,128)S(1)}, f32[72,128]{1,0:T(8,128)S(1)}, u32[]{:S(2)}, u32[]{:S(2)}) %collective-permute-start.13) | collective-permute-done | bytes 36896 | tf_op jit(solution)/shard_map/ppermute | solution.py:38
  38.8 0.0 collective-permute-done.14.refs_3_
  38.8 0.0 collective-permute-done.8.across_ref
  38.8 3.7 %shard_map.53 = (f32[4,1152]{1,0:T(4,128)S(1)}, f32[1,16]{1,0:T(1,128)}) custom-call(bf16[18,128,128]{2,1,0:T(8,128)(2,1)S(1)} %get-tuple-element.26.centered_ref, bf16[18,128,128]{2,1,0:T(8,128)(2,1)S(1)} %collective-permute-done.8.across_ref, f32[72,128]{1,0:T(8,128)S(1)} %add_add_fusion.refs_0_, f32[72,128]{1,0:T(8,128)S(1)} %collective-permute-done.12.refs_1_, ...), custom_call_target="tpu_custom_call" | custom-call | tf_op jit(solution)/shard_map/pallas_call | solution.py:385
  42.5 1.5 %collective-permute-start.15 = (f32[4,1152]{1,0:T(4,128)S(1)}, f32[4,1152]{1,0:T(4,128)S(1)}, u32[]{:S(2)}, u32[]{:S(2)}) collective-permute-start(f32[4,1152]{1,0:T(4,128)S(1)} %get-tuple-element.28), channel_id=1, source_target_pairs={{0,24},{4,28},{8,16},{12,20},{16,8},{20,12},{24,0},{28,4},{1,25},{... | collective-permute-start | bytes 55304 | tf_op jit(solution)/shard_map/ppermute | solution.py:38
  44.0 0.6 %collective-permute-start.16 = (f32[4,1152]{1,0:T(4,128)S(1)}, f32[4,1152]{1,0:T(4,128)S(1)}, u32[]{:S(2)}, u32[]{:S(2)}) collective-permute-start(f32[4,1152]{1,0:T(4,128)S(1)} %get-tuple-element.28), channel_id=1, source_target_pairs={{0,16},{4,20},{8,24},{12,28},{16,0},{20,4},{24,8},{28,12},{1,17},{... | collective-permute-start | bytes 55304 | tf_op jit(solution)/shard_map/ppermute | solution.py:38
  44.6 2.3 %collective-permute-start.17 = (f32[4,1152]{1,0:T(4,128)S(1)}, f32[4,1152]{1,0:T(4,128)S(1)}, u32[]{:S(2)}, u32[]{:S(2)}) collective-permute-start(f32[4,1152]{1,0:T(4,128)S(1)} %get-tuple-element.28), channel_id=1, source_target_pairs={{0,8},{4,12},{8,0},{12,4},{16,24},{20,28},{24,16},{28,20},{1,9},{5... | collective-permute-start | bytes 55304 | tf_op jit(solution)/shard_map/ppermute | solution.py:38
  46.9 1.2 %collective-permute-done.15 = f32[4,1152]{1,0:T(4,128)S(1)} collective-permute-done((f32[4,1152]{1,0:T(4,128)S(1)}, f32[4,1152]{1,0:T(4,128)S(1)}, u32[]{:S(2)}, u32[]{:S(2)}) %collective-permute-start.15) | collective-permute-done | bytes 18464 | tf_op jit(solution)/shard_map/ppermute | solution.py:38
  48.1 0.6 %collective-permute-done.16 = f32[4,1152]{1,0:T(4,128)S(1)} collective-permute-done((f32[4,1152]{1,0:T(4,128)S(1)}, f32[4,1152]{1,0:T(4,128)S(1)}, u32[]{:S(2)}, u32[]{:S(2)}) %collective-permute-start.16) | collective-permute-done | bytes 18464 | tf_op jit(solution)/shard_map/ppermute | solution.py:38
  48.6 0.2 collective-permute-done.17
  48.9 0.7 %pad_maximum_fusion = f32[16,1152]{1,0:T(8,128)} fusion(f32[4,1152]{1,0:T(4,128)S(1)} %get-tuple-element.31, f32[4,1152]{1,0:T(4,128)S(1)} %get-tuple-element.32, f32[4,1152]{1,0:T(4,128)S(1)} %get-tuple-element.33, f32[4,1152]{1,0:T(4,128)S(1)} %get-tuple-element.30), kind=kLoop, calls=%fused_computation | loop fusion | flops 55296 | bytes 147456 | tf_op jit(solution)/shard_map/concatenate | solution.py:325
  (20 shorter events, 0.3 us)
Async XLA Ops:
  2.8 11.1 %collective-permute-start = (f16[312,128]{1,0:T(8,128)(2,1)S(1)}, f16[312,128]{1,0:T(8,128)(2,1)S(1)}, u32[]{:S(2)}, u32[]{:S(2)}) collective-permute-start(f16[312,128]{1,0:T(8,128)(2,1)S(1)} %convert_element_type.42), channel_id=1, source_target_pairs={{0,16},{4,20},{8,24},{12,28},{16,0},{20,4},{24,8},{28,12},{1,17},{... | collective-permute-start | bytes 239624 | tf_op jit(solution)/shard_map/ppermute | solution.py:38
  6.9 11.0 %collective-permute-start.1 = (f16[312,128]{1,0:T(8,128)(2,1)S(1)}, f16[312,128]{1,0:T(8,128)(2,1)S(1)}, u32[]{:S(2)}, u32[]{:S(2)}) collective-permute-start(f16[312,128]{1,0:T(8,128)(2,1)S(1)} %convert_element_type.44), channel_id=1, source_target_pairs={{0,20},{4,16},{8,28},{12,24},{16,4},{20,0},{24,12},{28,8},{1,21},{... | collective-permute-start | bytes 239624 | tf_op jit(solution)/shard_map/ppermute | solution.py:38
  7.1 11.0 %collective-permute-start.2 = (f16[312,128]{1,0:T(8,128)(2,1)S(1)}, f16[312,128]{1,0:T(8,128)(2,1)S(1)}, u32[]{:S(2)}, u32[]{:S(2)}) collective-permute-start(f16[312,128]{1,0:T(8,128)(2,1)S(1)} %convert_element_type.46), channel_id=1, source_target_pairs={{0,24},{4,28},{8,16},{12,20},{16,8},{20,12},{24,0},{28,4},{1,25},{... | collective-permute-start | bytes 239624 | tf_op jit(solution)/shard_map/ppermute | solution.py:38
  10.2 7.9 %collective-permute-start.3 = (f16[312,128]{1,0:T(8,128)(2,1)S(1)}, f16[312,128]{1,0:T(8,128)(2,1)S(1)}, u32[]{:S(2)}, u32[]{:S(2)}) collective-permute-start(f16[312,128]{1,0:T(8,128)(2,1)S(1)} %convert_element_type.48), channel_id=1, source_target_pairs={{0,28},{4,24},{8,20},{12,16},{16,12},{20,8},{24,4},{28,0},{1,29},{... | collective-permute-start | bytes 239624 | tf_op jit(solution)/shard_map/ppermute | solution.py:38
  13.0 6.6 %collective-permute-start.4 = (f16[312,128]{1,0:T(8,128)(2,1)S(1)}, f16[312,128]{1,0:T(8,128)(2,1)S(1)}, u32[]{:S(2)}, u32[]{:S(2)}) collective-permute-start(f16[312,128]{1,0:T(8,128)(2,1)S(1)} %convert_element_type.50), channel_id=1, source_target_pairs={{0,8},{4,12},{8,0},{12,4},{16,24},{20,28},{24,16},{28,20},{1,9},{5... | collective-permute-start | bytes 239624 | tf_op jit(solution)/shard_map/ppermute | solution.py:38
  13.2 0.7 %copy-start = (f32[16]{0:T(128)S(1)}, f32[16]{0:T(128)}, u32[]{:S(2)}) copy-start(f32[16]{0:T(128)} %param.5) | copy-start | bytes 196
  13.9 7.3 %collective-permute-start.5 = (f16[312,128]{1,0:T(8,128)(2,1)S(1)}, f16[312,128]{1,0:T(8,128)(2,1)S(1)}, u32[]{:S(2)}, u32[]{:S(2)}) collective-permute-start(f16[312,128]{1,0:T(8,128)(2,1)S(1)} %convert_element_type.52), channel_id=1, source_target_pairs={{0,12},{4,8},{8,4},{12,0},{16,28},{20,24},{24,20},{28,16},{1,13},{... | collective-permute-start | bytes 239624 | tf_op jit(solution)/shard_map/ppermute | solution.py:38
  17.9 3.4 %collective-permute-start.6 = (f16[312,128]{1,0:T(8,128)(2,1)S(1)}, f16[312,128]{1,0:T(8,128)(2,1)S(1)}, u32[]{:S(2)}, u32[]{:S(2)}) collective-permute-start(f16[312,128]{1,0:T(8,128)(2,1)S(1)} %convert_element_type.54), channel_id=1, source_target_pairs={{0,4},{4,0},{8,12},{12,8},{16,20},{20,16},{24,28},{28,24},{1,5},{5... | collective-permute-start | bytes 239624 | tf_op jit(solution)/shard_map/ppermute | solution.py:38
  22.0 1.3 %collective-permute-start.7 = (f32[72,128]{1,0:T(8,128)S(1)}, f32[72,128]{1,0:T(8,128)S(1)}, u32[]{:S(2)}, u32[]{:S(2)}) collective-permute-start(f32[72,128]{1,0:T(8,128)S(1)} %get-tuple-element.25), channel_id=1, source_target_pairs={{0,4},{4,0},{8,12},{12,8},{16,20},{20,16},{24,28},{28,24},{1,5},{5... | collective-permute-start | bytes 110600 | tf_op jit(solution)/shard_map/ppermute | solution.py:38
  23.2 15.6 %collective-permute-start.8 = (bf16[18,128,128]{2,1,0:T(8,128)(2,1)S(1)}, bf16[18,128,128]{2,1,0:T(8,128)(2,1)S(1)}, u32[]{:S(2)}, u32[]{:S(2)}) collective-permute-start(bf16[18,128,128]{2,1,0:T(8,128)(2,1)S(1)} %get-tuple-element.26.centered_ref), channel_id=1, source_target_pairs={{0,4},{4,0},{8,12},{12,8},{16,20},{20,16},{24,28},{28,24},{1,5},{5... | collective-permute-start | bytes 1769480 | tf_op jit(solution)/shard_map/ppermute | solution.py:38
  23.4 4.9 %collective-permute-start.10 = (f32[72,128]{1,0:T(8,128)S(1)}, f32[72,128]{1,0:T(8,128)S(1)}, u32[]{:S(2)}, u32[]{:S(2)}) collective-permute-start(f32[72,128]{1,0:T(8,128)S(1)} %add.17), channel_id=1, source_target_pairs={{0,3},{1,2},{2,1},{3,0},{4,7},{5,6},{6,5},{7,4},{8,11},{9,10},{10,... | collective-permute-start | bytes 110600 | tf_op jit(solution)/shard_map/ppermute | solution.py:38
  26.1 4.0 %collective-permute-start.11 = (f32[72,128]{1,0:T(8,128)S(1)}, f32[72,128]{1,0:T(8,128)S(1)}, u32[]{:S(2)}, u32[]{:S(2)}) collective-permute-start(f32[72,128]{1,0:T(8,128)S(1)} %add.17), channel_id=1, source_target_pairs={{0,1},{1,0},{2,3},{3,2},{4,5},{5,4},{6,7},{7,6},{8,9},{9,8},{10,11... | collective-permute-start | bytes 110600 | tf_op jit(solution)/shard_map/ppermute | solution.py:38
  26.6 4.0 %collective-permute-start.9 = (f32[72,128]{1,0:T(8,128)S(1)}, f32[72,128]{1,0:T(8,128)S(1)}, u32[]{:S(2)}, u32[]{:S(2)}) collective-permute-start(f32[72,128]{1,0:T(8,128)S(1)} %add.17), channel_id=1, source_target_pairs={{0,2},{1,3},{2,0},{3,1},{4,6},{5,7},{6,4},{7,5},{8,10},{9,11},{10,... | collective-permute-start | bytes 110600 | tf_op jit(solution)/shard_map/ppermute | solution.py:38
  30.6 5.9 %collective-permute-start.12 = (f32[72,128]{1,0:T(8,128)S(1)}, f32[72,128]{1,0:T(8,128)S(1)}, u32[]{:S(2)}, u32[]{:S(2)}) collective-permute-start(f32[72,128]{1,0:T(8,128)S(1)} %add_add_fusion.refs_0_), channel_id=1, source_target_pairs={{0,24},{4,28},{8,16},{12,20},{16,8},{20,12},{24,0},{28,4},{1,25},{... | collective-permute-start | bytes 110600 | tf_op jit(solution)/shard_map/ppermute | solution.py:38
  33.9 4.9 %collective-permute-start.13 = (f32[72,128]{1,0:T(8,128)S(1)}, f32[72,128]{1,0:T(8,128)S(1)}, u32[]{:S(2)}, u32[]{:S(2)}) collective-permute-start(f32[72,128]{1,0:T(8,128)S(1)} %add_add_fusion.refs_0_), channel_id=1, source_target_pairs={{0,16},{4,20},{8,24},{12,28},{16,0},{20,4},{24,8},{28,12},{1,17},{... | collective-permute-start | bytes 110600 | tf_op jit(solution)/shard_map/ppermute | solution.py:38
  33.9 4.9 %collective-permute-start.14 = (f32[72,128]{1,0:T(8,128)S(1)}, f32[72,128]{1,0:T(8,128)S(1)}, u32[]{:S(2)}, u32[]{:S(2)}) collective-permute-start(f32[72,128]{1,0:T(8,128)S(1)} %add_add_fusion.refs_0_), channel_id=1, source_target_pairs={{0,8},{4,12},{8,0},{12,4},{16,24},{20,28},{24,16},{28,20},{1,9},{5... | collective-permute-start | bytes 110600 | tf_op jit(solution)/shard_map/ppermute | solution.py:38
  42.5 5.6 %collective-permute-start.15 = (f32[4,1152]{1,0:T(4,128)S(1)}, f32[4,1152]{1,0:T(4,128)S(1)}, u32[]{:S(2)}, u32[]{:S(2)}) collective-permute-start(f32[4,1152]{1,0:T(4,128)S(1)} %get-tuple-element.28), channel_id=1, source_target_pairs={{0,24},{4,28},{8,16},{12,20},{16,8},{20,12},{24,0},{28,4},{1,25},{... | collective-permute-start | bytes 55304 | tf_op jit(solution)/shard_map/ppermute | solution.py:38
  44.0 4.7 %collective-permute-start.16 = (f32[4,1152]{1,0:T(4,128)S(1)}, f32[4,1152]{1,0:T(4,128)S(1)}, u32[]{:S(2)}, u32[]{:S(2)}) collective-permute-start(f32[4,1152]{1,0:T(4,128)S(1)} %get-tuple-element.28), channel_id=1, source_target_pairs={{0,16},{4,20},{8,24},{12,28},{16,0},{20,4},{24,8},{28,12},{1,17},{... | collective-permute-start | bytes 55304 | tf_op jit(solution)/shard_map/ppermute | solution.py:38
  44.6 4.2 %collective-permute-start.17 = (f32[4,1152]{1,0:T(4,128)S(1)}, f32[4,1152]{1,0:T(4,128)S(1)}, u32[]{:S(2)}, u32[]{:S(2)}) collective-permute-start(f32[4,1152]{1,0:T(4,128)S(1)} %get-tuple-element.28), channel_id=1, source_target_pairs={{0,8},{4,12},{8,0},{12,4},{16,24},{20,28},{24,16},{28,20},{1,9},{5... | collective-permute-start | bytes 55304 | tf_op jit(solution)/shard_map/ppermute | solution.py:38
